TPU v7x, 32 devices: a whole 2x2x4 slice. The times are simulated.
32 devices in a mesh: row: 8 (over z, y), col: 4 (over x, core).
Axes of the slice: x: 2, y: 2, z: 4, core: 2. Of those that a mesh axis runs over, the one named last changes fastest.
Arguments:
- block_tiles: bfloat16 [8, 4, 128, 128, 128], P('row', 'col'), may hold values from -0.5 to 0.5
- tile_row: int32 [8, 4, 128], P('row', 'col'), may hold values from 0 to 495
- tile_col: int32 [8, 4, 128], P('row', 'col'), may hold values from 0 to 3903
- primal: float32 [1998848], P(('col', 'row')), may hold values from -6 to 6
- duals: float32 [507904], P('row'), may hold values from -6 to 6
- cost_vec: float32 [1998848], P(('col', 'row')), may hold values from -6 to 6
- lower_bound: float32 [1998848], P(('col', 'row')), may hold values from -1.5 to -0.25
- upper_bound: float32 [1998848], P(('col', 'row')), may hold values from 0.25 to 1.5
- bound_kind: int32 [1998848], P(('col', 'row')), may hold values from 0 to 3
- right_side: float32 [507904], P('row'), may hold values from -6 to 6
- row_kind: int32 [507904], P('row'), may hold values from 0 to 1
- step_sizes: float32 [2], replicated, may hold values from 0.3 to 1
Outputs:
- primal_next: float32 [1998848], P(('col', 'row'))
- dual_next: float32 [507904], P('row')
Inputs may be any that keep to these rules, and one draw needn't show every extreme that they name: `tile_row`: index of a tile row inside the device's own row range. `tile_col`: index of a tile column inside the device's own column range.
All inputs are finite; a program needn't handle non-finite values.
Results may differ from a plain program's by a relative error of at most 0.0031.
Values may be sent and summed in bfloat16 or wider, within the bound.
No kernel may reach another device: no remote copies, remote signals or barrier semaphores. Data moves between devices by JAX's collectives and lax.ppermute only.
A program may use at most 64 MiB of HBM per device.

v0:
```python
import jax
import jax.numpy as jnp
from jax import lax
from jax.sharding import PartitionSpec as P


def project(values, lower_bound, upper_bound, bound_kind):
    with_lower = bound_kind % 2 == 1
    with_upper = bound_kind >= 2
    values = jnp.where(with_lower, jnp.maximum(values, lower_bound), values)
    return jnp.where(with_upper, jnp.minimum(values, upper_bound), values)


def dual_update(duals, right_side, row_kind, row_sums, dual_step):
    updated = duals + dual_step * (right_side - row_sums)
    return jnp.where(row_kind == 1, jnp.maximum(updated, 0.0), updated)


def local(
    block_tiles,
    tile_row,
    tile_col,
    primal,
    duals,
    cost_vec,
    lower_bound,
    upper_bound,
    bound_kind,
    right_side,
    row_kind,
    step_sizes,
):
    tiles_here = block_tiles.reshape(block_tiles.shape[2], 128, 128)
    rows_here = tile_row.reshape(-1)
    cols_here = tile_col.reshape(-1)
    row_count = lax.axis_size("row")
    col_blocks = primal.shape[0] * row_count // 128
    row_blocks = duals.shape[0] // 128
    dual_blocks = duals.astype(jnp.bfloat16).reshape(row_blocks, 128)[rows_here]
    col_terms = jnp.einsum(
        "kij,ki->kj", tiles_here, dual_blocks, preferred_element_type=jnp.float32
    )
    partial_value = jax.ops.segment_sum(col_terms, cols_here, num_segments=col_blocks).reshape(-1)
    col_sums = lax.psum_scatter(partial_value, "row", scatter_dimension=0, tiled=True)
    stepped = primal - step_sizes[0] * (cost_vec - col_sums)
    primal_next = project(stepped, lower_bound, upper_bound, bound_kind)
    extrap = (2.0 * primal_next - primal).astype(jnp.bfloat16)
    whole_cols = lax.all_gather(extrap, "row", axis=0, tiled=True).reshape(col_blocks, 128)[
        cols_here
    ]
    row_terms = jnp.einsum("kij,kj->ki", tiles_here, whole_cols, preferred_element_type=jnp.float32)
    partial_rows = jax.ops.segment_sum(row_terms, rows_here, num_segments=row_blocks).reshape(-1)
    row_share = lax.psum_scatter(partial_rows, "col", scatter_dimension=0, tiled=True)
    share_len = row_share.shape[0]
    first_row = lax.axis_index("col") * share_len
    duals_part = lax.dynamic_slice_in_dim(duals, first_row, share_len)
    right_part = lax.dynamic_slice_in_dim(right_side, first_row, share_len)
    kind_part = lax.dynamic_slice_in_dim(row_kind, first_row, share_len)
    updated = dual_update(duals_part, right_part, kind_part, row_share, step_sizes[1])
    dual_next = lax.all_gather(updated, "col", axis=0, tiled=True)
    return (primal_next, dual_next)


def solution(mesh):
    return jax.shard_map(
        local,
        mesh=mesh,
        in_specs=(
            P("row", "col", None, None, None),
            P("row", "col", None),
            P("row", "col", None),
            P(("col", "row")),
            P("row"),
            P(("col", "row")),
            P(("col", "row")),
            P(("col", "row")),
            P(("col", "row")),
            P("row"),
            P("row"),
            P(),
        ),
        out_specs=(P(("col", "row")), P("row")),
        check_vma=False,
    )
```

profile of v0, /device:TPU:0, one launch (start us, length us, event | category | flops | bytes accessed | tf_op | source)
XLA Modules:
  0.0 206.3 jit_solution(4262153830548217612)
XLA Ops:
  7.2 0.0 all-reduce.5.cloned.1.call-start
  7.2 1.0 convert_bitcast_fusion
  8.2 0.7 fusion.16
  8.8 0.7 gather_fusion
  9.6 0.0 copy-start.6
  9.6 3.4 %fusion.2 = f32[128,1,128]{2,1,0:T(1,128)S(1)} fusion(bf16[1,1,128,128,128]{4,3,2,1,0:T(8,128)(2,1)} %param.12, bf16[128,128,1]{1,0,2:T(8,128)(2,1)S(1)} %bitcast.35), kind=kOutput, calls=%fused_computation.6 | convolution fusion | flops 4194304 | bytes 4292608 | tf_op jit(solution)/shard_map/kij,ki->kj/dot_general | solution.py:40
  12.9 0.0 copy-done.6
  12.9 0.0 copy-start.8
  12.9 0.0 copy-start.5
  12.9 0.0 copy-start
  13.0 0.0 copy-start.1
  13.0 0.0 copy-start.2
  13.0 0.0 copy-start.3
  13.0 0.0 copy-start.4
  13.0 2.4 %scatter_custom_fusion = f32[3904,128]{1,0:T(8,128)} fusion(s32[128]{0:T(128)S(1)} %bitcast.39, f32[128,128]{1,0:T(8,128)S(1)} %bitcast.38, f32[]{:T(128)} %constant.13.clone.1), kind=kCustom, calls=%fused_computation.8 | custom fusion | flops 16384 | bytes 1998852 | tf_op jit(solution)/shard_map/scatter-add | solution.py:43
  15.4 0.0 all-reduce.5.cloned.1.call-update
  15.4 0.0 all-reduce.7.cloned.1.call-start
  15.5 0.0 copy-done.8
  15.5 0.6 dynamic-slice
  16.7 0.0 copy-done.5
  16.7 0.6 fusion.18
  17.3 100.4 %all-reduce.5.cloned.1.call-done = f32[499712]{0:T(1024)} async-done(((f32[499712]{0:T(1024)}), f32[499712]{0:T(1024)}) %all-reduce.5.cloned.1.call-update) | async-done | bytes 1998864
  117.7 0.0 copy-done
  117.7 0.0 copy-done.1
  117.7 0.0 copy-done.2
  117.7 0.0 copy-done.3
  117.8 0.0 copy-done.4
  117.8 2.5 %subtract_convert_fusion = (bf16[62464]{0:T(1024)(128)(2,1)S(1)}, f32[62464]{0:T(1024)}) fusion(f32[62464]{0:T(1024)S(1)} %copy-done, f32[62464]{0:T(1024)S(1)} %copy-done.1, f32[62464]{0:T(1024)S(1)} %copy-done.2, f32[62464]{0:T(1024)S(1)} %copy-done.3, f32[499712]{0:T(1024)} %all-reduce.5.cloned.1.call-done, u32[]{:T(128)S(6)} %multiply.1, f32[]{:T(128)} %bitcast, ...), kind=kLoop, calls=%fused_computation.20 | loop fusion | flops 1436672 | bytes 1873928 | tf_op jit(solution)/shard_map/convert_element_type | solution.py:47
  120.3 32.6 %all_gather.6 = bf16[499712]{0:T(1024)(128)(2,1)S(1)} all-gather(bf16[62464]{0:T(1024)(128)(2,1)S(1)} %get-tuple-element.2), channel_id=1, replica_groups=mesh['row'=8,'col'=4] {'row'}, dimensions={0}, use_global_device_ids=true | all-gather | bytes 1124352 | tf_op jit(solution)/shard_map/all_gather | solution.py:48
  152.8 0.7 gather_fusion.1
  153.6 0.0 copy-start.7
  153.6 4.5 %fusion = f32[128,1,128]{2,1,0:T(1,128)S(1)} fusion(bf16[1,1,128,128,128]{4,3,2,1,0:T(8,128)(2,1)} %param.12, bf16[128,128,1]{1,0,2:T(8,128)(2,1)S(1)} %bitcast.36), kind=kOutput, calls=%fused_computation.4 | convolution fusion | flops 4194304 | bytes 4292608 | tf_op jit(solution)/shard_map/kij,kj->ki/dot_general | solution.py:51
  158.0 1.8 scatter_custom_fusion.1
  159.8 0.0 all-reduce.7.cloned.1.call-update
  159.9 0.0 copy-done.7
  159.9 0.6 dynamic-slice.2
  161.1 30.2 %all-reduce.7.cloned.1.call-done = f32[63488]{0:T(1024)} async-done(((f32[63488]{0:T(1024)}), f32[63488]{0:T(1024)}) %all-reduce.7.cloned.1.call-update) | async-done | bytes 253968
  191.3 1.7 maximum_select_fusion.1
  193.0 5.8 %all-gather = f32[4,1,15872]{2,1,0:T(1,128)S(1)} all-gather(f32[1,1,15872]{2,1,0:T(1,128)S(1)} %reshape.119), channel_id=1, replica_groups=mesh['row'=8,'col'=4] {'col'}, dimensions={0}, use_global_device_ids=true | all-gather | bytes 317440 | tf_op jit(solution)/shard_map/all_gather | solution.py:60
  198.8 0.7 copy.25
  (4 shorter events, 0.1 us)
Async XLA Ops:
  7.2 110.6 %all-reduce.5.cloned.1.call-start = ((), (), s32[]{:S(2)}) async-start(), calls=%async_computation | async-start | bytes 3997696
  9.6 3.4 %copy-start.6 = (s32[1,1,128]{2,1,0:T(1,128)S(1)}, s32[1,1,128]{2,1,0:T(1,128)}, u32[]{:S(2)}) copy-start(s32[1,1,128]{2,1,0:T(1,128)} %param.14) | copy-start | bytes 1540
  12.9 2.5 %copy-start.8 = (u32[32]{0:T(128)S(1)}, u32[32]{0:T(128)}, u32[]{:S(2)}) copy-start(u32[32]{0:T(128)} %constant.43) | copy-start | bytes 388
  12.9 3.8 %copy-start.5 = (f32[2]{0:T(128)S(1)}, f32[2]{0:T(128)}, u32[]{:S(2)}) copy-start(f32[2]{0:T(128)} %param.23) | copy-start | bytes 28
  12.9 104.8 %copy-start = (f32[62464]{0:T(1024)S(1)}, f32[62464]{0:T(1024)}, u32[]{:S(2)}) copy-start(f32[62464]{0:T(1024)} %param.15) | copy-start | bytes 749572
  13.0 104.8 %copy-start.1 = (f32[62464]{0:T(1024)S(1)}, f32[62464]{0:T(1024)}, u32[]{:S(2)}) copy-start(f32[62464]{0:T(1024)} %param.19) | copy-start | bytes 749572
  13.0 104.8 %copy-start.2 = (f32[62464]{0:T(1024)S(1)}, f32[62464]{0:T(1024)}, u32[]{:S(2)}) copy-start(f32[62464]{0:T(1024)} %param.18) | copy-start | bytes 749572
  13.0 104.8 %copy-start.3 = (f32[62464]{0:T(1024)S(1)}, f32[62464]{0:T(1024)}, u32[]{:S(2)}) copy-start(f32[62464]{0:T(1024)} %param.17) | copy-start | bytes 749572
  13.0 104.8 %copy-start.4 = (s32[62464]{0:T(1024)S(1)}, s32[62464]{0:T(1024)}, u32[]{:S(2)}) copy-start(s32[62464]{0:T(1024)} %param.20) | copy-start | bytes 749572
  15.4 175.9 %all-reduce.7.cloned.1.call-start = ((), (), s32[]{:S(2)}) async-start(), calls=%async_computation.1 | async-start | bytes 507904
  153.6 6.3 %copy-start.7 = (u32[32]{0:T(128)S(1)}, u32[32]{0:T(128)}, u32[]{:S(2)}) copy-start(u32[32]{0:T(128)} %constant.47) | copy-start | bytes 388
Sparse Core Ops, SparseCore 0:
  15.5 102.1 all-reduce.4
  160.0 31.2 all-reduce.6
where the time goes:
time: 207 us; the launch traced here: 206 us
  waiting for transfers between devices  131 us (63%)
  blocking collectives  38.4 us (19%)
  between operations  15.5 us (7%)
  other arithmetic  9.96 us (5%)
  matrix products  7.84 us (4%)
  local copies, waits for them, and re-layouts  3.97 us (2%)
    unnamed x4, waiting for transfers between devices  131 us
    all_gather x1, blocking collectives, local(): lax.all_gather(extrap, 'row', axis=0, tiled=True).reshape(col_blocks, 128)  32.6 us
    all_gather x1, blocking collectives, local(): dual_next = lax.all_gather(updated, 'col', axis=0, tiled=True)  5.77 us
    dot_general x1, matrix products, local(): jnp.einsum('kij,kj->ki', tiles_here, whole_cols, preferred_element_type=j...  4.46 us
  transfers between devices with their start and end apart: 2, of which 2 were waited for; matrix products, arithmetic and copies ran while one was open for 1% of the time, Pallas kernels for 0%

commit v1 on v0

v1 whole, which is shorter than its diff:
```python
import jax
import jax.numpy as jnp
from jax import lax
from jax.experimental import pallas as pl
from jax.experimental.pallas import tpu as pltpu
from jax.sharding import PartitionSpec as P

TILE = 128
GROUP = 16
SPARE = 8

f32 = jnp.float32
bf16 = jnp.bfloat16
VMEM = pl.BlockSpec(memory_space=pltpu.VMEM)
SMEM = pl.BlockSpec(memory_space=pltpu.SMEM)
HBM = pl.BlockSpec(memory_space=pl.ANY)


def tile_copies(tiles_hbm, tiles_vmem, sems):
    n_groups = tiles_vmem.shape[0] // GROUP
    return [
        pltpu.make_async_copy(
            tiles_hbm.at[pl.ds(g * GROUP, GROUP)],
            tiles_vmem.at[pl.ds(g * GROUP, GROUP)],
            sems.at[g],
        )
        for g in range(n_groups)
    ]


def one_row_of(block, position):
    rows = lax.broadcasted_iota(jnp.int32, block.shape, 0)
    return jnp.where(rows == position, block, 0.0).astype(bf16)


def halves(values):
    high = values.astype(bf16)
    low = (values - high.astype(f32)).astype(bf16)
    return jnp.concatenate([high, low], axis=-1)


def transpose_product_kernel(rows_ref, cols_ref, duals_ref, tiles_hbm, out_ref, tiles_vmem, picked, sems):
    copies = tile_copies(tiles_hbm, tiles_vmem, sems)
    for copy in copies:
        copy.start()
    k_tiles = tiles_vmem.shape[0]
    for k in range(k_tiles):
        picked[pl.ds(k, 1), :] = duals_ref[pl.ds(rows_ref[k], 1), :]
    out_ref[pl.ds(k_tiles, SPARE), :] = jnp.broadcast_to(cols_ref[...].astype(f32), (SPARE, TILE))
    for g, copy in enumerate(copies):
        here = pl.ds(g * GROUP, GROUP)
        block = picked[here, :].astype(bf16).astype(f32)
        left = jnp.concatenate([one_row_of(block, m) for m in range(GROUP)], axis=1)
        copy.wait()
        out_ref[here, :] = jnp.dot(
            left, tiles_vmem[here].reshape(GROUP * TILE, TILE), preferred_element_type=f32
        )


def primal_kernel(
    terms_ref, primal_ref, cost_ref, lower_ref, upper_ref, kind_ref, steps_ref, next_ref, wanted_ref, extrap
):
    sources, rows_each, _ = terms_ref.shape
    k_tiles = rows_each - SPARE
    blocks = primal_ref.shape[0]
    padded = extrap.shape[0]
    first = lax.axis_index("row") * blocks
    block_down = lax.broadcasted_iota(jnp.int32, (blocks, k_tiles), 0)
    masks, terms = [], []
    for s in range(sources):
        places = terms_ref[s, pl.ds(k_tiles, 1), :].astype(jnp.int32) - first
        masks.append(jnp.where(block_down == places, 1.0, 0.0).astype(bf16))
        terms.append(halves(terms_ref[s, pl.ds(0, k_tiles), :]))
    both = jnp.dot(
        jnp.concatenate(masks, axis=1), jnp.concatenate(terms, axis=0), preferred_element_type=f32
    )
    col_sums = both[:, :TILE] + both[:, TILE:]
    primal = primal_ref[...]
    kind = kind_ref[...]
    moved = primal - steps_ref[0] * (cost_ref[...] - col_sums)
    moved = jnp.where(kind % 2 == 1, jnp.maximum(moved, lower_ref[...]), moved)
    moved = jnp.where(kind >= 2, jnp.minimum(moved, upper_ref[...]), moved)
    next_ref[...] = moved
    if padded > blocks:
        extrap[pl.ds(padded - 32, 32), :] = jnp.zeros((32, TILE), f32)
    extrap[pl.ds(0, blocks), :] = 2.0 * moved - primal
    right = extrap[...].astype(bf16)
    block_across = lax.broadcasted_iota(jnp.int32, (k_tiles, padded), 1)
    for s in range(sources):
        places = jnp.transpose(terms_ref[s, pl.ds(k_tiles, SPARE), :])[:, 0:1].astype(jnp.int32) - first
        places = jnp.where(places < blocks, places, -1)
        mask = jnp.where(block_across == places, 1.0, 0.0).astype(bf16)
        wanted_ref[s] = jnp.dot(mask, right, preferred_element_type=f32).astype(bf16)


def product_kernel(rows_ref, wanted_ref, tiles_hbm, out_ref, tiles_vmem, sems):
    copies = tile_copies(tiles_hbm, tiles_vmem, sems)
    for copy in copies:
        copy.start()
    k_tiles = tiles_vmem.shape[0]
    out_ref[pl.ds(k_tiles, SPARE), :] = jnp.broadcast_to(rows_ref[...].astype(f32), (SPARE, TILE))
    for g, copy in enumerate(copies):
        here = pl.ds(g * GROUP, GROUP)
        block = jnp.zeros((GROUP, TILE), f32)
        for s in range(wanted_ref.shape[0]):
            block += wanted_ref[s, here, :].astype(f32)
        copy.wait()
        total = jnp.zeros((GROUP, TILE), f32)
        for m in range(GROUP):
            total += lax.dot_general(
                one_row_of(block, m),
                tiles_vmem[g * GROUP + m],
                (((1,), (1,)), ((), ())),
                preferred_element_type=f32,
            )
        out_ref[here, :] = total


def dual_kernel(terms_ref, duals_ref, right_ref, kind_ref, steps_ref, next_ref):
    sources, rows_each, _ = terms_ref.shape
    k_tiles = rows_each - SPARE
    blocks = duals_ref.shape[0]
    block_down = lax.broadcasted_iota(jnp.int32, (blocks, k_tiles), 0)
    masks, terms = [], []
    for s in range(sources):
        places = terms_ref[s, pl.ds(k_tiles, 1), :].astype(jnp.int32)
        masks.append(jnp.where(block_down == places, 1.0, 0.0).astype(bf16))
        terms.append(halves(terms_ref[s, pl.ds(0, k_tiles), :]))
    both = jnp.dot(
        jnp.concatenate(masks, axis=1), jnp.concatenate(terms, axis=0), preferred_element_type=f32
    )
    row_sums = both[:, :TILE] + both[:, TILE:]
    updated = duals_ref[...] + steps_ref[1] * (right_ref[...] - row_sums)
    next_ref[...] = jnp.where(kind_ref[...] == 1, jnp.maximum(updated, 0.0), updated)


def local(
    block_tiles,
    tile_row,
    tile_col,
    primal,
    duals,
    cost_vec,
    lower_bound,
    upper_bound,
    bound_kind,
    right_side,
    row_kind,
    step_sizes,
):
    k_tiles = block_tiles.shape[2]
    tiles = block_tiles.reshape(k_tiles, TILE, TILE)
    n_row = lax.axis_size("row")
    col_blocks = primal.shape[0] // TILE
    row_blocks = duals.shape[0] // TILE
    padded = -(-col_blocks // TILE) * TILE
    n_groups = k_tiles // GROUP
    by_block = lambda array: array.reshape(-1, TILE)
    tiles_scratch = pltpu.VMEM((k_tiles, TILE, TILE), bf16)
    payload = jax.ShapeDtypeStruct((k_tiles + SPARE, TILE), f32)
    params = pltpu.CompilerParams(vmem_limit_bytes=32 * 1024 * 1024)

    col_terms = pl.pallas_call(
        transpose_product_kernel,
        out_shape=payload,
        in_specs=[SMEM, VMEM, VMEM, HBM],
        out_specs=VMEM,
        scratch_shapes=[tiles_scratch, pltpu.VMEM((k_tiles, TILE), f32), pltpu.SemaphoreType.DMA((n_groups,))],
        compiler_params=params,
        name="transpose_product",
    )(tile_row.reshape(-1), tile_col.reshape(1, k_tiles), by_block(duals), tiles)
    all_col_terms = lax.all_gather(col_terms, "row")
    primal_next, wanted = pl.pallas_call(
        primal_kernel,
        out_shape=(
            jax.ShapeDtypeStruct((col_blocks, TILE), f32),
            jax.ShapeDtypeStruct((n_row, k_tiles, TILE), bf16),
        ),
        in_specs=[VMEM] * 6 + [SMEM],
        out_specs=(VMEM, VMEM),
        scratch_shapes=[pltpu.VMEM((padded, TILE), f32)],
        compiler_params=params,
        name="primal_step",
    )(
        all_col_terms,
        by_block(primal),
        by_block(cost_vec),
        by_block(lower_bound),
        by_block(upper_bound),
        by_block(bound_kind),
        step_sizes,
    )
    arrived = lax.all_to_all(wanted, "row", 0, 0)
    row_terms = pl.pallas_call(
        product_kernel,
        out_shape=payload,
        in_specs=[VMEM, VMEM, HBM],
        out_specs=VMEM,
        scratch_shapes=[tiles_scratch, pltpu.SemaphoreType.DMA((n_groups,))],
        compiler_params=params,
        name="product",
    )(tile_row.reshape(1, k_tiles), arrived, tiles)
    all_row_terms = lax.all_gather(row_terms, "col")
    dual_next = pl.pallas_call(
        dual_kernel,
        out_shape=jax.ShapeDtypeStruct((row_blocks, TILE), f32),
        in_specs=[VMEM] * 4 + [SMEM],
        out_specs=VMEM,
        compiler_params=params,
        name="dual_step",
    )(all_row_terms, by_block(duals), by_block(right_side), by_block(row_kind), step_sizes)
    return (primal_next.reshape(-1), dual_next.reshape(-1))


def solution(mesh):
    return jax.shard_map(
        local,
        mesh=mesh,
        in_specs=(
            P("row", "col", None, None, None),
            P("row", "col", None),
            P("row", "col", None),
            P(("col", "row")),
            P("row"),
            P(("col", "row")),
            P(("col", "row")),
            P(("col", "row")),
            P(("col", "row")),
            P("row"),
            P("row"),
            P(),
        ),
        out_specs=(P(("col", "row")), P("row")),
        check_vma=False,
    )
```

time: 207 us -> 71.8 us (0.35)
  waiting for transfers between devices: 131 us -> 0 us
  between operations: 15.5 us -> 0.73 us
  blocking collectives: 38.4 us -> 52.8 us
  Pallas kernels: 0 us -> 11.7 us
  other arithmetic: 9.96 us -> 0 us
  matrix products: 7.84 us -> 0 us
  local copies, waits for them, and re-layouts: 3.97 us -> 6.38 us
    unnamed x4 -> x0, waiting for transfers between devices: 131 us -> none
    all_to_all x0 -> x1, blocking collectives: none -> 13.6 us  [local(): arrived = lax.all_to_all(wanted, 'row', 0, 0)]
    pallas_call x0 -> x4, Pallas kernels: none -> 11.7 us  [the longest x1 5.62 us: local(): pl.pallas_call(product_kernel, out_shape=payload, in_specs=[VMEM, VMEM, H...]
    dot_general x2 -> x0, matrix products: 7.84 us -> none  [the longest x1 4.46 us: local(): jnp.einsum('kij,kj->ki', tiles_here, whole_cols, preferred_element_type=j...]
    unnamed x22 -> x30, local copies, waits for them, and re-layouts: 2 us -> 6.38 us
    scatter-add x2 -> x0, other arithmetic: 4.16 us -> none  [the longest x1 2.36 us: local(): jax.ops.segment_sum(col_terms, cols_here, num_segments=col_blocks)]
    convert_element_type x1 -> x0, other arithmetic: 2.49 us -> none  [local(): extrap = (2.0 * primal_next - primal).astype(jnp.bfloat16)]
    select_n x3 -> x0, other arithmetic: 2.34 us -> none  [the longest x1 1.67 us: dual_update(): return jnp.where(row_kind == 1, jnp.maximum(updated, 0.0), updated)]
  transfers between devices with their start and end apart: 2 -> 0, of which waited for: 2 -> 0; matrix products, arithmetic and copies ran while one was open for 1% -> 0% of each run, Pallas kernels for 0% -> 0%
where the time goes in v1:
time: 71.8 us; the launch traced here: 71.5 us
  blocking collectives  52.8 us (74%)
  Pallas kernels  11.7 us (16%)
  local copies, waits for them, and re-layouts  6.38 us (9%)
  between operations  0.73 us (1%)
    all_gather x1, blocking collectives, local(): all_col_terms = lax.all_gather(col_terms, 'row')  33.3 us
    all_to_all x1, blocking collectives, local(): arrived = lax.all_to_all(wanted, 'row', 0, 0)  13.6 us
    unnamed x30, local copies, waits for them, and re-layouts  6.38 us
    all_gather x1, blocking collectives, local(): all_row_terms = lax.all_gather(row_terms, 'col')  5.84 us
    pallas_call x1, Pallas kernels, local(): pl.pallas_call(product_kernel, out_shape=payload, in_specs=[VMEM, VMEM, H...  5.62 us
    pallas_call x1, Pallas kernels, local(): pl.pallas_call(transpose_product_kernel, out_shape=payload, in_specs=[SME...  2.48 us
    pallas_call x1, Pallas kernels, local(): pl.pallas_call(primal_kernel, out_shape=(jax.ShapeDtypeStruct((col_blocks...  2.01 us
    pallas_call x1, Pallas kernels, local(): pl.pallas_call(dual_kernel, out_shape=jax.ShapeDtypeStruct((row_blocks, T...  1.54 us

profile of v1, /device:TPU:0, one launch (start us, length us, event | category | flops | bytes accessed | tf_op | source)
XLA Modules:
  0.0 71.5 jit_solution(11913234082070250166)
XLA Ops:
  0.6 0.0 copy-start.13
  0.6 0.0 copy-start.11
  0.7 0.0 copy-start
  0.7 2.2 %copy-done = bf16[1,1,128,128,128]{4,3,2,1,0:T(8,128)(2,1)S(1)} copy-done((bf16[1,1,128,128,128]{4,3,2,1,0:T(8,128)(2,1)S(1)}, bf16[1,1,128,128,128]{4,3,2,1,0:T(8,128)(2,1)}, u32[]{:S(2)}) %copy-start) | copy-done | bytes 4194328
  2.9 0.0 copy-start.2
  2.9 0.9 %copy-done.2 = f32[63488]{0:T(1024)S(1)} copy-done((f32[63488]{0:T(1024)S(1)}, f32[63488]{0:T(1024)}, u32[]{:S(2)}) %copy-start.2) | copy-done | bytes 253976
  3.8 0.0 copy-start.12
  3.8 0.7 copy-done.12
  4.5 0.0 copy-start.14
  4.5 0.7 copy-done.14
  5.1 0.0 copy-start.6
  5.1 0.0 copy-start.7
  5.1 0.0 copy-start.8
  5.1 0.0 copy-start.1
  5.1 2.5 %transpose_product.1 = f32[136,128]{1,0:T(8,128)S(1)} custom-call(s32[128]{0:T(128)S(1)} %bitcast.29, s32[1,128]{1,0:T(1,128)S(1)} %bitcast.31, f32[496,128]{1,0:T(8,128)S(1)} %bitcast.20, bf16[128,128,128]{2,1,0:T(8,128)(2,1)S(1)} %bitcast.16), custom_call_target="tpu_custom_call" | custom-call | tf_op jit(solution)/shard_map/transpose_product/pallas_call | solution.py:163
  7.6 0.0 copy-start.3
  7.6 0.0 copy-start.4
  7.6 0.0 copy-start.5
  7.7 33.3 %all-gather = f32[1088,128]{1,0:T(8,128)S(1)} all-gather(f32[136,128]{1,0:T(8,128)S(1)} %transpose_product.1), channel_id=2, replica_groups=mesh['row'=8,'col'=4] {'row'}, dimensions={0}, use_global_device_ids=true | all-gather | bytes 626688 | tf_op jit(solution)/shard_map/all_gather | solution.py:172
  41.0 0.0 copy-done.11
  41.0 0.0 copy-done.6
  41.0 0.0 copy-done.7
  41.0 0.0 copy-done.8
  41.0 0.0 copy-start.9
  41.0 0.9 %copy-done.9 = f32[62464]{0:T(1024)S(1)} copy-done((f32[62464]{0:T(1024)S(1)}, f32[62464]{0:T(1024)}, u32[]{:S(2)}) %copy-start.9) | copy-done | bytes 249880
  41.9 0.0 copy-start.10
  41.9 0.9 %copy-done.10 = s32[62464]{0:T(1024)S(1)} copy-done((s32[62464]{0:T(1024)S(1)}, s32[62464]{0:T(1024)}, u32[]{:S(2)}) %copy-start.10) | copy-done | bytes 249880
  42.9 2.0 %primal_step.1 = (f32[488,128]{1,0:T(8,128)}, bf16[8,128,128]{2,1,0:T(8,128)(2,1)S(1)}) custom-call(f32[8,136,128]{2,1,0:T(8,128)S(1)} %bitcast.18, f32[488,128]{1,0:T(8,128)S(1)} %bitcast.24, f32[488,128]{1,0:T(8,128)S(1)} %bitcast.25, f32[488,128]{1,0:T(8,128)S(1)} %bitcast.26, f32[488,128]{1,0:T(8,128)S(1)} %bitcast.27, s32[488,128]{1,0:T(8,128)S(1)} %bitcast.28, ...), custom_call_target="tpu_custom_call" | custom-call | tf_op jit(solution)/shard_map/primal_step/pallas_call | solution.py:173
  44.9 13.6 %all_to_all.5.wanted_ref = bf16[8,128,128]{2,1,0:T(8,128)(2,1)S(1)} all-to-all(bf16[8,128,128]{2,1,0:T(8,128)(2,1)S(1)} %get-tuple-element.5), channel_id=1, replica_groups=mesh['row'=8,'col'=4] {'row'}, dimensions={0} | all-to-all | bytes 524288 | tf_op jit(solution)/shard_map/all_to_all | solution.py:193
  58.5 0.0 copy-done.13
  58.5 0.0 copy-done.1
  58.5 5.6 %product.1 = f32[136,128]{1,0:T(8,128)S(1)} custom-call(s32[1,128]{1,0:T(1,128)S(1)} %bitcast.30, bf16[8,128,128]{2,1,0:T(8,128)(2,1)S(1)} %all_to_all.5.wanted_ref, bf16[128,128,128]{2,1,0:T(8,128)(2,1)S(1)} %bitcast.17), custom_call_target="tpu_custom_call" | custom-call | tf_op jit(solution)/shard_map/product/pallas_call | solution.py:194
  64.1 5.8 %all-gather.1 = f32[544,128]{1,0:T(8,128)S(1)} all-gather(f32[136,128]{1,0:T(8,128)S(1)} %product.1), channel_id=3, replica_groups=mesh['row'=8,'col'=4] {'col'}, dimensions={0}, use_global_device_ids=true | all-gather | bytes 348160 | tf_op jit(solution)/shard_map/all_gather | solution.py:203
  70.0 0.0 copy-done.3
  70.0 0.0 copy-done.4
  70.0 0.0 copy-done.5
  70.0 1.5 %dual_step.1 = f32[496,128]{1,0:T(8,128)} custom-call(f32[4,136,128]{2,1,0:T(8,128)S(1)} %bitcast.19, f32[496,128]{1,0:T(8,128)S(1)} %bitcast.21, f32[496,128]{1,0:T(8,128)S(1)} %bitcast.22, s32[496,128]{1,0:T(8,128)S(1)} %bitcast.23, f32[2]{0:T(128)S(1)} %copy-done.11), custom_call_target="tpu_custom_call" | custom-call | tf_op jit(solution)/shard_map/dual_step/pallas_call | solution.py:204
Async XLA Ops:
  0.6 57.9 %copy-start.13 = (s32[1,1,128]{2,1,0:T(1,128)S(1)}, s32[1,1,128]{2,1,0:T(1,128)}, u32[]{:S(2)}) copy-start(s32[1,1,128]{2,1,0:T(1,128)} %param.13) | copy-start | bytes 1540
  0.6 40.3 %copy-start.11 = (f32[2]{0:T(128)S(1)}, f32[2]{0:T(128)}, u32[]{:S(2)}) copy-start(f32[2]{0:T(128)} %steps_ref.3) | copy-start | bytes 28
  0.7 2.2 %copy-start = (bf16[1,1,128,128,128]{4,3,2,1,0:T(8,128)(2,1)S(1)}, bf16[1,1,128,128,128]{4,3,2,1,0:T(8,128)(2,1)}, u32[]{:S(2)}) copy-start(bf16[1,1,128,128,128]{4,3,2,1,0:T(8,128)(2,1)} %param.12) | copy-start | bytes 12582916
  2.9 0.9 %copy-start.2 = (f32[63488]{0:T(1024)S(1)}, f32[63488]{0:T(1024)}, u32[]{:S(2)}) copy-start(f32[63488]{0:T(1024)} %param.16) | copy-start | bytes 761860
  3.8 0.7 copy-start.12
  4.5 0.7 copy-start.14
  5.1 35.9 %copy-start.6 = (f32[62464]{0:T(1024)S(1)}, f32[62464]{0:T(1024)}, u32[]{:S(2)}) copy-start(f32[62464]{0:T(1024)} %param.15) | copy-start | bytes 749572
  5.1 35.9 %copy-start.7 = (f32[62464]{0:T(1024)S(1)}, f32[62464]{0:T(1024)}, u32[]{:S(2)}) copy-start(f32[62464]{0:T(1024)} %param.17) | copy-start | bytes 749572
  5.1 35.9 %copy-start.8 = (f32[62464]{0:T(1024)S(1)}, f32[62464]{0:T(1024)}, u32[]{:S(2)}) copy-start(f32[62464]{0:T(1024)} %param.18) | copy-start | bytes 749572
  5.1 53.4 %copy-start.1 = (bf16[1,1,128,128,128]{4,3,2,1,0:T(8,128)(2,1)S(1)}, bf16[1,1,128,128,128]{4,3,2,1,0:T(8,128)(2,1)}, u32[]{:S(2)}) copy-start(bf16[1,1,128,128,128]{4,3,2,1,0:T(8,128)(2,1)} %param.12) | copy-start | bytes 12582916
  7.6 62.4 %copy-start.3 = (f32[63488]{0:T(1024)S(1)}, f32[63488]{0:T(1024)}, u32[]{:S(2)}) copy-start(f32[63488]{0:T(1024)} %param.16) | copy-start | bytes 761860
  7.6 62.4 %copy-start.4 = (f32[63488]{0:T(1024)S(1)}, f32[63488]{0:T(1024)}, u32[]{:S(2)}) copy-start(f32[63488]{0:T(1024)} %param.21) | copy-start | bytes 761860
  7.6 62.3 %copy-start.5 = (s32[63488]{0:T(1024)S(1)}, s32[63488]{0:T(1024)}, u32[]{:S(2)}) copy-start(s32[63488]{0:T(1024)} %param.22) | copy-start | bytes 761860
  41.0 0.9 %copy-start.9 = (f32[62464]{0:T(1024)S(1)}, f32[62464]{0:T(1024)}, u32[]{:S(2)}) copy-start(f32[62464]{0:T(1024)} %param.19) | copy-start | bytes 749572
  41.9 0.9 %copy-start.10 = (s32[62464]{0:T(1024)S(1)}, s32[62464]{0:T(1024)}, u32[]{:S(2)}) copy-start(s32[62464]{0:T(1024)} %param.20) | copy-start | bytes 749572

commit v2 on v0

v2 whole, which is shorter than its diff:
```python
import jax
import jax.numpy as jnp
from jax import lax
from jax.experimental import pallas as pl
from jax.experimental.pallas import tpu as pltpu
from jax.sharding import PartitionSpec as P

TILE = 128
GROUP = 16
HEAD = 16
BITS = 14

f32 = jnp.float32
bf16 = jnp.bfloat16
i32 = jnp.int32
i16 = jnp.int16
VMEM = pl.BlockSpec(memory_space=pltpu.VMEM)
SMEM = pl.BlockSpec(memory_space=pltpu.SMEM)
HBM = pl.BlockSpec(memory_space=pltpu.HBM)


def iota(shape, axis):
    return lax.broadcasted_iota(i32, shape, axis)


def one_row_of(block, position):
    return jnp.where(iota(block.shape, 0) == position, block, 0.0).astype(bf16)


def coded(values):
    largest = jnp.maximum(jnp.max(jnp.abs(values), axis=1, keepdims=True), 1e-30)
    exponent = jnp.ceil(jnp.log2(largest))
    whole = jnp.floor(values * jnp.exp2(BITS - exponent) + 0.5)
    return whole.astype(i32).astype(i16), jnp.broadcast_to(exponent, values.shape)


def head_of(places, exponents):
    across = jnp.transpose(exponents)[0:HEAD, :].astype(i32)
    return jnp.where(iota((HEAD, TILE), 0) == 0, places, across).astype(i16)


def block_sums(payloads, first, blocks):
    down = iota((blocks, TILE), 0)
    masks, terms = [], []
    for payload in payloads:
        k_tiles = payload.shape[0] - HEAD
        head = payload[pl.ds(k_tiles, HEAD), :].astype(i32)
        scale = jnp.exp2(head[1:2, :].astype(f32) - BITS)
        masks.append(jnp.where(down == head[0:1, :] - first, scale, 0.0).astype(bf16))
        whole = payload[pl.ds(0, k_tiles), :].astype(i32)
        low = jnp.bitwise_and(whole, 255)
        parts = [(whole - low).astype(f32).astype(bf16), low.astype(f32).astype(bf16)]
        terms.append(jnp.concatenate(parts, axis=1))
    both = jnp.dot(
        jnp.concatenate(masks, axis=1), jnp.concatenate(terms, axis=0), preferred_element_type=f32
    )
    return both[:, :TILE] + both[:, TILE:]


def started(sources, targets, sems):
    copies = [
        pltpu.make_async_copy(source, target, sems.at[n])
        for n, (source, target) in enumerate(zip(sources, targets))
    ]
    for copy in copies:
        copy.start()
    return copies


def transpose_product_kernel(
    rows_hbm, cols_hbm, duals_hbm, tiles_hbm, out_ref, rows, cols, duals, tiles, picked, exponents, sems
):
    k_tiles = tiles.shape[0]
    n_groups = k_tiles // GROUP
    small = [
        pltpu.make_async_copy(source, target, sems.at[n_groups + n])
        for n, (source, target) in enumerate([(rows_hbm, rows), (duals_hbm, duals), (cols_hbm, cols)])
    ]
    large = [
        pltpu.make_async_copy(
            tiles_hbm.at[pl.ds(g * GROUP, GROUP)], tiles.at[pl.ds(g * GROUP, GROUP)], sems.at[g]
        )
        for g in range(n_groups)
    ]
    for copy in small + large:
        copy.start()
    for copy in small:
        copy.wait()
    for k in range(k_tiles):
        picked[pl.ds(k, 1), :] = duals[pl.ds(rows[k], 1), :]
    for g, copy in enumerate(large):
        here = pl.ds(g * GROUP, GROUP)
        block = picked[here, :].astype(bf16).astype(f32)
        left = jnp.concatenate([one_row_of(block, m) for m in range(GROUP)], axis=1)
        copy.wait()
        terms = jnp.dot(left, tiles[here].reshape(GROUP * TILE, TILE), preferred_element_type=f32)
        out_ref[here, :], exponents[here, :] = coded(terms)
    out_ref[pl.ds(k_tiles, HEAD), :] = head_of(cols[...], exponents[...])


def primal_kernel(n_row, *refs):
    payloads, refs = refs[:n_row], refs[n_row:]
    sources, (steps_ref, next_ref), refs = refs[:5], refs[5:7], refs[7:]
    wanted, (extrap, *local_refs, sems) = refs[:n_row], refs[n_row:]
    primal_ref, cost_ref, lower_ref, upper_ref, kind_ref = local_refs
    copies = started(sources, local_refs, sems)
    blocks = primal_ref.shape[0]
    padded = extrap.shape[0]
    first = lax.axis_index("row") * blocks
    col_sums = block_sums(payloads, first, blocks)
    for copy in copies:
        copy.wait()
    primal = primal_ref[...]
    kind = kind_ref[...]
    moved = primal - steps_ref[0] * (cost_ref[...] - col_sums)
    moved = jnp.where(kind % 2 == 1, jnp.maximum(moved, lower_ref[...]), moved)
    moved = jnp.where(kind >= 2, jnp.minimum(moved, upper_ref[...]), moved)
    next_ref[...] = moved
    whole = blocks // 8 * 8
    if padded > whole:
        extrap[pl.ds(whole, padded - whole), :] = jnp.zeros((padded - whole, TILE), f32)
    extrap[pl.ds(0, blocks), :] = 2.0 * moved - primal
    right = extrap[...].astype(bf16)
    for payload, target in zip(payloads, wanted):
        k_tiles = target.shape[0]
        head = payload[pl.ds(k_tiles, HEAD), :].astype(i32)
        places = jnp.transpose(head.astype(f32))[:, 0:1].astype(i32) - first
        mask = jnp.where(iota((k_tiles, padded), 1) == places, 1.0, 0.0)
        target[...] = jnp.dot(mask.astype(bf16), right, preferred_element_type=f32).astype(bf16)


def product_kernel(rows_ref, tiles_ref, *refs):
    arrived, out_ref = refs[:-1], refs[-1]
    k_tiles = tiles_ref.shape[0]
    block = arrived[0][...].astype(f32)
    for ref in arrived[1:]:
        block += ref[...].astype(f32)
    down = jnp.transpose(block)
    lane = iota((TILE, k_tiles), 1)
    right = jnp.concatenate(
        [jnp.where(lane % 2 == 0, down, 0.0), jnp.where(lane % 2 == 1, down, 0.0)], axis=0
    ).astype(bf16)
    terms = jnp.zeros((TILE, k_tiles), f32)
    for g in range(k_tiles // 8):
        even = jnp.concatenate([tiles_ref[8 * g + m] for m in (0, 2, 4, 6)], axis=0)
        odd = jnp.concatenate([tiles_ref[8 * g + m] for m in (1, 3, 5, 7)], axis=0)
        products = jnp.dot(jnp.concatenate([even, odd], axis=1), right, preferred_element_type=f32)
        for p in range(4):
            terms = jnp.where(lane // 2 == 4 * g + p, products[p * TILE : (p + 1) * TILE], terms)
    out_ref[pl.ds(0, k_tiles), :], exponents = coded(jnp.transpose(terms))
    out_ref[pl.ds(k_tiles, HEAD), :] = head_of(rows_ref[...], exponents)


def dual_kernel(n_col, *refs):
    payloads, sources, (steps_ref, next_ref) = refs[:n_col], refs[n_col : n_col + 3], refs[n_col + 3 : n_col + 5]
    *local_refs, sems = refs[n_col + 5 :]
    duals_ref, right_ref, kind_ref = local_refs
    copies = started(sources, local_refs, sems)
    row_sums = block_sums(payloads, 0, duals_ref.shape[0])
    for copy in copies:
        copy.wait()
    updated = duals_ref[...] + steps_ref[1] * (right_ref[...] - row_sums)
    next_ref[...] = jnp.where(kind_ref[...] == 1, jnp.maximum(updated, 0.0), updated)


def exchange(arrays, axis, back=False):
    size = lax.axis_size(axis)
    arrived = []
    for n, array in enumerate(arrays):
        if n == 0:
            arrived.append(array)
            continue
        if size & (size - 1) == 0:
            pairs = [(i, i ^ n) for i in range(size)]
        else:
            pairs = [(i, (i + (-n if back else n)) % size) for i in range(size)]
        arrived.append(lax.ppermute(array, axis, pairs))
    return arrived


def local(
    block_tiles,
    tile_row,
    tile_col,
    primal,
    duals,
    cost_vec,
    lower_bound,
    upper_bound,
    bound_kind,
    right_side,
    row_kind,
    step_sizes,
):
    k_tiles = block_tiles.shape[2]
    tiles = block_tiles.reshape(k_tiles, TILE, TILE)
    n_row = lax.axis_size("row")
    n_col = lax.axis_size("col")
    col_blocks = primal.shape[0] // TILE
    row_blocks = duals.shape[0] // TILE
    padded = -(-col_blocks // TILE) * TILE
    in_hbm = lambda array: pltpu.with_memory_space_constraint(array, pltpu.HBM)
    by_block = lambda array: in_hbm(array.reshape(-1, TILE))
    blocks_of = lambda blocks, kind: pltpu.VMEM((blocks, TILE), kind)
    payload = jax.ShapeDtypeStruct((k_tiles + HEAD, TILE), i16)
    block = jax.ShapeDtypeStruct((k_tiles, TILE), bf16)
    params = pltpu.CompilerParams(vmem_limit_bytes=32 * 1024 * 1024)

    col_terms = pl.pallas_call(
        transpose_product_kernel,
        out_shape=payload,
        in_specs=[HBM] * 4,
        out_specs=VMEM,
        scratch_shapes=[
            pltpu.SMEM((k_tiles,), i32),
            pltpu.VMEM((1, k_tiles), i32),
            pltpu.VMEM((row_blocks, TILE), f32),
            pltpu.VMEM((k_tiles, TILE, TILE), bf16),
            pltpu.VMEM((k_tiles, TILE), f32),
            pltpu.VMEM((k_tiles, TILE), f32),
            pltpu.SemaphoreType.DMA((k_tiles // GROUP + 3,)),
        ],
        compiler_params=params,
        name="transpose_product",
    )(in_hbm(tile_row.reshape(-1)), in_hbm(tile_col.reshape(1, k_tiles)), by_block(duals), in_hbm(tiles))
    primal_next, *wanted = pl.pallas_call(
        lambda *refs: primal_kernel(n_row, *refs),
        out_shape=(jax.ShapeDtypeStruct((col_blocks, TILE), f32), *[block] * n_row),
        in_specs=[VMEM] * n_row + [HBM] * 5 + [SMEM],
        out_specs=(VMEM,) * (n_row + 1),
        scratch_shapes=[
            blocks_of(padded, f32),
            *[blocks_of(col_blocks, f32)] * 4,
            blocks_of(col_blocks, i32),
            pltpu.SemaphoreType.DMA((5,)),
        ],
        compiler_params=params,
        name="primal_step",
    )(
        *exchange([col_terms] * n_row, "row"),
        by_block(primal),
        by_block(cost_vec),
        by_block(lower_bound),
        by_block(upper_bound),
        by_block(bound_kind),
        step_sizes,
    )
    row_terms = pl.pallas_call(
        product_kernel,
        out_shape=payload,
        in_specs=[VMEM] * (n_row + 2),
        out_specs=VMEM,
        compiler_params=params,
        name="product",
    )(tile_row.reshape(1, k_tiles), tiles, *exchange(wanted, "row", back=True))
    dual_next = pl.pallas_call(
        lambda *refs: dual_kernel(n_col, *refs),
        out_shape=jax.ShapeDtypeStruct((row_blocks, TILE), f32),
        in_specs=[VMEM] * n_col + [HBM] * 3 + [SMEM],
        out_specs=VMEM,
        scratch_shapes=[
            *[blocks_of(row_blocks, f32)] * 2,
            blocks_of(row_blocks, i32),
            pltpu.SemaphoreType.DMA((3,)),
        ],
        compiler_params=params,
        name="dual_step",
    )(*exchange([row_terms] * n_col, "col"), by_block(duals), by_block(right_side), by_block(row_kind), step_sizes)
    return (primal_next.reshape(-1), dual_next.reshape(-1))


def solution(mesh):
    return jax.shard_map(
        local,
        mesh=mesh,
        in_specs=(
            P("row", "col", None, None, None),
            P("row", "col", None),
            P("row", "col", None),
            P(("col", "row")),
            P("row"),
            P(("col", "row")),
            P(("col", "row")),
            P(("col", "row")),
            P(("col", "row")),
            P("row"),
            P("row"),
            P(),
        ),
        out_specs=(P(("col", "row")), P("row")),
        check_vma=False,
    )
```

time: 207 us -> 49.5 us (0.24)
  waiting for transfers between devices: 131 us -> 11.3 us
  blocking collectives: 38.4 us -> 0 us
  starting transfers between devices: 0.08 us -> 25.7 us
  between operations: 15.5 us -> 0.7 us
  Pallas kernels: 0 us -> 11.7 us
  other arithmetic: 9.96 us -> 0 us
  matrix products: 7.84 us -> 0 us
  local copies, waits for them, and re-layouts: 3.97 us -> 0.01 us
    unnamed x4 -> x0, waiting for transfers between devices: 131 us -> none
    all_gather x2 -> x0, blocking collectives: 38.4 us -> none  [the longest x1 32.6 us: local(): lax.all_gather(extrap, 'row', axis=0, tiled=True).reshape(col_blocks, 128)]
    ppermute x0 -> x17, starting transfers between devices: none -> 25.7 us  [exchange(): arrived.append(lax.ppermute(array, axis, pairs))]
    pallas_call x0 -> x4, Pallas kernels: none -> 11.7 us  [the longest x1 3.82 us: local(): pl.pallas_call(lambda *refs: primal_kernel(n_row, *refs), out_shape=(jax....]
    ppermute x0 -> x17, waiting for transfers between devices: none -> 11.3 us  [exchange(): arrived.append(lax.ppermute(array, axis, pairs))]
    dot_general x2 -> x0, matrix products: 7.84 us -> none  [the longest x1 4.46 us: local(): jnp.einsum('kij,kj->ki', tiles_here, whole_cols, preferred_element_type=j...]
    scatter-add x2 -> x0, other arithmetic: 4.16 us -> none  [the longest x1 2.36 us: local(): jax.ops.segment_sum(col_terms, cols_here, num_segments=col_blocks)]
    convert_element_type x1 -> x0, other arithmetic: 2.49 us -> none  [local(): extrap = (2.0 * primal_next - primal).astype(jnp.bfloat16)]
  transfers between devices with their start and end apart: 2 -> 17, of which waited for: 2 -> 10; matrix products, arithmetic and copies ran while one was open for 1% -> 0% of each run, Pallas kernels for 0% -> 0%
where the time goes in v2:
time: 49.5 us; the launch traced here: 49.3 us
  starting transfers between devices  25.7 us (52%)
  Pallas kernels  11.7 us (24%)
  waiting for transfers between devices  11.3 us (23%)
  between operations  0.7 us (1%)
    ppermute x17, starting transfers between devices, exchange(): arrived.append(lax.ppermute(array, axis, pairs))  25.7 us
    ppermute x17, waiting for transfers between devices, exchange(): arrived.append(lax.ppermute(array, axis, pairs))  11.3 us
    pallas_call x1, Pallas kernels, local(): pl.pallas_call(lambda *refs: primal_kernel(n_row, *refs), out_shape=(jax....  3.82 us
    pallas_call x1, Pallas kernels, local(): pl.pallas_call(transpose_product_kernel, out_shape=payload, in_specs=[HBM...  3.75 us
    pallas_call x1, Pallas kernels, local(): pl.pallas_call(lambda *refs: dual_kernel(n_col, *refs), out_shape=jax.Sha...  2.55 us
    pallas_call x1, Pallas kernels, local(): pl.pallas_call(product_kernel, out_shape=payload, in_specs=[VMEM] * (n_ro...  1.55 us
  transfers between devices with their start and end apart: 17, of which 10 were waited for; matrix products, arithmetic and copies ran while one was open for 0% of the time, Pallas kernels for 0%

profile of v2, /device:TPU:0, one launch (start us, length us, event | category | flops | bytes accessed | tf_op | source)
XLA Modules:
  0.0 49.3 jit_solution(13977170259740988764)
XLA Ops:
  0.6 0.0 copy-start.2
  0.6 0.0 copy-start
  0.7 0.0 copy-start.1
  0.7 3.7 %transpose_product.1.refs_0_ = s16[144,128]{1,0:T(8,128)(2,1)S(1)} custom-call(s32[128]{0:T(128)} %bitcast.16, s32[1,128]{1,0:T(1,128)} %bitcast.28, f32[496,128]{1,0:T(8,128)} %bitcast.18, bf16[128,128,128]{2,1,0:T(8,128)(2,1)} %bitcast.14), custom_call_target="tpu_custom_call" | custom-call | tf_op jit(solution)/shard_map/transpose_product/pallas_call | solution.py:209
  4.4 6.1 %collective-permute-start.6 = (s16[144,128]{1,0:T(8,128)(2,1)S(1)}, s16[144,128]{1,0:T(8,128)(2,1)S(1)}, u32[]{:S(2)}, u32[]{:S(2)}) collective-permute-start(s16[144,128]{1,0:T(8,128)(2,1)S(1)} %transpose_product.1.refs_0_), channel_id=1, source_target_pairs={{0,28},{4,24},{8,20},{12,16},{16,12},{20,8},{24,4},{28,0},{1,29},{... | collective-permute-start | bytes 110600 | tf_op jit(solution)/shard_map/ppermute | solution.py:177
  10.5 0.2 collective-permute-start.5
  10.7 0.7 %collective-permute-start.4 = (s16[144,128]{1,0:T(8,128)(2,1)S(1)}, s16[144,128]{1,0:T(8,128)(2,1)S(1)}, u32[]{:S(2)}, u32[]{:S(2)}) collective-permute-start(s16[144,128]{1,0:T(8,128)(2,1)S(1)} %transpose_product.1.refs_0_), channel_id=1, source_target_pairs={{0,20},{4,16},{8,28},{12,24},{16,4},{20,0},{24,12},{28,8},{1,21},{... | collective-permute-start | bytes 110600 | tf_op jit(solution)/shard_map/ppermute | solution.py:177
  11.4 2.0 %collective-permute-start.3 = (s16[144,128]{1,0:T(8,128)(2,1)S(1)}, s16[144,128]{1,0:T(8,128)(2,1)S(1)}, u32[]{:S(2)}, u32[]{:S(2)}) collective-permute-start(s16[144,128]{1,0:T(8,128)(2,1)S(1)} %transpose_product.1.refs_0_), channel_id=1, source_target_pairs={{0,16},{4,20},{8,24},{12,28},{16,0},{20,4},{24,8},{28,12},{1,17},{... | collective-permute-start | bytes 110600 | tf_op jit(solution)/shard_map/ppermute | solution.py:177
  13.5 2.3 %collective-permute-start.2 = (s16[144,128]{1,0:T(8,128)(2,1)S(1)}, s16[144,128]{1,0:T(8,128)(2,1)S(1)}, u32[]{:S(2)}, u32[]{:S(2)}) collective-permute-start(s16[144,128]{1,0:T(8,128)(2,1)S(1)} %transpose_product.1.refs_0_), channel_id=1, source_target_pairs={{0,12},{4,8},{8,4},{12,0},{16,28},{20,24},{24,20},{28,16},{1,13},{... | collective-permute-start | bytes 110600 | tf_op jit(solution)/shard_map/ppermute | solution.py:177
  15.8 0.0 collective-permute-done.6.refs_7_
  15.8 0.8 %collective-permute-start.1 = (s16[144,128]{1,0:T(8,128)(2,1)S(1)}, s16[144,128]{1,0:T(8,128)(2,1)S(1)}, u32[]{:S(2)}, u32[]{:S(2)}) collective-permute-start(s16[144,128]{1,0:T(8,128)(2,1)S(1)} %transpose_product.1.refs_0_), channel_id=1, source_target_pairs={{0,8},{4,12},{8,0},{12,4},{16,24},{20,28},{24,16},{28,20},{1,9},{5... | collective-permute-start | bytes 110600 | tf_op jit(solution)/shard_map/ppermute | solution.py:177
  16.6 0.0 collective-permute-done.5.refs_6_
  16.6 0.4 collective-permute-start
  17.0 0.2 collective-permute-done.4.refs_5_
  17.1 0.3 collective-permute-done.3.refs_4_
  17.5 0.9 %collective-permute-done.2.refs_3_ = s16[144,128]{1,0:T(8,128)(2,1)S(1)} collective-permute-done((s16[144,128]{1,0:T(8,128)(2,1)S(1)}, s16[144,128]{1,0:T(8,128)(2,1)S(1)}, u32[]{:S(2)}, u32[]{:S(2)}) %collective-permute-start.2) | collective-permute-done | bytes 36896 | tf_op jit(solution)/shard_map/ppermute | solution.py:177
  18.4 1.4 %collective-permute-done.1.refs_2_ = s16[144,128]{1,0:T(8,128)(2,1)S(1)} collective-permute-done((s16[144,128]{1,0:T(8,128)(2,1)S(1)}, s16[144,128]{1,0:T(8,128)(2,1)S(1)}, u32[]{:S(2)}, u32[]{:S(2)}) %collective-permute-start.1) | collective-permute-done | bytes 36896 | tf_op jit(solution)/shard_map/ppermute | solution.py:177
  19.7 0.8 %collective-permute-done.refs_1_ = s16[144,128]{1,0:T(8,128)(2,1)S(1)} collective-permute-done((s16[144,128]{1,0:T(8,128)(2,1)S(1)}, s16[144,128]{1,0:T(8,128)(2,1)S(1)}, u32[]{:S(2)}, u32[]{:S(2)}) %collective-permute-start) | collective-permute-done | bytes 36896 | tf_op jit(solution)/shard_map/ppermute | solution.py:177
  20.5 0.0 copy-done.1
  20.5 3.8 %primal_step.1 = (f32[488,128]{1,0:T(8,128)}, bf16[128,128]{1,0:T(8,128)(2,1)S(1)}, bf16[128,128]{1,0:T(8,128)(2,1)S(1)}, bf16[128,128]{1,0:T(8,128)(2,1)S(1)}, ...) custom-call(s16[144,128]{1,0:T(8,128)(2,1)S(1)} %transpose_product.1, ...), custom_call_target="tpu_custom_call" | custom-call | tf_op jit(solution)/shard_map/primal_step/pallas_call | solution.py:226
  24.4 0.5 collective-permute-start.7
  24.8 1.4 %collective-permute-start.8 = (bf16[128,128]{1,0:T(8,128)(2,1)S(1)}, bf16[128,128]{1,0:T(8,128)(2,1)S(1)}, u32[]{:S(2)}, u32[]{:S(2)}) collective-permute-start(bf16[128,128]{1,0:T(8,128)(2,1)S(1)} %get-tuple-element.14), channel_id=1, source_target_pairs={{0,8},{4,12},{8,0},{12,4},{16,24},{20,28},{24,16},{28,20},{1,9},{5... | collective-permute-start | bytes 98312 | tf_op jit(solution)/shard_map/ppermute | solution.py:177
  26.2 1.7 %collective-permute-start.9 = (bf16[128,128]{1,0:T(8,128)(2,1)S(1)}, bf16[128,128]{1,0:T(8,128)(2,1)S(1)}, u32[]{:S(2)}, u32[]{:S(2)}) collective-permute-start(bf16[128,128]{1,0:T(8,128)(2,1)S(1)} %get-tuple-element.15), channel_id=1, source_target_pairs={{0,12},{4,8},{8,4},{12,0},{16,28},{20,24},{24,20},{28,16},{1,13},{... | collective-permute-start | bytes 98312 | tf_op jit(solution)/shard_map/ppermute | solution.py:177
  27.9 2.2 %collective-permute-start.10 = (bf16[128,128]{1,0:T(8,128)(2,1)S(1)}, bf16[128,128]{1,0:T(8,128)(2,1)S(1)}, u32[]{:S(2)}, u32[]{:S(2)}) collective-permute-start(bf16[128,128]{1,0:T(8,128)(2,1)S(1)} %get-tuple-element.16), channel_id=1, source_target_pairs={{0,16},{4,20},{8,24},{12,28},{16,0},{20,4},{24,8},{28,12},{1,17},{... | collective-permute-start | bytes 98312 | tf_op jit(solution)/shard_map/ppermute | solution.py:177
  30.1 0.6 %collective-permute-start.11 = (bf16[128,128]{1,0:T(8,128)(2,1)S(1)}, bf16[128,128]{1,0:T(8,128)(2,1)S(1)}, u32[]{:S(2)}, u32[]{:S(2)}) collective-permute-start(bf16[128,128]{1,0:T(8,128)(2,1)S(1)} %get-tuple-element.17), channel_id=1, source_target_pairs={{0,20},{4,16},{8,28},{12,24},{16,4},{20,0},{24,12},{28,8},{1,21},{... | collective-permute-start | bytes 98312 | tf_op jit(solution)/shard_map/ppermute | solution.py:177
  30.7 0.0 collective-permute-done.7.refs_1_
  30.7 3.7 %collective-permute-start.12 = (bf16[128,128]{1,0:T(8,128)(2,1)S(1)}, bf16[128,128]{1,0:T(8,128)(2,1)S(1)}, u32[]{:S(2)}, u32[]{:S(2)}) collective-permute-start(bf16[128,128]{1,0:T(8,128)(2,1)S(1)} %get-tuple-element.18), channel_id=1, source_target_pairs={{0,24},{4,28},{8,16},{12,20},{16,8},{20,12},{24,0},{28,4},{1,25},{... | collective-permute-start | bytes 98312 | tf_op jit(solution)/shard_map/ppermute | solution.py:177
  34.4 0.0 collective-permute-done.8.refs_2_
  34.4 1.2 %collective-permute-start.13 = (bf16[128,128]{1,0:T(8,128)(2,1)S(1)}, bf16[128,128]{1,0:T(8,128)(2,1)S(1)}, u32[]{:S(2)}, u32[]{:S(2)}) collective-permute-start(bf16[128,128]{1,0:T(8,128)(2,1)S(1)} %get-tuple-element.19), channel_id=1, source_target_pairs={{0,28},{4,24},{8,20},{12,16},{16,12},{20,8},{24,4},{28,0},{1,29},{... | collective-permute-start | bytes 98312 | tf_op jit(solution)/shard_map/ppermute | solution.py:177
  35.6 0.0 collective-permute-done.9.refs_3_
  35.6 0.0 collective-permute-done.10.refs_4_
  35.6 0.5 collective-permute-done.11.refs_5_
  36.0 0.6 %collective-permute-done.12.refs_6_ = bf16[128,128]{1,0:T(8,128)(2,1)S(1)} collective-permute-done((bf16[128,128]{1,0:T(8,128)(2,1)S(1)}, bf16[128,128]{1,0:T(8,128)(2,1)S(1)}, u32[]{:S(2)}, u32[]{:S(2)}) %collective-permute-start.12) | collective-permute-done | bytes 32800 | tf_op jit(solution)/shard_map/ppermute | solution.py:177
  36.6 4.4 %collective-permute-done.13.refs_7_ = bf16[128,128]{1,0:T(8,128)(2,1)S(1)} collective-permute-done((bf16[128,128]{1,0:T(8,128)(2,1)S(1)}, bf16[128,128]{1,0:T(8,128)(2,1)S(1)}, u32[]{:S(2)}, u32[]{:S(2)}) %collective-permute-start.13) | collective-permute-done | bytes 32800 | tf_op jit(solution)/shard_map/ppermute | solution.py:177
  41.0 0.0 copy-done.2
  41.0 0.0 copy-done
  41.0 1.6 %product.1.refs_0_ = s16[144,128]{1,0:T(8,128)(2,1)S(1)} custom-call(s32[1,128]{1,0:T(1,128)S(1)} %bitcast.17, bf16[128,128,128]{2,1,0:T(8,128)(2,1)S(1)} %bitcast.15, bf16[128,128]{1,0:T(8,128)(2,1)S(1)} %get-tuple-element.12.refs_0_, bf16[128,128]{1,0:T(8,128)(2,1)S(1)} %collective-permute-done.7.refs_1_, ...), custom_call_target="tpu_custom_call" | custom-call | tf_op jit(solution)/shard_map/product/pallas_call | solution.py:248
  42.6 0.1 collective-permute-start.16
  42.6 1.6 %collective-permute-start.15 = (s16[144,128]{1,0:T(8,128)(2,1)S(1)}, s16[144,128]{1,0:T(8,128)(2,1)S(1)}, u32[]{:S(2)}, u32[]{:S(2)}) collective-permute-start(s16[144,128]{1,0:T(8,128)(2,1)S(1)} %product.1.refs_0_), channel_id=1, source_target_pairs={{0,2},{1,3},{2,0},{3,1},{4,6},{5,7},{6,4},{7,5},{8,10},{9,11},{10,... | collective-permute-start | bytes 110600 | tf_op jit(solution)/shard_map/ppermute | solution.py:177
  44.2 0.3 collective-permute-start.14
  44.5 1.9 %collective-permute-done.16.refs_3_ = s16[144,128]{1,0:T(8,128)(2,1)S(1)} collective-permute-done((s16[144,128]{1,0:T(8,128)(2,1)S(1)}, s16[144,128]{1,0:T(8,128)(2,1)S(1)}, u32[]{:S(2)}, u32[]{:S(2)}) %collective-permute-start.16) | collective-permute-done | bytes 36896 | tf_op jit(solution)/shard_map/ppermute | solution.py:177
  46.3 0.4 collective-permute-done.15.refs_2_
  46.8 0.0 collective-permute-done.14.refs_1_
  46.8 2.5 %dual_step.1 = f32[496,128]{1,0:T(8,128)} custom-call(s16[144,128]{1,0:T(8,128)(2,1)S(1)} %product.1.refs_0_, s16[144,128]{1,0:T(8,128)(2,1)S(1)} %collective-permute-done.14.refs_1_, s16[144,128]{1,0:T(8,128)(2,1)S(1)} %collective-permute-done.15.refs_2_, s16[144,128]{1,0:T(8,128)(2,1)S(1)} %collective-permute-done.16.refs_3_, f32[496,128]{1,0:T(8,128)} %bitcast.19, ...), custom_call_target="tpu_custom_call" | custom-call | tf_op jit(solution)/shard_map/dual_step/pallas_call | solution.py:256
Async XLA Ops:
  0.6 40.4 %copy-start.2 = (s32[1,1,128]{2,1,0:T(1,128)S(1)}, s32[1,1,128]{2,1,0:T(1,128)}, u32[]{:S(2)}) copy-start(s32[1,1,128]{2,1,0:T(1,128)} %param.13) | copy-start | bytes 1540
  0.6 40.4 %copy-start = (bf16[1,1,128,128,128]{4,3,2,1,0:T(8,128)(2,1)S(1)}, bf16[1,1,128,128,128]{4,3,2,1,0:T(8,128)(2,1)}, u32[]{:S(2)}) copy-start(bf16[1,1,128,128,128]{4,3,2,1,0:T(8,128)(2,1)} %param.12) | copy-start | bytes 12582916
  0.7 19.9 %copy-start.1 = (f32[2]{0:T(128)S(1)}, f32[2]{0:T(128)}, u32[]{:S(2)}) copy-start(f32[2]{0:T(128)} %refs_7_.1) | copy-start | bytes 28
  4.4 11.4 %collective-permute-start.6 = (s16[144,128]{1,0:T(8,128)(2,1)S(1)}, s16[144,128]{1,0:T(8,128)(2,1)S(1)}, u32[]{:S(2)}, u32[]{:S(2)}) collective-permute-start(s16[144,128]{1,0:T(8,128)(2,1)S(1)} %transpose_product.1.refs_0_), channel_id=1, source_target_pairs={{0,28},{4,24},{8,20},{12,16},{16,12},{20,8},{24,4},{28,0},{1,29},{... | collective-permute-start | bytes 110600 | tf_op jit(solution)/shard_map/ppermute | solution.py:177
  10.5 6.1 %collective-permute-start.5 = (s16[144,128]{1,0:T(8,128)(2,1)S(1)}, s16[144,128]{1,0:T(8,128)(2,1)S(1)}, u32[]{:S(2)}, u32[]{:S(2)}) collective-permute-start(s16[144,128]{1,0:T(8,128)(2,1)S(1)} %transpose_product.1.refs_0_), channel_id=1, source_target_pairs={{0,24},{4,28},{8,16},{12,20},{16,8},{20,12},{24,0},{28,4},{1,25},{... | collective-permute-start | bytes 110600 | tf_op jit(solution)/shard_map/ppermute | solution.py:177
  10.7 6.4 %collective-permute-start.4 = (s16[144,128]{1,0:T(8,128)(2,1)S(1)}, s16[144,128]{1,0:T(8,128)(2,1)S(1)}, u32[]{:S(2)}, u32[]{:S(2)}) collective-permute-start(s16[144,128]{1,0:T(8,128)(2,1)S(1)} %transpose_product.1.refs_0_), channel_id=1, source_target_pairs={{0,20},{4,16},{8,28},{12,24},{16,4},{20,0},{24,12},{28,8},{1,21},{... | collective-permute-start | bytes 110600 | tf_op jit(solution)/shard_map/ppermute | solution.py:177
  11.4 6.0 %collective-permute-start.3 = (s16[144,128]{1,0:T(8,128)(2,1)S(1)}, s16[144,128]{1,0:T(8,128)(2,1)S(1)}, u32[]{:S(2)}, u32[]{:S(2)}) collective-permute-start(s16[144,128]{1,0:T(8,128)(2,1)S(1)} %transpose_product.1.refs_0_), channel_id=1, source_target_pairs={{0,16},{4,20},{8,24},{12,28},{16,0},{20,4},{24,8},{28,12},{1,17},{... | collective-permute-start | bytes 110600 | tf_op jit(solution)/shard_map/ppermute | solution.py:177
  13.5 4.9 %collective-permute-start.2 = (s16[144,128]{1,0:T(8,128)(2,1)S(1)}, s16[144,128]{1,0:T(8,128)(2,1)S(1)}, u32[]{:S(2)}, u32[]{:S(2)}) collective-permute-start(s16[144,128]{1,0:T(8,128)(2,1)S(1)} %transpose_product.1.refs_0_), channel_id=1, source_target_pairs={{0,12},{4,8},{8,4},{12,0},{16,28},{20,24},{24,20},{28,16},{1,13},{... | collective-permute-start | bytes 110600 | tf_op jit(solution)/shard_map/ppermute | solution.py:177
  15.8 4.0 %collective-permute-start.1 = (s16[144,128]{1,0:T(8,128)(2,1)S(1)}, s16[144,128]{1,0:T(8,128)(2,1)S(1)}, u32[]{:S(2)}, u32[]{:S(2)}) collective-permute-start(s16[144,128]{1,0:T(8,128)(2,1)S(1)} %transpose_product.1.refs_0_), channel_id=1, source_target_pairs={{0,8},{4,12},{8,0},{12,4},{16,24},{20,28},{24,16},{28,20},{1,9},{5... | collective-permute-start | bytes 110600 | tf_op jit(solution)/shard_map/ppermute | solution.py:177
  16.6 4.0 %collective-permute-start = (s16[144,128]{1,0:T(8,128)(2,1)S(1)}, s16[144,128]{1,0:T(8,128)(2,1)S(1)}, u32[]{:S(2)}, u32[]{:S(2)}) collective-permute-start(s16[144,128]{1,0:T(8,128)(2,1)S(1)} %transpose_product.1.refs_0_), channel_id=1, source_target_pairs={{0,4},{4,0},{8,12},{12,8},{16,20},{20,16},{24,28},{28,24},{1,5},{5... | collective-permute-start | bytes 110600 | tf_op jit(solution)/shard_map/ppermute | solution.py:177
  24.4 6.3 %collective-permute-start.7 = (bf16[128,128]{1,0:T(8,128)(2,1)S(1)}, bf16[128,128]{1,0:T(8,128)(2,1)S(1)}, u32[]{:S(2)}, u32[]{:S(2)}) collective-permute-start(bf16[128,128]{1,0:T(8,128)(2,1)S(1)} %get-tuple-element.13), channel_id=1, source_target_pairs={{0,4},{4,0},{8,12},{12,8},{16,20},{20,16},{24,28},{28,24},{1,5},{5... | collective-permute-start | bytes 98312 | tf_op jit(solution)/shard_map/ppermute | solution.py:177
  24.8 9.5 %collective-permute-start.8 = (bf16[128,128]{1,0:T(8,128)(2,1)S(1)}, bf16[128,128]{1,0:T(8,128)(2,1)S(1)}, u32[]{:S(2)}, u32[]{:S(2)}) collective-permute-start(bf16[128,128]{1,0:T(8,128)(2,1)S(1)} %get-tuple-element.14), channel_id=1, source_target_pairs={{0,8},{4,12},{8,0},{12,4},{16,24},{20,28},{24,16},{28,20},{1,9},{5... | collective-permute-start | bytes 98312 | tf_op jit(solution)/shard_map/ppermute | solution.py:177
  26.2 9.3 %collective-permute-start.9 = (bf16[128,128]{1,0:T(8,128)(2,1)S(1)}, bf16[128,128]{1,0:T(8,128)(2,1)S(1)}, u32[]{:S(2)}, u32[]{:S(2)}) collective-permute-start(bf16[128,128]{1,0:T(8,128)(2,1)S(1)} %get-tuple-element.15), channel_id=1, source_target_pairs={{0,12},{4,8},{8,4},{12,0},{16,28},{20,24},{24,20},{28,16},{1,13},{... | collective-permute-start | bytes 98312 | tf_op jit(solution)/shard_map/ppermute | solution.py:177
  27.9 7.7 %collective-permute-start.10 = (bf16[128,128]{1,0:T(8,128)(2,1)S(1)}, bf16[128,128]{1,0:T(8,128)(2,1)S(1)}, u32[]{:S(2)}, u32[]{:S(2)}) collective-permute-start(bf16[128,128]{1,0:T(8,128)(2,1)S(1)} %get-tuple-element.16), channel_id=1, source_target_pairs={{0,16},{4,20},{8,24},{12,28},{16,0},{20,4},{24,8},{28,12},{1,17},{... | collective-permute-start | bytes 98312 | tf_op jit(solution)/shard_map/ppermute | solution.py:177
  30.1 5.9 %collective-permute-start.11 = (bf16[128,128]{1,0:T(8,128)(2,1)S(1)}, bf16[128,128]{1,0:T(8,128)(2,1)S(1)}, u32[]{:S(2)}, u32[]{:S(2)}) collective-permute-start(bf16[128,128]{1,0:T(8,128)(2,1)S(1)} %get-tuple-element.17), channel_id=1, source_target_pairs={{0,20},{4,16},{8,28},{12,24},{16,4},{20,0},{24,12},{28,8},{1,21},{... | collective-permute-start | bytes 98312 | tf_op jit(solution)/shard_map/ppermute | solution.py:177
  30.7 5.9 %collective-permute-start.12 = (bf16[128,128]{1,0:T(8,128)(2,1)S(1)}, bf16[128,128]{1,0:T(8,128)(2,1)S(1)}, u32[]{:S(2)}, u32[]{:S(2)}) collective-permute-start(bf16[128,128]{1,0:T(8,128)(2,1)S(1)} %get-tuple-element.18), channel_id=1, source_target_pairs={{0,24},{4,28},{8,16},{12,20},{16,8},{20,12},{24,0},{28,4},{1,25},{... | collective-permute-start | bytes 98312 | tf_op jit(solution)/shard_map/ppermute | solution.py:177
  34.4 6.6 %collective-permute-start.13 = (bf16[128,128]{1,0:T(8,128)(2,1)S(1)}, bf16[128,128]{1,0:T(8,128)(2,1)S(1)}, u32[]{:S(2)}, u32[]{:S(2)}) collective-permute-start(bf16[128,128]{1,0:T(8,128)(2,1)S(1)} %get-tuple-element.19), channel_id=1, source_target_pairs={{0,28},{4,24},{8,20},{12,16},{16,12},{20,8},{24,4},{28,0},{1,29},{... | collective-permute-start | bytes 98312 | tf_op jit(solution)/shard_map/ppermute | solution.py:177
  42.6 3.8 %collective-permute-start.16 = (s16[144,128]{1,0:T(8,128)(2,1)S(1)}, s16[144,128]{1,0:T(8,128)(2,1)S(1)}, u32[]{:S(2)}, u32[]{:S(2)}) collective-permute-start(s16[144,128]{1,0:T(8,128)(2,1)S(1)} %product.1.refs_0_), channel_id=1, source_target_pairs={{0,3},{1,2},{2,1},{3,0},{4,7},{5,6},{6,5},{7,4},{8,11},{9,10},{10,... | collective-permute-start | bytes 110600 | tf_op jit(solution)/shard_map/ppermute | solution.py:177
  42.6 4.2 %collective-permute-start.15 = (s16[144,128]{1,0:T(8,128)(2,1)S(1)}, s16[144,128]{1,0:T(8,128)(2,1)S(1)}, u32[]{:S(2)}, u32[]{:S(2)}) collective-permute-start(s16[144,128]{1,0:T(8,128)(2,1)S(1)} %product.1.refs_0_), channel_id=1, source_target_pairs={{0,2},{1,3},{2,0},{3,1},{4,6},{5,7},{6,4},{7,5},{8,10},{9,11},{10,... | collective-permute-start | bytes 110600 | tf_op jit(solution)/shard_map/ppermute | solution.py:177
  44.2 2.6 %collective-permute-start.14 = (s16[144,128]{1,0:T(8,128)(2,1)S(1)}, s16[144,128]{1,0:T(8,128)(2,1)S(1)}, u32[]{:S(2)}, u32[]{:S(2)}) collective-permute-start(s16[144,128]{1,0:T(8,128)(2,1)S(1)} %product.1.refs_0_), channel_id=1, source_target_pairs={{0,1},{1,0},{2,3},{3,2},{4,5},{5,4},{6,7},{7,6},{8,9},{9,8},{10,11... | collective-permute-start | bytes 110600 | tf_op jit(solution)/shard_map/ppermute | solution.py:177

commit v3 on v2

--- a/solution.py
+++ b/solution.py
@@ -67,49 +67,43 @@
     return copies
 
 
-def transpose_product_kernel(
-    rows_hbm, cols_hbm, duals_hbm, tiles_hbm, out_ref, rows, cols, duals, tiles, picked, exponents, sems
-):
+def transpose_product_kernel(*refs):
+    (rows_hbm, cols_hbm, duals_hbm, tiles_hbm), others_hbm, refs = refs[:4], refs[4:11], refs[11:]
+    (out_ref, duals, tiles), others, refs = refs[:3], refs[3:10], refs[10:]
+    rows, cols, picked, exponents, small_sems, tile_sems, other_sems = refs
     k_tiles = tiles.shape[0]
     n_groups = k_tiles // GROUP
-    small = [
-        pltpu.make_async_copy(source, target, sems.at[n_groups + n])
-        for n, (source, target) in enumerate([(rows_hbm, rows), (duals_hbm, duals), (cols_hbm, cols)])
-    ]
-    large = [
-        pltpu.make_async_copy(
-            tiles_hbm.at[pl.ds(g * GROUP, GROUP)], tiles.at[pl.ds(g * GROUP, GROUP)], sems.at[g]
-        )
-        for g in range(n_groups)
-    ]
-    for copy in small + large:
-        copy.start()
+    groups = [pl.ds(g * GROUP, GROUP) for g in range(n_groups)]
+    small = started([rows_hbm, duals_hbm, cols_hbm], [rows, duals, cols], small_sems)
+    large = started([tiles_hbm.at[g] for g in groups], [tiles.at[g] for g in groups], tile_sems)
+    later = started(others_hbm, others, other_sems)
     for copy in small:
         copy.wait()
     for k in range(k_tiles):
         picked[pl.ds(k, 1), :] = duals[pl.ds(rows[k], 1), :]
-    for g, copy in enumerate(large):
-        here = pl.ds(g * GROUP, GROUP)
+    for here, copy in zip(groups, large):
         block = picked[here, :].astype(bf16).astype(f32)
         left = jnp.concatenate([one_row_of(block, m) for m in range(GROUP)], axis=1)
         copy.wait()
         terms = jnp.dot(left, tiles[here].reshape(GROUP * TILE, TILE), preferred_element_type=f32)
-        out_ref[here, :], exponents[here, :] = coded(terms)
-    out_ref[pl.ds(k_tiles, HEAD), :] = head_of(cols[...], exponents[...])
-
-
-def primal_kernel(n_row, *refs):
-    payloads, refs = refs[:n_row], refs[n_row:]
-    sources, (steps_ref, next_ref), refs = refs[:5], refs[5:7], refs[7:]
-    wanted, (extrap, *local_refs, sems) = refs[:n_row], refs[n_row:]
-    primal_ref, cost_ref, lower_ref, upper_ref, kind_ref = local_refs
-    copies = started(sources, local_refs, sems)
+        whole, exponents[here, :] = coded(terms)
+        for target in range(out_ref.shape[0]):
+            out_ref[target, here, :] = whole
+    head = head_of(cols[...], exponents[...])
+    for target in range(out_ref.shape[0]):
+        out_ref[target, pl.ds(k_tiles, HEAD), :] = head
+    for copy in later:
+        copy.wait()
+
+
+def primal_kernel(
+    payloads, primal_ref, cost_ref, lower_ref, upper_ref, kind_ref, steps_ref, next_ref, wanted, extrap
+):
+    n_row, k_tiles, _ = wanted.shape
     blocks = primal_ref.shape[0]
     padded = extrap.shape[0]
     first = lax.axis_index("row") * blocks
-    col_sums = block_sums(payloads, first, blocks)
-    for copy in copies:
-        copy.wait()
+    col_sums = block_sums([payloads.at[s] for s in range(n_row)], first, blocks)
     primal = primal_ref[...]
     kind = kind_ref[...]
     moved = primal - steps_ref[0] * (cost_ref[...] - col_sums)
@@ -121,20 +115,18 @@
         extrap[pl.ds(whole, padded - whole), :] = jnp.zeros((padded - whole, TILE), f32)
     extrap[pl.ds(0, blocks), :] = 2.0 * moved - primal
     right = extrap[...].astype(bf16)
-    for payload, target in zip(payloads, wanted):
-        k_tiles = target.shape[0]
-        head = payload[pl.ds(k_tiles, HEAD), :].astype(i32)
-        places = jnp.transpose(head.astype(f32))[:, 0:1].astype(i32) - first
+    for s in range(n_row):
+        head = payloads[s, pl.ds(k_tiles, HEAD), :].astype(f32)
+        places = jnp.transpose(head)[:, 0:1].astype(i32) - first
         mask = jnp.where(iota((k_tiles, padded), 1) == places, 1.0, 0.0)
-        target[...] = jnp.dot(mask.astype(bf16), right, preferred_element_type=f32).astype(bf16)
-
-
-def product_kernel(rows_ref, tiles_ref, *refs):
-    arrived, out_ref = refs[:-1], refs[-1]
+        wanted[s] = jnp.dot(mask.astype(bf16), right, preferred_element_type=f32).astype(bf16)
+
+
+def product_kernel(rows_ref, tiles_ref, arrived, out_ref):
     k_tiles = tiles_ref.shape[0]
-    block = arrived[0][...].astype(f32)
-    for ref in arrived[1:]:
-        block += ref[...].astype(f32)
+    block = arrived[0].astype(f32)
+    for s in range(1, arrived.shape[0]):
+        block += arrived[s].astype(f32)
     down = jnp.transpose(block)
     lane = iota((TILE, k_tiles), 1)
     right = jnp.concatenate(
@@ -152,13 +144,8 @@
 
 
 def dual_kernel(n_col, *refs):
-    payloads, sources, (steps_ref, next_ref) = refs[:n_col], refs[n_col : n_col + 3], refs[n_col + 3 : n_col + 5]
-    *local_refs, sems = refs[n_col + 5 :]
-    duals_ref, right_ref, kind_ref = local_refs
-    copies = started(sources, local_refs, sems)
+    payloads, (duals_ref, right_ref, kind_ref, steps_ref, next_ref) = refs[:n_col], refs[n_col:]
     row_sums = block_sums(payloads, 0, duals_ref.shape[0])
-    for copy in copies:
-        copy.wait()
     updated = duals_ref[...] + steps_ref[1] * (right_ref[...] - row_sums)
     next_ref[...] = jnp.where(kind_ref[...] == 1, jnp.maximum(updated, 0.0), updated)
 
@@ -201,71 +188,61 @@
     padded = -(-col_blocks // TILE) * TILE
     in_hbm = lambda array: pltpu.with_memory_space_constraint(array, pltpu.HBM)
     by_block = lambda array: in_hbm(array.reshape(-1, TILE))
-    blocks_of = lambda blocks, kind: pltpu.VMEM((blocks, TILE), kind)
-    payload = jax.ShapeDtypeStruct((k_tiles + HEAD, TILE), i16)
-    block = jax.ShapeDtypeStruct((k_tiles, TILE), bf16)
+    shape_of = lambda array: jax.ShapeDtypeStruct(array.shape, array.dtype)
     params = pltpu.CompilerParams(vmem_limit_bytes=32 * 1024 * 1024)
-
-    col_terms = pl.pallas_call(
+    primal_side = [by_block(a) for a in (primal, cost_vec, lower_bound, upper_bound, bound_kind)]
+    dual_side = [by_block(a) for a in (right_side, row_kind)]
+    own = [by_block(duals), in_hbm(tiles)]
+
+    col_terms, *kept = pl.pallas_call(
         transpose_product_kernel,
-        out_shape=payload,
-        in_specs=[HBM] * 4,
-        out_specs=VMEM,
+        out_shape=(
+            jax.ShapeDtypeStruct((n_row, k_tiles + HEAD, TILE), i16),
+            *[shape_of(a) for a in own + primal_side + dual_side],
+        ),
+        in_specs=[HBM] * 11,
+        out_specs=(VMEM,) * 10,
         scratch_shapes=[
             pltpu.SMEM((k_tiles,), i32),
             pltpu.VMEM((1, k_tiles), i32),
-            pltpu.VMEM((row_blocks, TILE), f32),
-            pltpu.VMEM((k_tiles, TILE, TILE), bf16),
             pltpu.VMEM((k_tiles, TILE), f32),
             pltpu.VMEM((k_tiles, TILE), f32),
-            pltpu.SemaphoreType.DMA((k_tiles // GROUP + 3,)),
+            pltpu.SemaphoreType.DMA((3,)),
+            pltpu.SemaphoreType.DMA((k_tiles // GROUP,)),
+            pltpu.SemaphoreType.DMA((7,)),
         ],
         compiler_params=params,
         name="transpose_product",
-    )(in_hbm(tile_row.reshape(-1)), in_hbm(tile_col.reshape(1, k_tiles)), by_block(duals), in_hbm(tiles))
-    primal_next, *wanted = pl.pallas_call(
-        lambda *refs: primal_kernel(n_row, *refs),
-        out_shape=(jax.ShapeDtypeStruct((col_blocks, TILE), f32), *[block] * n_row),
-        in_specs=[VMEM] * n_row + [HBM] * 5 + [SMEM],
-        out_specs=(VMEM,) * (n_row + 1),
-        scratch_shapes=[
-            blocks_of(padded, f32),
-            *[blocks_of(col_blocks, f32)] * 4,
-            blocks_of(col_blocks, i32),
-            pltpu.SemaphoreType.DMA((5,)),
-        ],
+    )(in_hbm(tile_row.reshape(-1)), in_hbm(tile_col.reshape(1, k_tiles)), *own, *primal_side, *dual_side)
+    duals_kept, tiles_kept = kept[:2]
+    primal_next, wanted = pl.pallas_call(
+        primal_kernel,
+        out_shape=(
+            jax.ShapeDtypeStruct((col_blocks, TILE), f32),
+            jax.ShapeDtypeStruct((n_row, k_tiles, TILE), bf16),
+        ),
+        in_specs=[VMEM] * 6 + [SMEM],
+        out_specs=(VMEM,) * 2,
+        scratch_shapes=[pltpu.VMEM((padded, TILE), f32)],
         compiler_params=params,
         name="primal_step",
-    )(
-        *exchange([col_terms] * n_row, "row"),
-        by_block(primal),
-        by_block(cost_vec),
-        by_block(lower_bound),
-        by_block(upper_bound),
-        by_block(bound_kind),
-        step_sizes,
-    )
+    )(lax.all_to_all(col_terms, "row", 0, 0), *kept[2:7], step_sizes)
     row_terms = pl.pallas_call(
         product_kernel,
-        out_shape=payload,
-        in_specs=[VMEM] * (n_row + 2),
+        out_shape=jax.ShapeDtypeStruct((k_tiles + HEAD, TILE), i16),
+        in_specs=[VMEM] * 3,
         out_specs=VMEM,
         compiler_params=params,
         name="product",
-    )(tile_row.reshape(1, k_tiles), tiles, *exchange(wanted, "row", back=True))
+    )(tile_row.reshape(1, k_tiles), tiles_kept, lax.all_to_all(wanted, "row", 0, 0))
     dual_next = pl.pallas_call(
         lambda *refs: dual_kernel(n_col, *refs),
         out_shape=jax.ShapeDtypeStruct((row_blocks, TILE), f32),
-        in_specs=[VMEM] * n_col + [HBM] * 3 + [SMEM],
+        in_specs=[VMEM] * (n_col + 3) + [SMEM],
         out_specs=VMEM,
-        scratch_shapes=[
-            *[blocks_of(row_blocks, f32)] * 2,
-            blocks_of(row_blocks, i32),
-            pltpu.SemaphoreType.DMA((3,)),
-        ],
         compiler_params=params,
         name="dual_step",
-    )(*exchange([row_terms] * n_col, "col"), by_block(duals), by_block(right_side), by_block(row_kind), step_sizes)
+    )(*exchange([row_terms] * n_col, "col"), duals_kept, *kept[7:], step_sizes)
     return (primal_next.reshape(-1), dual_next.reshape(-1))
 
 

time: 49.5 us -> 44 us (0.89)
  blocking collectives: 0 us -> 28.8 us
  starting transfers between devices: 25.7 us -> 1.9 us
  waiting for transfers between devices: 11.3 us -> 2.31 us
  Pallas kernels: 11.7 us -> 10.1 us
    all_to_all x0 -> x2, blocking collectives: none -> 28.8 us  [the longest x1 17.4 us: local(): lax.all_to_all(col_terms, 'row', 0, 0)]
    ppermute x17 -> x3, starting transfers between devices: 25.7 us -> 1.9 us  [exchange(): arrived.append(lax.ppermute(array, axis, pairs))]
    ppermute x17 -> x3, waiting for transfers between devices: 11.3 us -> 2.31 us  [exchange(): arrived.append(lax.ppermute(array, axis, pairs))]
    pallas_call x1, Pallas kernels: 2.55 us -> 1.56 us  [local(): pl.pallas_call(lambda *refs: dual_kernel(n_col, *refs), out_shape=jax.Sha...]
    pallas_call x3, Pallas kernels: 9.12 us -> 8.56 us  [the longest x1 5.02 us: local(): pl.pallas_call(transpose_product_kernel, out_shape=(jax.ShapeDtypeStruct(...]
  transfers between devices with their start and end apart: 17 -> 3, of which waited for: 10 -> 2; matrix products, arithmetic and copies ran while one was open for 0% -> 0% of each run, Pallas kernels for 0% -> 0%
where the time goes in v3:
time: 44 us; the launch traced here: 43.8 us
  blocking collectives  28.8 us (65%)
  Pallas kernels  10.1 us (23%)
  waiting for transfers between devices  2.31 us (5%)
  starting transfers between devices  1.9 us (4%)
  between operations  0.67 us (2%)
    all_to_all x1, blocking collectives, local(): lax.all_to_all(col_terms, 'row', 0, 0)  17.4 us
    all_to_all x1, blocking collectives, local(): lax.all_to_all(wanted, 'row', 0, 0)  11.4 us
    pallas_call x1, Pallas kernels, local(): pl.pallas_call(transpose_product_kernel, out_shape=(jax.ShapeDtypeStruct(...  5.02 us
    ppermute x3, waiting for transfers between devices, exchange(): arrived.append(lax.ppermute(array, axis, pairs))  2.31 us
    pallas_call x1, Pallas kernels, local(): pl.pallas_call(primal_kernel, out_shape=(jax.ShapeDtypeStruct((col_blocks...  1.99 us
    ppermute x3, starting transfers between devices, exchange(): arrived.append(lax.ppermute(array, axis, pairs))  1.9 us
    pallas_call x1, Pallas kernels, local(): pl.pallas_call(lambda *refs: dual_kernel(n_col, *refs), out_shape=jax.Sha...  1.56 us
    pallas_call x1, Pallas kernels, local(): pl.pallas_call(product_kernel, out_shape=jax.ShapeDtypeStruct((k_tiles +...  1.55 us
  transfers between devices with their start and end apart: 3, of which 2 were waited for; matrix products, arithmetic and copies ran while one was open for 0% of the time, Pallas kernels for 0%

profile of v3, /device:TPU:0, one launch (start us, length us, event | category | flops | bytes accessed | tf_op | source)
XLA Modules:
  0.0 43.8 jit_solution(5209309781243734472)
XLA Ops:
  0.6 0.0 copy-start
  0.6 0.0 copy-start.1
  0.7 5.0 %transpose_product.1 = (s16[8,144,128]{2,1,0:T(8,128)(2,1)S(1)}, f32[496,128]{1,0:T(8,128)S(1)}, bf16[128,128,128]{2,1,0:T(8,128)(2,1)S(1)}, f32[488,128]{1,0:T(...) custom-call(s32[128]{0:T(128)} %bitcast.14, ...), custom_call_target="tpu_custom_call" | custom-call | tf_op jit(solution)/shard_map/transpose_product/pallas_call | solution.py:197
  5.7 17.4 %all_to_all.10.payloads = s16[8,144,128]{2,1,0:T(8,128)(2,1)S(1)} all-to-all(s16[8,144,128]{2,1,0:T(8,128)(2,1)S(1)} %get-tuple-element.14), channel_id=1, replica_groups=mesh['row'=8,'col'=4] {'row'}, dimensions={0} | all-to-all | bytes 589824 | tf_op jit(solution)/shard_map/all_to_all | solution.py:229
  23.1 0.0 copy-done
  23.1 2.0 %primal_step.1 = (f32[488,128]{1,0:T(8,128)}, bf16[8,128,128]{2,1,0:T(8,128)(2,1)S(1)}) custom-call(s16[8,144,128]{2,1,0:T(8,128)(2,1)S(1)} %all_to_all.10.payloads, f32[488,128]{1,0:T(8,128)S(1)} %get-tuple-element.15.primal_ref, f32[488,128]{1,0:T(8,128)S(1)} %get-tuple-element.16.cost_ref, f32[488,128]{1,0:T(8,128)S(1)} %get-tuple-element.17.lower_ref, ...), custom_call_target="tpu_custom_call" | custom-call | tf_op jit(solution)/shard_map/primal_step/pallas_call | solution.py:218
  25.1 11.4 %all_to_all.11.arrived = bf16[8,128,128]{2,1,0:T(8,128)(2,1)S(1)} all-to-all(bf16[8,128,128]{2,1,0:T(8,128)(2,1)S(1)} %get-tuple-element.22), channel_id=1, replica_groups=mesh['row'=8,'col'=4] {'row'}, dimensions={0} | all-to-all | bytes 524288 | tf_op jit(solution)/shard_map/all_to_all | solution.py:237
  36.5 0.0 copy-done.1
  36.5 1.5 %product.1.refs_0_ = s16[144,128]{1,0:T(8,128)(2,1)S(1)} custom-call(s32[1,128]{1,0:T(1,128)S(1)} %bitcast.15, bf16[128,128,128]{2,1,0:T(8,128)(2,1)S(1)} %get-tuple-element.21.tiles_ref, bf16[8,128,128]{2,1,0:T(8,128)(2,1)S(1)} %all_to_all.11.arrived), custom_call_target="tpu_custom_call" | custom-call | tf_op jit(solution)/shard_map/product/pallas_call | solution.py:230
  38.0 0.1 collective-permute-start.2
  38.1 1.6 %collective-permute-start.1 = (s16[144,128]{1,0:T(8,128)(2,1)S(1)}, s16[144,128]{1,0:T(8,128)(2,1)S(1)}, u32[]{:S(2)}, u32[]{:S(2)}) collective-permute-start(s16[144,128]{1,0:T(8,128)(2,1)S(1)} %product.1.refs_0_), channel_id=1, source_target_pairs={{0,2},{1,3},{2,0},{3,1},{4,6},{5,7},{6,4},{7,5},{8,10},{9,11},{10,... | collective-permute-start | bytes 110600 | tf_op jit(solution)/shard_map/ppermute | solution.py:164
  39.7 0.3 collective-permute-start
  40.0 1.9 %collective-permute-done.2.refs_3_ = s16[144,128]{1,0:T(8,128)(2,1)S(1)} collective-permute-done((s16[144,128]{1,0:T(8,128)(2,1)S(1)}, s16[144,128]{1,0:T(8,128)(2,1)S(1)}, u32[]{:S(2)}, u32[]{:S(2)}) %collective-permute-start.2) | collective-permute-done | bytes 36896 | tf_op jit(solution)/shard_map/ppermute | solution.py:164
  41.8 0.4 %collective-permute-done.1.refs_2_ = s16[144,128]{1,0:T(8,128)(2,1)S(1)} collective-permute-done((s16[144,128]{1,0:T(8,128)(2,1)S(1)}, s16[144,128]{1,0:T(8,128)(2,1)S(1)}, u32[]{:S(2)}, u32[]{:S(2)}) %collective-permute-start.1) | collective-permute-done | bytes 36896 | tf_op jit(solution)/shard_map/ppermute | solution.py:164
  42.3 0.0 collective-permute-done.refs_1_
  42.3 1.6 %dual_step.1 = f32[496,128]{1,0:T(8,128)} custom-call(s16[144,128]{1,0:T(8,128)(2,1)S(1)} %product.1.refs_0_, s16[144,128]{1,0:T(8,128)(2,1)S(1)} %collective-permute-done.refs_1_, s16[144,128]{1,0:T(8,128)(2,1)S(1)} %collective-permute-done.1.refs_2_, s16[144,128]{1,0:T(8,128)(2,1)S(1)} %collective-permute-done.2.refs_3_, ...), custom_call_target="tpu_custom_call" | custom-call | tf_op jit(solution)/shard_map/dual_step/pallas_call | solution.py:238
Async XLA Ops:
  0.6 22.5 %copy-start = (f32[2]{0:T(128)S(1)}, f32[2]{0:T(128)}, u32[]{:S(2)}) copy-start(f32[2]{0:T(128)} %refs_7_.1) | copy-start | bytes 28
  0.6 35.9 %copy-start.1 = (s32[1,1,128]{2,1,0:T(1,128)S(1)}, s32[1,1,128]{2,1,0:T(1,128)}, u32[]{:S(2)}) copy-start(s32[1,1,128]{2,1,0:T(1,128)} %param.13) | copy-start | bytes 1540
  38.0 3.8 %collective-permute-start.2 = (s16[144,128]{1,0:T(8,128)(2,1)S(1)}, s16[144,128]{1,0:T(8,128)(2,1)S(1)}, u32[]{:S(2)}, u32[]{:S(2)}) collective-permute-start(s16[144,128]{1,0:T(8,128)(2,1)S(1)} %product.1.refs_0_), channel_id=1, source_target_pairs={{0,3},{1,2},{2,1},{3,0},{4,7},{5,6},{6,5},{7,4},{8,11},{9,10},{10,... | collective-permute-start | bytes 110600 | tf_op jit(solution)/shard_map/ppermute | solution.py:164
  38.1 4.2 %collective-permute-start.1 = (s16[144,128]{1,0:T(8,128)(2,1)S(1)}, s16[144,128]{1,0:T(8,128)(2,1)S(1)}, u32[]{:S(2)}, u32[]{:S(2)}) collective-permute-start(s16[144,128]{1,0:T(8,128)(2,1)S(1)} %product.1.refs_0_), channel_id=1, source_target_pairs={{0,2},{1,3},{2,0},{3,1},{4,6},{5,7},{6,4},{7,5},{8,10},{9,11},{10,... | collective-permute-start | bytes 110600 | tf_op jit(solution)/shard_map/ppermute | solution.py:164
  39.7 2.6 %collective-permute-start = (s16[144,128]{1,0:T(8,128)(2,1)S(1)}, s16[144,128]{1,0:T(8,128)(2,1)S(1)}, u32[]{:S(2)}, u32[]{:S(2)}) collective-permute-start(s16[144,128]{1,0:T(8,128)(2,1)S(1)} %product.1.refs_0_), channel_id=1, source_target_pairs={{0,1},{1,0},{2,3},{3,2},{4,5},{5,4},{6,7},{7,6},{8,9},{9,8},{10,11... | collective-permute-start | bytes 110600 | tf_op jit(solution)/shard_map/ppermute | solution.py:164

commit v4 on v3

v4 whole, which is shorter than its diff:
```python
import functools
import jax
import jax.numpy as jnp
from jax import lax
from jax.experimental import pallas as pl
from jax.experimental.pallas import tpu as pltpu
from jax.sharding import PartitionSpec as P

TILE = 128
GROUP = 16
SLOTS = 48
HEAD = 16
BITS = 14

f32 = jnp.float32
bf16 = jnp.bfloat16
i32 = jnp.int32
i16 = jnp.int16
VMEM = pl.BlockSpec(memory_space=pltpu.VMEM)
SMEM = pl.BlockSpec(memory_space=pltpu.SMEM)
HBM = pl.BlockSpec(memory_space=pltpu.HBM)


def iota(shape, axis):
    return lax.broadcasted_iota(i32, shape, axis)


def where_one(condition):
    return jnp.where(condition, 1.0, 0.0)


def one_row_of(block, position):
    return jnp.where(iota(block.shape, 0) == position, block, 0.0).astype(bf16)


def rounds_of(n_row):
    chunks = n_row * SLOTS // TILE
    return chunks, -(-(2 * chunks + 1) // 8) * 8


def coded(values):
    largest = jnp.maximum(jnp.max(jnp.abs(values), axis=1, keepdims=True), 1e-30)
    exponent = jnp.ceil(jnp.log2(largest))
    whole = jnp.floor(values * jnp.exp2(BITS - exponent) + 0.5).astype(i32)
    return whole, jnp.broadcast_to(exponent, values.shape)


def two_parts(whole):
    low = jnp.bitwise_and(whole, 255)
    parts = [(whole - low).astype(f32), low.astype(f32)]
    return jnp.concatenate(parts, axis=1).astype(bf16)


def picked_sums(masks, wholes):
    left = masks[0] if len(masks) == 1 else jnp.concatenate(masks, axis=1)
    both = jnp.dot(
        left.astype(bf16),
        jnp.concatenate([two_parts(w) for w in wholes], axis=0),
        preferred_element_type=f32,
    )
    return both[:, :TILE] + both[:, TILE:]


def scaled_mask(down, places, exponents):
    return jnp.where(down == places, jnp.exp2(exponents.astype(f32) - BITS), 0.0)


def started(sources, targets, sems):
    copies = [
        pltpu.make_async_copy(source, target, sems.at[n])
        for n, (source, target) in enumerate(zip(sources, targets))
    ]
    for copy in copies:
        copy.start()
    return copies


def transpose_product_kernel(owned, *refs):
    (rows_hbm, cols_hbm, duals_hbm, tiles_hbm), others_hbm, refs = refs[:4], refs[4:9], refs[9:]
    (out_ref, slot_ref, duals, tiles), others, refs = refs[:4], refs[4:9], refs[9:]
    rows, cols, picked, exponents, parts, small_sems, tile_sems, other_sems = refs
    n_row = out_ref.shape[0]
    chunks, head_rows = rounds_of(n_row)
    most = SLOTS - head_rows
    k_tiles = tiles.shape[0]
    n_groups = k_tiles // GROUP
    groups = [pl.ds(g * GROUP, GROUP) for g in range(n_groups)]
    small = started([cols_hbm, rows_hbm, duals_hbm], [cols, rows, duals], small_sems)
    large = started([tiles_hbm.at[g] for g in groups], [tiles.at[g] for g in groups], tile_sems)
    later = started(others_hbm, others, other_sems)

    small[0].wait()
    square = (k_tiles, k_tiles)
    col_across = cols[...]
    col_down = jnp.transpose(jnp.broadcast_to(col_across.astype(f32), square)).astype(i32)
    owner_across = sum((col_across >= o * owned).astype(i32) for o in range(1, n_row))
    owner_down = sum((col_down >= o * owned).astype(i32) for o in range(1, n_row))
    same = owner_down == owner_across
    earlier_down = iota(square, 0) < iota(square, 1)
    earlier_across = iota(square, 1) < iota(square, 0)
    rank_across = jnp.sum(where_one(same & earlier_down), axis=0, keepdims=True).astype(i32)
    rank_down = jnp.sum(where_one(same & earlier_across), axis=1, keepdims=True).astype(i32)
    slot_across = jnp.where(rank_across < most, owner_across * SLOTS + head_rows + rank_across, -1)
    slot_down = jnp.where(rank_down < most, owner_down * SLOTS + head_rows + rank_down, -1)
    slot_ref[...] = slot_down
    too_many = where_one(jnp.max(rank_across, axis=1, keepdims=True) >= most)
    to_slots = where_one(iota((n_row * SLOTS, k_tiles), 0) == slot_across)
    here = jnp.where(rank_down < most, lax.axis_index("row") * SLOTS + head_rows + rank_down, -1)
    to_lanes = where_one(iota((k_tiles, n_row * SLOTS), 1) == here)
    of_owner = where_one(iota((n_row, k_tiles), 0) == owner_across)
    place = col_across - owner_across * owned + 1
    place_low = jnp.bitwise_and(place, 255)
    head_left = jnp.concatenate(
        [of_owner * (place - place_low).astype(f32), of_owner * place_low.astype(f32), of_owner], axis=0
    ).astype(bf16)

    for copy in small[1:]:
        copy.wait()
    for k in range(k_tiles):
        picked[pl.ds(k, 1), :] = duals[pl.ds(rows[k], 1), :]
    for group, copy in zip(groups, large):
        block = picked[group, :].astype(bf16).astype(f32)
        left = jnp.concatenate([one_row_of(block, m) for m in range(GROUP)], axis=1)
        copy.wait()
        terms = jnp.dot(left, tiles[group].reshape(GROUP * TILE, TILE), preferred_element_type=f32)
        whole, exponents[group, :] = coded(terms)
        parts[group, :] = two_parts(whole)

    scaled = [to_lanes, to_lanes * jnp.concatenate([exponents[...]] * chunks, axis=1)]
    heads = jnp.dot(head_left, jnp.concatenate(scaled, axis=1).astype(bf16), preferred_element_type=f32)
    width = n_row * SLOTS
    places = heads[:n_row, :width] + heads[n_row : 2 * n_row, :width]
    scales = heads[2 * n_row :, width:]
    both = jnp.dot(to_slots.astype(bf16), parts[...], preferred_element_type=f32)
    body = both[:, :TILE] + both[:, TILE:]
    line = iota((head_rows, TILE), 0)
    for o in range(n_row):
        head = jnp.where(line == 2 * chunks, too_many, 0.0)
        for c in range(chunks):
            lanes = slice(c * TILE, (c + 1) * TILE)
            head = jnp.where(line == c, places[o : o + 1, lanes], head)
            head = jnp.where(line == chunks + c, scales[o : o + 1, lanes], head)
        rows_of = body[o * SLOTS + head_rows : (o + 1) * SLOTS]
        out_ref[o] = jnp.concatenate([head, rows_of], axis=0).astype(i32).astype(i16)
    for copy in later:
        copy.wait()


def primal_kernel(
    payloads, primal_ref, cost_ref, lower_ref, upper_ref, kind_ref, steps_ref, next_ref, wanted, flag_ref, extrap
):
    n_row = payloads.shape[0]
    chunks, head_rows = rounds_of(n_row)
    blocks = primal_ref.shape[0]
    padded = extrap.shape[0]
    head = jnp.zeros((head_rows, TILE), f32)
    for s in range(n_row):
        head += payloads[s].astype(i32)[:head_rows].astype(f32)
    flag_ref[...] = jnp.broadcast_to(head[2 * chunks : 2 * chunks + 1], flag_ref.shape)
    whole = payloads[...].reshape(n_row * SLOTS, TILE).astype(i32)
    down = iota((blocks, TILE), 0) + 1
    head_whole = head.astype(i32)
    masks, wholes = [], []
    for c in range(chunks):
        masks.append(scaled_mask(down, head_whole[c : c + 1], head_whole[chunks + c : chunks + c + 1]))
        wholes.append(whole[c * TILE : (c + 1) * TILE])
    col_sums = picked_sums(masks, wholes)
    primal = primal_ref[...]
    kind = kind_ref[...]
    moved = primal - steps_ref[0] * (cost_ref[...] - col_sums)
    moved = jnp.where(kind % 2 == 1, jnp.maximum(moved, lower_ref[...]), moved)
    moved = jnp.where(kind >= 2, jnp.minimum(moved, upper_ref[...]), moved)
    next_ref[...] = moved
    aligned = blocks // 8 * 8
    if padded > aligned:
        extrap[pl.ds(aligned, padded - aligned), :] = jnp.zeros((padded - aligned, TILE), f32)
    extrap[pl.ds(0, blocks), :] = 2.0 * moved - primal
    right = extrap[...].astype(bf16)
    across = iota((TILE, padded), 1) + 1
    places = jnp.transpose(head).astype(i32)
    sent = [
        jnp.dot(where_one(across == places[:, c : c + 1]).astype(bf16), right, preferred_element_type=f32)
        for c in range(chunks)
    ]
    wanted[...] = jnp.concatenate(sent, axis=0).astype(bf16).reshape(wanted.shape)


def product_kernel(*refs):
    (rows_ref, slot_ref, tiles_ref, arrived, flag_ref), others_hbm, refs = refs[:5], refs[5:7], refs[7:]
    out_ref, others, sems = refs[0], refs[1:3], refs[3]
    later = started(others_hbm, others, sems)
    k_tiles = tiles_ref.shape[0]
    received = arrived[...].reshape(-1, TILE)
    across = iota((k_tiles, received.shape[0]), 1)
    slots = jnp.concatenate([slot_ref[...]] * (received.shape[0] // TILE), axis=1)
    block = jnp.dot(where_one(across == slots).astype(bf16), received, preferred_element_type=f32)
    down = jnp.transpose(block)
    lane = iota((TILE, k_tiles), 1)
    right = jnp.concatenate(
        [jnp.where(lane % 2 == 0, down, 0.0), jnp.where(lane % 2 == 1, down, 0.0)], axis=0
    ).astype(bf16)
    terms = jnp.zeros((TILE, k_tiles), f32)
    for g in range(k_tiles // 8):
        even = jnp.concatenate([tiles_ref[8 * g + m] for m in (0, 2, 4, 6)], axis=0)
        odd = jnp.concatenate([tiles_ref[8 * g + m] for m in (1, 3, 5, 7)], axis=0)
        products = jnp.dot(jnp.concatenate([even, odd], axis=1), right, preferred_element_type=f32)
        for p in range(4):
            terms = jnp.where(lane // 2 == 4 * g + p, products[p * TILE : (p + 1) * TILE], terms)
    whole, exponents = coded(jnp.transpose(terms))
    out_ref[pl.ds(0, k_tiles), :] = whole.astype(i16)
    line = iota((HEAD, TILE), 0)
    head = jnp.where(line == 0, rows_ref[...], jnp.transpose(exponents)[0:HEAD, :].astype(i32))
    head = jnp.where(line == 2, flag_ref[0:1, :].astype(i32), head)
    out_ref[pl.ds(k_tiles, HEAD), :] = head.astype(i16)
    for copy in later:
        copy.wait()


def dual_kernel(n_col, *refs):
    payloads, (duals_ref, right_ref, kind_ref, steps_ref, next_ref, flag_ref) = refs[:n_col], refs[n_col:]
    k_tiles = payloads[0].shape[0] - HEAD
    down = iota((duals_ref.shape[0], k_tiles), 0)
    masks, wholes = [], []
    flags = jnp.zeros((1, TILE), i32)
    for payload in payloads:
        head = payload[pl.ds(k_tiles, HEAD), :].astype(i32)
        masks.append(scaled_mask(down, head[0:1], head[1:2]))
        wholes.append(payload[pl.ds(0, k_tiles), :].astype(i32))
        flags += head[2:3]
    row_sums = picked_sums(masks, wholes)
    updated = duals_ref[...] + steps_ref[1] * (right_ref[...] - row_sums)
    next_ref[...] = jnp.where(kind_ref[...] == 1, jnp.maximum(updated, 0.0), updated)
    flag_ref[0] = jnp.max(flags)


def partners(axis):
    size = lax.axis_size(axis)
    if size & (size - 1) == 0:
        there = [[(i, i ^ n) for i in range(size)] for n in range(1, size)]
    else:
        there = [[(i, (i + n) % size) for i in range(size)] for n in range(1, size)]
    return [(pairs, [(j, i) for i, j in pairs]) for pairs in there]


def gathered_along(array, axis):
    return [array] + [lax.ppermute(array, axis, there) for there, _ in partners(axis)]


def sums_at(places, terms, blocks):
    mask = (jnp.arange(blocks)[:, None] == jnp.concatenate(places)[None, :]).astype(f32)
    return jnp.dot(mask, jnp.concatenate(terms), precision=lax.Precision.HIGHEST).reshape(-1)


def full_step(
    tiles, rows, cols, primal, duals, cost_vec, lower_bound, upper_bound, bound_kind, right_side, row_kind, steps
):
    col_blocks = primal.shape[0] // TILE
    row_blocks = duals.shape[0] // TILE
    wide = tiles.astype(f32)
    dual_blocks = duals.astype(bf16).astype(f32).reshape(row_blocks, TILE)[rows]
    col_terms = jnp.einsum("kij,ki->kj", wide, dual_blocks)
    first = lax.axis_index("row") * col_blocks
    places = [there - first for there in gathered_along(cols, "row")]
    places = [jnp.where((p >= 0) & (p < col_blocks), p, col_blocks) for p in places]
    col_sums = sums_at(places, gathered_along(col_terms, "row"), col_blocks)
    moved = primal - steps[0] * (cost_vec - col_sums)
    moved = jnp.where(bound_kind % 2 == 1, jnp.maximum(moved, lower_bound), moved)
    moved = jnp.where(bound_kind >= 2, jnp.minimum(moved, upper_bound), moved)
    extrap = (2.0 * moved - primal).astype(bf16).reshape(col_blocks, TILE)
    wanted = [
        jnp.where((p < col_blocks)[:, None], extrap[jnp.minimum(p, col_blocks - 1)], jnp.zeros((), bf16))
        for p in places
    ]
    blocks = wanted[0].astype(f32)
    for block, (_, back) in zip(wanted[1:], partners("row")):
        blocks += lax.ppermute(block, "row", back).astype(f32)
    row_terms = jnp.einsum("kij,kj->ki", wide, blocks)
    row_sums = sums_at(gathered_along(rows, "col"), gathered_along(row_terms, "col"), row_blocks)
    updated = duals + steps[1] * (right_side - row_sums)
    return moved, jnp.where(row_kind == 1, jnp.maximum(updated, 0.0), updated)


def local(
    block_tiles,
    tile_row,
    tile_col,
    primal,
    duals,
    cost_vec,
    lower_bound,
    upper_bound,
    bound_kind,
    right_side,
    row_kind,
    step_sizes,
):
    k_tiles = block_tiles.shape[2]
    tiles = block_tiles.reshape(k_tiles, TILE, TILE)
    rows = tile_row.reshape(-1)
    cols = tile_col.reshape(-1)
    n_row = lax.axis_size("row")
    n_col = lax.axis_size("col")
    col_blocks = primal.shape[0] // TILE
    row_blocks = duals.shape[0] // TILE
    padded = -(-col_blocks // TILE) * TILE
    in_hbm = lambda array: pltpu.with_memory_space_constraint(array, pltpu.HBM)
    by_block = lambda array: in_hbm(array.reshape(-1, TILE))
    shape_of = lambda array: jax.ShapeDtypeStruct(array.shape, array.dtype)
    params = pltpu.CompilerParams(vmem_limit_bytes=32 * 1024 * 1024)
    primal_side = [by_block(a) for a in (primal, cost_vec, lower_bound, upper_bound, bound_kind)]
    dual_side = [by_block(a) for a in (right_side, row_kind)]
    own = [by_block(duals), in_hbm(tiles)]

    col_terms, slots, duals_kept, tiles_kept, *primal_kept = pl.pallas_call(
        functools.partial(transpose_product_kernel, col_blocks),
        out_shape=(
            jax.ShapeDtypeStruct((n_row, SLOTS, TILE), i16),
            jax.ShapeDtypeStruct((k_tiles, TILE), i32),
            *[shape_of(a) for a in own + primal_side],
        ),
        in_specs=[HBM] * 9,
        out_specs=(VMEM,) * 9,
        scratch_shapes=[
            pltpu.SMEM((k_tiles,), i32),
            pltpu.VMEM((1, k_tiles), i32),
            pltpu.VMEM((k_tiles, TILE), f32),
            pltpu.VMEM((k_tiles, TILE), f32),
            pltpu.VMEM((k_tiles, 2 * TILE), bf16),
            pltpu.SemaphoreType.DMA((3,)),
            pltpu.SemaphoreType.DMA((k_tiles // GROUP,)),
            pltpu.SemaphoreType.DMA((5,)),
        ],
        compiler_params=params,
        name="transpose_product",
    )(in_hbm(rows), in_hbm(cols.reshape(1, k_tiles)), *own, *primal_side)
    primal_next, wanted, flag = pl.pallas_call(
        primal_kernel,
        out_shape=(
            jax.ShapeDtypeStruct((col_blocks, TILE), f32),
            jax.ShapeDtypeStruct((n_row, SLOTS, TILE), bf16),
            jax.ShapeDtypeStruct((8, TILE), f32),
        ),
        in_specs=[VMEM] * 6 + [SMEM],
        out_specs=(VMEM,) * 3,
        scratch_shapes=[pltpu.VMEM((padded, TILE), f32)],
        compiler_params=params,
        name="primal_step",
    )(lax.all_to_all(col_terms, "row", 0, 0), *primal_kept, step_sizes)
    row_terms, *dual_kept = pl.pallas_call(
        product_kernel,
        out_shape=(
            jax.ShapeDtypeStruct((k_tiles + HEAD, TILE), i16),
            *[shape_of(a) for a in dual_side],
        ),
        in_specs=[VMEM] * 5 + [HBM] * 2,
        out_specs=(VMEM,) * 3,
        scratch_shapes=[pltpu.SemaphoreType.DMA((2,))],
        compiler_params=params,
        name="product",
    )(rows.reshape(1, k_tiles), slots, tiles_kept, lax.all_to_all(wanted, "row", 0, 0), flag, *dual_side)
    dual_next, too_many = pl.pallas_call(
        functools.partial(dual_kernel, n_col),
        out_shape=(jax.ShapeDtypeStruct((row_blocks, TILE), f32), jax.ShapeDtypeStruct((1,), i32)),
        in_specs=[VMEM] * (n_col + 3) + [SMEM],
        out_specs=(VMEM, SMEM),
        compiler_params=params,
        name="dual_step",
    )(*gathered_along(row_terms, "col"), duals_kept, *dual_kept, step_sizes)
    vectors = (primal, duals, cost_vec, lower_bound, upper_bound, bound_kind, right_side, row_kind, step_sizes)
    return lax.cond(
        too_many[0] > 0,
        lambda done: full_step(tiles, rows, cols, *vectors),
        lambda done: done,
        (primal_next.reshape(-1), dual_next.reshape(-1)),
    )


def solution(mesh):
    return jax.shard_map(
        local,
        mesh=mesh,
        in_specs=(
            P("row", "col", None, None, None),
            P("row", "col", None),
            P("row", "col", None),
            P(("col", "row")),
            P("row"),
            P(("col", "row")),
            P(("col", "row")),
            P(("col", "row")),
            P(("col", "row")),
            P("row"),
            P("row"),
            P(),
        ),
        out_specs=(P(("col", "row")), P("row")),
        check_vma=False,
    )
```

time: 44 us -> 40 us (0.909)
  blocking collectives: 28.8 us -> 23.8 us
  between operations: 0.67 us -> 1.46 us
    all_to_all x1, blocking collectives: 17.4 us -> 14.3 us  [local(): lax.all_to_all(col_terms, 'row', 0, 0)]
    all_to_all x1, blocking collectives: 11.4 us -> 9.5 us  [local(): lax.all_to_all(wanted, 'row', 0, 0)]
where the time goes in v4:
time: 40 us; the launch traced here: 39.8 us
  blocking collectives  23.8 us (60%)
  Pallas kernels  10.2 us (25%)
  waiting for transfers between devices  2.31 us (6%)
  starting transfers between devices  1.92 us (5%)
  between operations  1.46 us (4%)
    all_to_all x1, blocking collectives, local(): lax.all_to_all(col_terms, 'row', 0, 0)  14.3 us
    all_to_all x1, blocking collectives, local(): lax.all_to_all(wanted, 'row', 0, 0)  9.5 us
    pallas_call x1, Pallas kernels, local(): pl.pallas_call(functools.partial(transpose_product_kernel, col_blocks), o...  5.17 us
    ppermute x3, waiting for transfers between devices, gathered_along(): lax.ppermute(array, axis, there)  2.31 us
    ppermute x3, starting transfers between devices, gathered_along(): lax.ppermute(array, axis, there)  1.92 us
    pallas_call x1, Pallas kernels, local(): pl.pallas_call(primal_kernel, out_shape=(jax.ShapeDtypeStruct((col_blocks...  1.72 us
    pallas_call x1, Pallas kernels, local(): pl.pallas_call(product_kernel, out_shape=(jax.ShapeDtypeStruct((k_tiles +...  1.71 us
    pallas_call x1, Pallas kernels, local(): pl.pallas_call(functools.partial(dual_kernel, n_col), out_shape=(jax.Shap...  1.58 us
  transfers between devices with their start and end apart: 3, of which 2 were waited for; matrix products, arithmetic and copies ran while one was open for 0% of the time, Pallas kernels for 0%

profile of v4, /device:TPU:0, one launch (start us, length us, event | category | flops | bytes accessed | tf_op | source)
XLA Modules:
  0.0 39.8 jit_solution(10455968495514433565)
XLA Ops:
  0.6 0.0 copy-start.10
  0.6 0.0 copy-start.9
  0.6 5.2 %transpose_product.1 = (s16[8,48,128]{2,1,0:T(8,128)(2,1)S(1)}, s32[128,128]{1,0:T(8,128)S(1)}, f32[496,128]{1,0:T(8,128)S(1)}, bf16[128,128,128]{2,1,0:T(8,128)...) custom-call(s32[128]{0:T(128)} %bitcast.90, ...), custom_call_target="tpu_custom_call" | custom-call | tf_op jit(solution)/shard_map/transpose_product/pallas_call | solution.py:314
  5.8 0.0 copy-start
  5.8 0.0 copy-start.1
  5.9 0.0 copy-start.2
  5.9 0.0 copy-start.3
  5.9 0.0 copy-start.4
  5.9 0.0 copy-start.5
  5.9 0.0 copy-start.6
  5.9 0.0 copy-start.7
  5.9 0.0 copy-start.11
  5.9 14.3 %all_to_all.10.payloads = s16[8,48,128]{2,1,0:T(8,128)(2,1)S(1)} all-to-all(s16[8,48,128]{2,1,0:T(8,128)(2,1)S(1)} %get-tuple-element.68), channel_id=1, replica_groups=mesh['row'=8,'col'=4] {'row'}, dimensions={0} | all-to-all | bytes 196608 | tf_op jit(solution)/shard_map/all_to_all | solution.py:348
  20.3 0.0 copy-done.9
  20.3 1.7 %primal_step.1 = (f32[488,128]{1,0:T(8,128)}, bf16[8,48,128]{2,1,0:T(8,128)(2,1)S(1)}, f32[8,128]{1,0:T(8,128)S(1)}) custom-call(s16[8,48,128]{2,1,0:T(8,128)(2,1)S(1)} %all_to_all.10.payloads, f32[488,128]{1,0:T(8,128)S(1)} %get-tuple-element.69.primal_ref, f32[488,128]{1,0:T(8,128)S(1)} %get-tuple-element.70.cost_ref, ...), custom_call_target="tpu_custom_call" | custom-call | tf_op jit(solution)/shard_map/primal_step/pallas_call | solution.py:336
  22.0 9.5 %all_to_all.11.refs_3_ = bf16[8,48,128]{2,1,0:T(8,128)(2,1)S(1)} all-to-all(bf16[8,48,128]{2,1,0:T(8,128)(2,1)S(1)} %get-tuple-element.74), channel_id=1, replica_groups=mesh['row'=8,'col'=4] {'row'}, dimensions={0} | all-to-all | bytes 196608 | tf_op jit(solution)/shard_map/all_to_all | solution.py:360
  31.5 0.0 copy-done.10
  31.5 1.7 %product.1 = (s16[144,128]{1,0:T(8,128)(2,1)S(1)}, f32[496,128]{1,0:T(8,128)S(1)}, s32[496,128]{1,0:T(8,128)S(1)}) custom-call(s32[1,128]{1,0:T(1,128)S(1)} %bitcast.91, s32[128,128]{1,0:T(8,128)S(1)} %get-tuple-element.66.refs_1_, bf16[128,128,128]{2,1,0:T(8,128)(2,1)S(1)} %get-tuple-element.67.refs_2_, bf16[8,48,128]{2,1,0:T(8,128)(2,1)S(1)} %all_to_all.11.refs_3_, ...), custom_call_target="tpu_custom_call" | custom-call | tf_op jit(solution)/shard_map/product/pallas_call | solution.py:349
  33.2 0.1 collective-permute-start.29
  33.3 1.6 %collective-permute-start.28 = (s16[144,128]{1,0:T(8,128)(2,1)S(1)}, s16[144,128]{1,0:T(8,128)(2,1)S(1)}, u32[]{:S(2)}, u32[]{:S(2)}) collective-permute-start(s16[144,128]{1,0:T(8,128)(2,1)S(1)} %get-tuple-element.76.refs_0_), channel_id=1, source_target_pairs={{0,2},{1,3},{2,0},{3,1},{4,6},{5,7},{6,4},{7,5},{8,10},{9,11},{10,... | collective-permute-start | bytes 110600 | tf_op jit(solution)/shard_map/ppermute | solution.py:246
  34.9 0.3 collective-permute-start.27
  35.1 1.9 %collective-permute-done.29.refs_3_ = s16[144,128]{1,0:T(8,128)(2,1)S(1)} collective-permute-done((s16[144,128]{1,0:T(8,128)(2,1)S(1)}, s16[144,128]{1,0:T(8,128)(2,1)S(1)}, u32[]{:S(2)}, u32[]{:S(2)}) %collective-permute-start.29) | collective-permute-done | bytes 36896 | tf_op jit(solution)/shard_map/ppermute | solution.py:246
  37.0 0.4 %collective-permute-done.28.refs_2_ = s16[144,128]{1,0:T(8,128)(2,1)S(1)} collective-permute-done((s16[144,128]{1,0:T(8,128)(2,1)S(1)}, s16[144,128]{1,0:T(8,128)(2,1)S(1)}, u32[]{:S(2)}, u32[]{:S(2)}) %collective-permute-start.28) | collective-permute-done | bytes 36896 | tf_op jit(solution)/shard_map/ppermute | solution.py:246
  37.5 0.0 collective-permute-done.27.refs_1_
  37.5 1.6 %dual_step.1 = (f32[496,128]{1,0:T(8,128)}, s32[1]{0:T(128)}) custom-call(s16[144,128]{1,0:T(8,128)(2,1)S(1)} %get-tuple-element.76.refs_0_, s16[144,128]{1,0:T(8,128)(2,1)S(1)} %collective-permute-done.27.refs_1_, s16[144,128]{1,0:T(8,128)(2,1)S(1)} %collective-permute-done.28.refs_2_, s16[144,128]{1,0:T(8,128)(2,1)S(1)} %collective-permute-done.29.refs_3_, ...), custom_call_target="tpu_custom_call" | custom-call | tf_op jit(solution)/shard_map/dual_step/pallas_call | solution.py:361
  39.7 0.0 copy-done
  39.7 0.0 copy-done.1
  39.7 0.0 copy-done.2
  39.7 0.0 copy-done.3
  39.7 0.0 copy-done.4
  39.7 0.0 copy-done.5
  39.7 0.0 copy-done.6
  39.7 0.0 copy-done.7
  39.8 0.0 copy-done.11
  (1 shorter events, 0.0 us)
Async XLA Ops:
  0.6 30.9 %copy-start.10 = (s32[1,1,128]{2,1,0:T(1,128)S(1)}, s32[1,1,128]{2,1,0:T(1,128)}, u32[]{:S(2)}) copy-start(s32[1,1,128]{2,1,0:T(1,128)} %param.15) | copy-start | bytes 1540
  0.6 19.6 %copy-start.9 = (f32[2]{0:T(128)S(1)}, f32[2]{0:T(128)}, u32[]{:S(2)}) copy-start(f32[2]{0:T(128)} %refs_7_.1) | copy-start | bytes 28
  5.8 33.8 %copy-start = (f32[63488]{0:T(1024)S(1)}, f32[63488]{0:T(1024)}, u32[]{:S(2)}) copy-start(f32[63488]{0:T(1024)} %param.18) | copy-start | bytes 761860
  5.8 33.8 %copy-start.1 = (f32[63488]{0:T(1024)S(1)}, f32[63488]{0:T(1024)}, u32[]{:S(2)}) copy-start(f32[63488]{0:T(1024)} %param.23) | copy-start | bytes 761860
  5.9 33.8 %copy-start.2 = (s32[63488]{0:T(1024)S(1)}, s32[63488]{0:T(1024)}, u32[]{:S(2)}) copy-start(s32[63488]{0:T(1024)} %param.24) | copy-start | bytes 761860
  5.9 33.8 %copy-start.3 = (f32[62464]{0:T(1024)S(1)}, f32[62464]{0:T(1024)}, u32[]{:S(2)}) copy-start(f32[62464]{0:T(1024)} %param.17) | copy-start | bytes 749572
  5.9 33.8 %copy-start.4 = (f32[62464]{0:T(1024)S(1)}, f32[62464]{0:T(1024)}, u32[]{:S(2)}) copy-start(f32[62464]{0:T(1024)} %param.19) | copy-start | bytes 749572
  5.9 33.8 %copy-start.5 = (f32[62464]{0:T(1024)S(1)}, f32[62464]{0:T(1024)}, u32[]{:S(2)}) copy-start(f32[62464]{0:T(1024)} %param.20) | copy-start | bytes 749572
  5.9 33.8 %copy-start.6 = (f32[62464]{0:T(1024)S(1)}, f32[62464]{0:T(1024)}, u32[]{:S(2)}) copy-start(f32[62464]{0:T(1024)} %param.21) | copy-start | bytes 749572
  5.9 33.8 %copy-start.7 = (s32[62464]{0:T(1024)S(1)}, s32[62464]{0:T(1024)}, u32[]{:S(2)}) copy-start(s32[62464]{0:T(1024)} %param.22) | copy-start | bytes 749572
  5.9 33.8 %copy-start.11 = (s32[1,1,128]{2,1,0:T(1,128)S(1)}, s32[1,1,128]{2,1,0:T(1,128)}, u32[]{:S(2)}) copy-start(s32[1,1,128]{2,1,0:T(1,128)} %param.16) | copy-start | bytes 1540
  33.2 3.8 %collective-permute-start.29 = (s16[144,128]{1,0:T(8,128)(2,1)S(1)}, s16[144,128]{1,0:T(8,128)(2,1)S(1)}, u32[]{:S(2)}, u32[]{:S(2)}) collective-permute-start(s16[144,128]{1,0:T(8,128)(2,1)S(1)} %get-tuple-element.76.refs_0_), channel_id=1, source_target_pairs={{0,3},{1,2},{2,1},{3,0},{4,7},{5,6},{6,5},{7,4},{8,11},{9,10},{10,... | collective-permute-start | bytes 110600 | tf_op jit(solution)/shard_map/ppermute | solution.py:246
  33.3 4.2 %collective-permute-start.28 = (s16[144,128]{1,0:T(8,128)(2,1)S(1)}, s16[144,128]{1,0:T(8,128)(2,1)S(1)}, u32[]{:S(2)}, u32[]{:S(2)}) collective-permute-start(s16[144,128]{1,0:T(8,128)(2,1)S(1)} %get-tuple-element.76.refs_0_), channel_id=1, source_target_pairs={{0,2},{1,3},{2,0},{3,1},{4,6},{5,7},{6,4},{7,5},{8,10},{9,11},{10,... | collective-permute-start | bytes 110600 | tf_op jit(solution)/shard_map/ppermute | solution.py:246
  34.9 2.6 %collective-permute-start.27 = (s16[144,128]{1,0:T(8,128)(2,1)S(1)}, s16[144,128]{1,0:T(8,128)(2,1)S(1)}, u32[]{:S(2)}, u32[]{:S(2)}) collective-permute-start(s16[144,128]{1,0:T(8,128)(2,1)S(1)} %get-tuple-element.76.refs_0_), channel_id=1, source_target_pairs={{0,1},{1,0},{2,3},{3,2},{4,5},{5,4},{6,7},{7,6},{8,9},{9,8},{10,11... | collective-permute-start | bytes 110600 | tf_op jit(solution)/shard_map/ppermute | solution.py:246

commit v5 on v4

--- a/solution.py
+++ b/solution.py
@@ -76,18 +76,17 @@
 
 
 def transpose_product_kernel(owned, *refs):
-    (rows_hbm, cols_hbm, duals_hbm, tiles_hbm), others_hbm, refs = refs[:4], refs[4:9], refs[9:]
-    (out_ref, slot_ref, duals, tiles), others, refs = refs[:4], refs[4:9], refs[9:]
-    rows, cols, picked, exponents, parts, small_sems, tile_sems, other_sems = refs
-    n_row = out_ref.shape[0]
+    (rows_hbm, cols_hbm, duals_hbm, tiles_hbm), (out_ref, slot_ref, duals, tiles), refs = refs[:4], refs[4:8], refs[8:]
+    rows, cols, picked, exponents, parts, small_sems, tile_sems = refs
+    n_row = 2 * out_ref.shape[0]
     chunks, head_rows = rounds_of(n_row)
     most = SLOTS - head_rows
+    me = lax.axis_index("row")
     k_tiles = tiles.shape[0]
     n_groups = k_tiles // GROUP
     groups = [pl.ds(g * GROUP, GROUP) for g in range(n_groups)]
     small = started([cols_hbm, rows_hbm, duals_hbm], [cols, rows, duals], small_sems)
     large = started([tiles_hbm.at[g] for g in groups], [tiles.at[g] for g in groups], tile_sems)
-    later = started(others_hbm, others, other_sems)
 
     small[0].wait()
     square = (k_tiles, k_tiles)
@@ -105,7 +104,7 @@
     slot_ref[...] = slot_down
     too_many = where_one(jnp.max(rank_across, axis=1, keepdims=True) >= most)
     to_slots = where_one(iota((n_row * SLOTS, k_tiles), 0) == slot_across)
-    here = jnp.where(rank_down < most, lax.axis_index("row") * SLOTS + head_rows + rank_down, -1)
+    here = jnp.where(rank_down < most, me * SLOTS + head_rows + rank_down, -1)
     to_lanes = where_one(iota((k_tiles, n_row * SLOTS), 1) == here)
     of_owner = where_one(iota((n_row, k_tiles), 0) == owner_across)
     place = col_across - owner_across * owned + 1
@@ -134,6 +133,7 @@
     both = jnp.dot(to_slots.astype(bf16), parts[...], preferred_element_type=f32)
     body = both[:, :TILE] + both[:, TILE:]
     line = iota((head_rows, TILE), 0)
+    payloads = []
     for o in range(n_row):
         head = jnp.where(line == 2 * chunks, too_many, 0.0)
         for c in range(chunks):
@@ -141,23 +141,43 @@
             head = jnp.where(line == c, places[o : o + 1, lanes], head)
             head = jnp.where(line == chunks + c, scales[o : o + 1, lanes], head)
         rows_of = body[o * SLOTS + head_rows : (o + 1) * SLOTS]
-        out_ref[o] = jnp.concatenate([head, rows_of], axis=0).astype(i32).astype(i16)
-    for copy in later:
-        copy.wait()
+        payloads.append(jnp.concatenate([head, rows_of], axis=0))
+    for z, (same_side, other_side) in enumerate(by_side(me, payloads)):
+        out_ref[z, 0] = same_side.astype(i32).astype(i16)
+        out_ref[z, 1] = other_side.astype(i32).astype(i16)
+
+
+def by_side(me, blocks):
+    even = me % 2 == 0
+    return [
+        (jnp.where(even, first, second), jnp.where(even, second, first))
+        for first, second in zip(blocks[0::2], blocks[1::2])
+    ]
+
+
+def by_place(me, near, far):
+    even = me % 2 == 0
+    blocks = []
+    for z in range(far.shape[0]):
+        same_side, other_side = near[z, 0].astype(f32), far[z].astype(f32)
+        blocks += [jnp.where(even, same_side, other_side), jnp.where(even, other_side, same_side)]
+    return jnp.concatenate(blocks, axis=0)
 
 
 def primal_kernel(
-    payloads, primal_ref, cost_ref, lower_ref, upper_ref, kind_ref, steps_ref, next_ref, wanted, flag_ref, extrap
+    near, far, primal_ref, cost_ref, lower_ref, upper_ref, kind_ref, steps_ref, next_ref, wanted, flag_ref, extrap
 ):
-    n_row = payloads.shape[0]
+    n_row = 2 * far.shape[0]
+    me = lax.axis_index("row")
     chunks, head_rows = rounds_of(n_row)
     blocks = primal_ref.shape[0]
     padded = extrap.shape[0]
+    arrived = by_place(me, near, far)
     head = jnp.zeros((head_rows, TILE), f32)
     for s in range(n_row):
-        head += payloads[s].astype(i32)[:head_rows].astype(f32)
+        head += arrived[s * SLOTS : s * SLOTS + head_rows]
     flag_ref[...] = jnp.broadcast_to(head[2 * chunks : 2 * chunks + 1], flag_ref.shape)
-    whole = payloads[...].reshape(n_row * SLOTS, TILE).astype(i32)
+    whole = arrived.astype(i32)
     down = iota((blocks, TILE), 0) + 1
     head_whole = head.astype(i32)
     masks, wholes = [], []
@@ -182,15 +202,19 @@
         jnp.dot(where_one(across == places[:, c : c + 1]).astype(bf16), right, preferred_element_type=f32)
         for c in range(chunks)
     ]
-    wanted[...] = jnp.concatenate(sent, axis=0).astype(bf16).reshape(wanted.shape)
+    sent = jnp.concatenate(sent, axis=0)
+    blocks_sent = [sent[s * SLOTS : (s + 1) * SLOTS] for s in range(n_row)]
+    for z, (same_side, other_side) in enumerate(by_side(me, blocks_sent)):
+        wanted[z, 0] = same_side.astype(bf16)
+        wanted[z, 1] = other_side.astype(bf16)
 
 
 def product_kernel(*refs):
-    (rows_ref, slot_ref, tiles_ref, arrived, flag_ref), others_hbm, refs = refs[:5], refs[5:7], refs[7:]
+    (rows_ref, slot_ref, tiles_ref, near, far, flag_ref), others_hbm, refs = refs[:6], refs[6:8], refs[8:]
     out_ref, others, sems = refs[0], refs[1:3], refs[3]
     later = started(others_hbm, others, sems)
     k_tiles = tiles_ref.shape[0]
-    received = arrived[...].reshape(-1, TILE)
+    received = by_place(lax.axis_index("row"), near, far).astype(bf16)
     across = iota((k_tiles, received.shape[0]), 1)
     slots = jnp.concatenate([slot_ref[...]] * (received.shape[0] // TILE), axis=1)
     block = jnp.dot(where_one(across == slots).astype(bf16), received, preferred_element_type=f32)
@@ -244,6 +268,13 @@
 
 def gathered_along(array, axis):
     return [array] + [lax.ppermute(array, axis, there) for there, _ in partners(axis)]
+
+
+def exchanged_along_row(array):
+    size = lax.axis_size("row")
+    groups = [list(range(0, size, 2)), list(range(1, size, 2))]
+    near = lax.all_to_all(array, "row", 0, 0, axis_index_groups=groups)
+    return near, lax.ppermute(near[:, 1], "row", [(i, i ^ 1) for i in range(size)])
 
 
 def sums_at(places, terms, blocks):
@@ -307,19 +338,19 @@
     by_block = lambda array: in_hbm(array.reshape(-1, TILE))
     shape_of = lambda array: jax.ShapeDtypeStruct(array.shape, array.dtype)
     params = pltpu.CompilerParams(vmem_limit_bytes=32 * 1024 * 1024)
-    primal_side = [by_block(a) for a in (primal, cost_vec, lower_bound, upper_bound, bound_kind)]
+    primal_side = [a.reshape(-1, TILE) for a in (primal, cost_vec, lower_bound, upper_bound, bound_kind)]
     dual_side = [by_block(a) for a in (right_side, row_kind)]
     own = [by_block(duals), in_hbm(tiles)]
 
-    col_terms, slots, duals_kept, tiles_kept, *primal_kept = pl.pallas_call(
+    col_terms, slots, duals_kept, tiles_kept = pl.pallas_call(
         functools.partial(transpose_product_kernel, col_blocks),
         out_shape=(
-            jax.ShapeDtypeStruct((n_row, SLOTS, TILE), i16),
+            jax.ShapeDtypeStruct((n_row // 2, 2, SLOTS, TILE), i16),
             jax.ShapeDtypeStruct((k_tiles, TILE), i32),
-            *[shape_of(a) for a in own + primal_side],
+            *[shape_of(a) for a in own],
         ),
-        in_specs=[HBM] * 9,
-        out_specs=(VMEM,) * 9,
+        in_specs=[HBM] * 4,
+        out_specs=(VMEM,) * 4,
         scratch_shapes=[
             pltpu.SMEM((k_tiles,), i32),
             pltpu.VMEM((1, k_tiles), i32),
@@ -328,36 +359,35 @@
             pltpu.VMEM((k_tiles, 2 * TILE), bf16),
             pltpu.SemaphoreType.DMA((3,)),
             pltpu.SemaphoreType.DMA((k_tiles // GROUP,)),
-            pltpu.SemaphoreType.DMA((5,)),
         ],
         compiler_params=params,
         name="transpose_product",
-    )(in_hbm(rows), in_hbm(cols.reshape(1, k_tiles)), *own, *primal_side)
+    )(in_hbm(rows), in_hbm(cols.reshape(1, k_tiles)), *own)
     primal_next, wanted, flag = pl.pallas_call(
         primal_kernel,
         out_shape=(
             jax.ShapeDtypeStruct((col_blocks, TILE), f32),
-            jax.ShapeDtypeStruct((n_row, SLOTS, TILE), bf16),
+            jax.ShapeDtypeStruct((n_row // 2, 2, SLOTS, TILE), bf16),
             jax.ShapeDtypeStruct((8, TILE), f32),
         ),
-        in_specs=[VMEM] * 6 + [SMEM],
+        in_specs=[VMEM] * 7 + [SMEM],
         out_specs=(VMEM,) * 3,
         scratch_shapes=[pltpu.VMEM((padded, TILE), f32)],
         compiler_params=params,
         name="primal_step",
-    )(lax.all_to_all(col_terms, "row", 0, 0), *primal_kept, step_sizes)
+    )(*exchanged_along_row(col_terms), *primal_side, step_sizes)
     row_terms, *dual_kept = pl.pallas_call(
         product_kernel,
         out_shape=(
             jax.ShapeDtypeStruct((k_tiles + HEAD, TILE), i16),
             *[shape_of(a) for a in dual_side],
         ),
-        in_specs=[VMEM] * 5 + [HBM] * 2,
+        in_specs=[VMEM] * 6 + [HBM] * 2,
         out_specs=(VMEM,) * 3,
         scratch_shapes=[pltpu.SemaphoreType.DMA((2,))],
         compiler_params=params,
         name="product",
-    )(rows.reshape(1, k_tiles), slots, tiles_kept, lax.all_to_all(wanted, "row", 0, 0), flag, *dual_side)
+    )(rows.reshape(1, k_tiles), slots, tiles_kept, *exchanged_along_row(wanted), flag, *dual_side)
     dual_next, too_many = pl.pallas_call(
         functools.partial(dual_kernel, n_col),
         out_shape=(jax.ShapeDtypeStruct((row_blocks, TILE), f32), jax.ShapeDtypeStruct((1,), i32)),

time: 40 us -> 44.2 us (1.10)
  waiting for transfers between devices: 2.31 us -> 7.45 us
  blocking collectives: 23.8 us -> 20.3 us
  starting transfers between devices: 1.92 us -> 4.96 us
    ppermute x0 -> x2, waiting for transfers between devices: none -> 5.14 us  [exchanged_along_row(): lax.ppermute(near[:, 1], 'row', [(i, i ^ 1) for i in range(size)])]
    all_to_all x2, blocking collectives: 23.8 us -> 20.3 us  [exchanged_along_row(): near = lax.all_to_all(array, 'row', 0, 0, axis_index_groups=groups)]
    ppermute x0 -> x2, starting transfers between devices: none -> 3.04 us  [exchanged_along_row(): lax.ppermute(near[:, 1], 'row', [(i, i ^ 1) for i in range(size)])]
  transfers between devices with their start and end apart: 3 -> 5, of which waited for: 2 -> 4; matrix products, arithmetic and copies ran while one was open for 0% -> 0% of each run, Pallas kernels for 0% -> 0%
where the time goes in v5:
time: 44.2 us; the launch traced here: 44 us
  blocking collectives  20.3 us (46%)
  Pallas kernels  9.87 us (22%)
  waiting for transfers between devices  7.45 us (17%)
  starting transfers between devices  4.96 us (11%)
  between operations  1.39 us (3%)
    all_to_all x2, blocking collectives, exchanged_along_row(): near = lax.all_to_all(array, 'row', 0, 0, axis_index_groups=groups)  20.3 us
    ppermute x2, waiting for transfers between devices, exchanged_along_row(): lax.ppermute(near[:, 1], 'row', [(i, i ^ 1) for i in range(size)])  5.14 us
    pallas_call x1, Pallas kernels, local(): pl.pallas_call(functools.partial(transpose_product_kernel, col_blocks), o...  4.83 us
    ppermute x2, starting transfers between devices, exchanged_along_row(): lax.ppermute(near[:, 1], 'row', [(i, i ^ 1) for i in range(size)])  3.04 us
    ppermute x3, waiting for transfers between devices, gathered_along(): lax.ppermute(array, axis, there)  2.31 us
    ppermute x3, starting transfers between devices, gathered_along(): lax.ppermute(array, axis, there)  1.92 us
    pallas_call x1, Pallas kernels, local(): pl.pallas_call(primal_kernel, out_shape=(jax.ShapeDtypeStruct((col_blocks...  1.74 us
    pallas_call x1, Pallas kernels, local(): pl.pallas_call(product_kernel, out_shape=(jax.ShapeDtypeStruct((k_tiles +...  1.73 us
  transfers between devices with their start and end apart: 5, of which 4 were waited for; matrix products, arithmetic and copies ran while one was open for 0% of the time, Pallas kernels for 0%

profile of v5, /device:TPU:0, one launch (start us, length us, event | category | flops | bytes accessed | tf_op | source)
XLA Modules:
  0.0 44.0 jit_solution(11282257353461241100)
XLA Ops:
  0.6 0.0 copy-start.10
  0.6 0.0 copy-start.9
  0.7 0.0 copy-start.3
  0.7 0.0 copy-start.4
  0.7 0.0 copy-start.5
  0.7 0.0 copy-start.6
  0.7 0.0 copy-start.7
  0.7 4.8 %transpose_product.1 = (s16[4,2,48,128]{3,2,1,0:T(8,128)(2,1)S(1)}, s32[128,128]{1,0:T(8,128)S(1)}, f32[496,128]{1,0:T(8,128)S(1)}, bf16[128,128,128]{2,1,0:T(8,128)(2,1)S(1)}) custom-call(s32[128]{0:T(128)} %bitcast.98, s32[1,128]{1,0:T(1,128)} %bitcast.101, f32[496,128]{1,0:T(8,128)} %bitcast.75, bf16[128,128,128]{2,1,0:T(8,128)(2,1)} %bitcast.73), custom_call_target="tpu_custom_call" | custom-call | tf_op jit(solution)/shard_map/transpose_product/pallas_call | solution.py:345
  5.5 0.0 copy-start
  5.6 0.0 copy-start.1
  5.6 0.0 copy-start.2
  5.6 0.0 copy-start.11
  5.6 12.1 %all_to_all.10.near = s16[4,2,48,128]{3,2,1,0:T(8,128)(2,1)S(1)} all-to-all(s16[4,2,48,128]{3,2,1,0:T(8,128)(2,1)S(1)} %get-tuple-element.63), channel_id=1, replica_groups={{0,8,16,24},{4,12,20,28},{1,9,17,25},{5,13,21,29},{2,10,18,26},{6,14,22..., dimensions={0} | all-to-all | bytes 196608 | tf_op jit(solution)/shard_map/all_to_all | solution.py:276
  17.7 1.5 %collective-permute-start.27 = (s16[4,48,128]{2,1,0:T(8,128)(2,1)S(1)}, s16[4,48,128]{2,1,0:T(8,128)(2,1)S(1)}, u32[]{:S(2)}, u32[]{:S(2)}) collective-permute-start(s16[4,48,128]{2,1,0:T(8,128)(2,1)S(1)} %slice_bitcast_fusion.1), channel_id=1, source_target_pairs={{0,4},{4,0},{8,12},{12,8},{16,20},{20,16},{24,28},{28,24},{1,5},{5... | collective-permute-start | bytes 147464 | tf_op jit(solution)/shard_map/ppermute | solution.py:277
  19.2 2.6 %collective-permute-done.27.far = s16[4,48,128]{2,1,0:T(8,128)(2,1)S(1)} collective-permute-done((s16[4,48,128]{2,1,0:T(8,128)(2,1)S(1)}, s16[4,48,128]{2,1,0:T(8,128)(2,1)S(1)}, u32[]{:S(2)}, u32[]{:S(2)}) %collective-permute-start.27) | collective-permute-done | bytes 49184 | tf_op jit(solution)/shard_map/ppermute | solution.py:277
  21.8 0.0 copy-done.9
  21.8 0.0 copy-done.3
  21.8 0.0 copy-done.4
  21.8 0.0 copy-done.5
  21.8 0.0 copy-done.6
  21.8 0.0 copy-done.7
  21.8 1.7 %primal_step.1 = (f32[488,128]{1,0:T(8,128)}, bf16[4,2,48,128]{3,2,1,0:T(8,128)(2,1)S(1)}, f32[8,128]{1,0:T(8,128)S(1)}) custom-call(s16[4,2,48,128]{3,2,1,0:T(8,128)(2,1)S(1)} %all_to_all.10.near, s16[4,48,128]{2,1,0:T(8,128)(2,1)S(1)} %collective-permute-done.27.far, f32[488,128]{1,0:T(8,128)S(1)} %bitcast.78, f32[488,128]{1,0:T(8,128)S(1)} %bitcast.93, ...), custom_call_target="tpu_custom_call" | custom-call | tf_op jit(solution)/shard_map/primal_step/pallas_call | solution.py:366
  23.5 8.2 %all_to_all.11.refs_3_ = bf16[4,2,48,128]{3,2,1,0:T(8,128)(2,1)S(1)} all-to-all(bf16[4,2,48,128]{3,2,1,0:T(8,128)(2,1)S(1)} %get-tuple-element.64), channel_id=1, replica_groups={{0,8,16,24},{4,12,20,28},{1,9,17,25},{5,13,21,29},{2,10,18,26},{6,14,22..., dimensions={0} | all-to-all | bytes 196608 | tf_op jit(solution)/shard_map/all_to_all | solution.py:276
  31.7 1.5 %collective-permute-start.28 = (bf16[4,48,128]{2,1,0:T(8,128)(2,1)S(1)}, bf16[4,48,128]{2,1,0:T(8,128)(2,1)S(1)}, u32[]{:S(2)}, u32[]{:S(2)}) collective-permute-start(bf16[4,48,128]{2,1,0:T(8,128)(2,1)S(1)} %slice_bitcast_fusion), channel_id=1, source_target_pairs={{0,4},{4,0},{8,12},{12,8},{16,20},{20,16},{24,28},{28,24},{1,5},{5... | collective-permute-start | bytes 147464 | tf_op jit(solution)/shard_map/ppermute | solution.py:277
  33.3 2.6 %collective-permute-done.28.refs_4_ = bf16[4,48,128]{2,1,0:T(8,128)(2,1)S(1)} collective-permute-done((bf16[4,48,128]{2,1,0:T(8,128)(2,1)S(1)}, bf16[4,48,128]{2,1,0:T(8,128)(2,1)S(1)}, u32[]{:S(2)}, u32[]{:S(2)}) %collective-permute-start.28) | collective-permute-done | bytes 49184 | tf_op jit(solution)/shard_map/ppermute | solution.py:277
  35.8 0.0 copy-done.10
  35.8 1.7 %product.1 = (s16[144,128]{1,0:T(8,128)(2,1)S(1)}, f32[496,128]{1,0:T(8,128)S(1)}, s32[496,128]{1,0:T(8,128)S(1)}) custom-call(s32[1,128]{1,0:T(1,128)S(1)} %bitcast.99, s32[128,128]{1,0:T(8,128)S(1)} %get-tuple-element.61.refs_1_, bf16[128,128,128]{2,1,0:T(8,128)(2,1)S(1)} %get-tuple-element.62.refs_2_, bf16[4,2,48,128]{3,2,1,0:T(8,128)(2,1)S(1)} %all_to_all.11.refs_3_, ...), custom_call_target="tpu_custom_call" | custom-call | tf_op jit(solution)/shard_map/product/pallas_call | solution.py:379
  37.6 0.1 collective-permute-start.31
  37.7 1.6 %collective-permute-start.30 = (s16[144,128]{1,0:T(8,128)(2,1)S(1)}, s16[144,128]{1,0:T(8,128)(2,1)S(1)}, u32[]{:S(2)}, u32[]{:S(2)}) collective-permute-start(s16[144,128]{1,0:T(8,128)(2,1)S(1)} %get-tuple-element.66.refs_0_), channel_id=1, source_target_pairs={{0,2},{1,3},{2,0},{3,1},{4,6},{5,7},{6,4},{7,5},{8,10},{9,11},{10,... | collective-permute-start | bytes 110600 | tf_op jit(solution)/shard_map/ppermute | solution.py:270
  39.2 0.3 collective-permute-start.29
  39.5 1.9 %collective-permute-done.31.refs_3_ = s16[144,128]{1,0:T(8,128)(2,1)S(1)} collective-permute-done((s16[144,128]{1,0:T(8,128)(2,1)S(1)}, s16[144,128]{1,0:T(8,128)(2,1)S(1)}, u32[]{:S(2)}, u32[]{:S(2)}) %collective-permute-start.31) | collective-permute-done | bytes 36896 | tf_op jit(solution)/shard_map/ppermute | solution.py:270
  41.4 0.4 %collective-permute-done.30.refs_2_ = s16[144,128]{1,0:T(8,128)(2,1)S(1)} collective-permute-done((s16[144,128]{1,0:T(8,128)(2,1)S(1)}, s16[144,128]{1,0:T(8,128)(2,1)S(1)}, u32[]{:S(2)}, u32[]{:S(2)}) %collective-permute-start.30) | collective-permute-done | bytes 36896 | tf_op jit(solution)/shard_map/ppermute | solution.py:270
  41.8 0.0 collective-permute-done.29.refs_1_
  41.8 1.6 %dual_step.1 = (f32[496,128]{1,0:T(8,128)}, s32[1]{0:T(128)}) custom-call(s16[144,128]{1,0:T(8,128)(2,1)S(1)} %get-tuple-element.66.refs_0_, s16[144,128]{1,0:T(8,128)(2,1)S(1)} %collective-permute-done.29.refs_1_, s16[144,128]{1,0:T(8,128)(2,1)S(1)} %collective-permute-done.30.refs_2_, s16[144,128]{1,0:T(8,128)(2,1)S(1)} %collective-permute-done.31.refs_3_, ...), custom_call_target="tpu_custom_call" | custom-call | tf_op jit(solution)/shard_map/dual_step/pallas_call | solution.py:391
  44.0 0.0 copy-done
  44.0 0.0 copy-done.1
  44.0 0.0 copy-done.2
  44.0 0.0 copy-done.11
  (3 shorter events, 0.0 us)
Async XLA Ops:
  0.6 35.2 %copy-start.10 = (s32[1,1,128]{2,1,0:T(1,128)S(1)}, s32[1,1,128]{2,1,0:T(1,128)}, u32[]{:S(2)}) copy-start(s32[1,1,128]{2,1,0:T(1,128)} %param.15) | copy-start | bytes 1540
  0.6 21.1 %copy-start.9 = (f32[2]{0:T(128)S(1)}, f32[2]{0:T(128)}, u32[]{:S(2)}) copy-start(f32[2]{0:T(128)} %refs_7_.1) | copy-start | bytes 28
  0.7 21.1 %copy-start.3 = (f32[62464]{0:T(1024)S(1)}, f32[62464]{0:T(1024)}, u32[]{:S(2)}) copy-start(f32[62464]{0:T(1024)} %param.17) | copy-start | bytes 749572
  0.7 21.1 %copy-start.4 = (f32[62464]{0:T(1024)S(1)}, f32[62464]{0:T(1024)}, u32[]{:S(2)}) copy-start(f32[62464]{0:T(1024)} %param.19) | copy-start | bytes 749572
  0.7 21.1 %copy-start.5 = (f32[62464]{0:T(1024)S(1)}, f32[62464]{0:T(1024)}, u32[]{:S(2)}) copy-start(f32[62464]{0:T(1024)} %param.20) | copy-start | bytes 749572
  0.7 21.1 %copy-start.6 = (f32[62464]{0:T(1024)S(1)}, f32[62464]{0:T(1024)}, u32[]{:S(2)}) copy-start(f32[62464]{0:T(1024)} %param.21) | copy-start | bytes 749572
  0.7 21.1 %copy-start.7 = (s32[62464]{0:T(1024)S(1)}, s32[62464]{0:T(1024)}, u32[]{:S(2)}) copy-start(s32[62464]{0:T(1024)} %param.22) | copy-start | bytes 749572
  5.5 38.4 %copy-start = (f32[63488]{0:T(1024)S(1)}, f32[63488]{0:T(1024)}, u32[]{:S(2)}) copy-start(f32[63488]{0:T(1024)} %param.18) | copy-start | bytes 761860
  5.6 38.4 %copy-start.1 = (f32[63488]{0:T(1024)S(1)}, f32[63488]{0:T(1024)}, u32[]{:S(2)}) copy-start(f32[63488]{0:T(1024)} %param.23) | copy-start | bytes 761860
  5.6 38.4 %copy-start.2 = (s32[63488]{0:T(1024)S(1)}, s32[63488]{0:T(1024)}, u32[]{:S(2)}) copy-start(s32[63488]{0:T(1024)} %param.24) | copy-start | bytes 761860
  5.6 38.4 %copy-start.11 = (s32[1,1,128]{2,1,0:T(1,128)S(1)}, s32[1,1,128]{2,1,0:T(1,128)}, u32[]{:S(2)}) copy-start(s32[1,1,128]{2,1,0:T(1,128)} %param.16) | copy-start | bytes 1540
  17.7 4.1 %collective-permute-start.27 = (s16[4,48,128]{2,1,0:T(8,128)(2,1)S(1)}, s16[4,48,128]{2,1,0:T(8,128)(2,1)S(1)}, u32[]{:S(2)}, u32[]{:S(2)}) collective-permute-start(s16[4,48,128]{2,1,0:T(8,128)(2,1)S(1)} %slice_bitcast_fusion.1), channel_id=1, source_target_pairs={{0,4},{4,0},{8,12},{12,8},{16,20},{20,16},{24,28},{28,24},{1,5},{5... | collective-permute-start | bytes 147464 | tf_op jit(solution)/shard_map/ppermute | solution.py:277
  31.7 4.1 %collective-permute-start.28 = (bf16[4,48,128]{2,1,0:T(8,128)(2,1)S(1)}, bf16[4,48,128]{2,1,0:T(8,128)(2,1)S(1)}, u32[]{:S(2)}, u32[]{:S(2)}) collective-permute-start(bf16[4,48,128]{2,1,0:T(8,128)(2,1)S(1)} %slice_bitcast_fusion), channel_id=1, source_target_pairs={{0,4},{4,0},{8,12},{12,8},{16,20},{20,16},{24,28},{28,24},{1,5},{5... | collective-permute-start | bytes 147464 | tf_op jit(solution)/shard_map/ppermute | solution.py:277
  37.6 3.8 %collective-permute-start.31 = (s16[144,128]{1,0:T(8,128)(2,1)S(1)}, s16[144,128]{1,0:T(8,128)(2,1)S(1)}, u32[]{:S(2)}, u32[]{:S(2)}) collective-permute-start(s16[144,128]{1,0:T(8,128)(2,1)S(1)} %get-tuple-element.66.refs_0_), channel_id=1, source_target_pairs={{0,3},{1,2},{2,1},{3,0},{4,7},{5,6},{6,5},{7,4},{8,11},{9,10},{10,... | collective-permute-start | bytes 110600 | tf_op jit(solution)/shard_map/ppermute | solution.py:270
  37.7 4.2 %collective-permute-start.30 = (s16[144,128]{1,0:T(8,128)(2,1)S(1)}, s16[144,128]{1,0:T(8,128)(2,1)S(1)}, u32[]{:S(2)}, u32[]{:S(2)}) collective-permute-start(s16[144,128]{1,0:T(8,128)(2,1)S(1)} %get-tuple-element.66.refs_0_), channel_id=1, source_target_pairs={{0,2},{1,3},{2,0},{3,1},{4,6},{5,7},{6,4},{7,5},{8,10},{9,11},{10,... | collective-permute-start | bytes 110600 | tf_op jit(solution)/shard_map/ppermute | solution.py:270
  39.2 2.6 %collective-permute-start.29 = (s16[144,128]{1,0:T(8,128)(2,1)S(1)}, s16[144,128]{1,0:T(8,128)(2,1)S(1)}, u32[]{:S(2)}, u32[]{:S(2)}) collective-permute-start(s16[144,128]{1,0:T(8,128)(2,1)S(1)} %get-tuple-element.66.refs_0_), channel_id=1, source_target_pairs={{0,1},{1,0},{2,3},{3,2},{4,5},{5,4},{6,7},{7,6},{8,9},{9,8},{10,11... | collective-permute-start | bytes 110600 | tf_op jit(solution)/shard_map/ppermute | solution.py:270

commit v6 on v4

--- a/solution.py
+++ b/solution.py
@@ -8,6 +8,7 @@
 
 TILE = 128
 GROUP = 16
+CHUNK = 32
 SLOTS = 48
 HEAD = 16
 BITS = 14
@@ -76,18 +77,15 @@
 
 
 def transpose_product_kernel(owned, *refs):
-    (rows_hbm, cols_hbm, duals_hbm, tiles_hbm), others_hbm, refs = refs[:4], refs[4:9], refs[9:]
-    (out_ref, slot_ref, duals, tiles), others, refs = refs[:4], refs[4:9], refs[9:]
-    rows, cols, picked, exponents, parts, small_sems, tile_sems, other_sems = refs
+    (rows_hbm, cols_hbm, duals_hbm, tiles_hbm), (out_ref, slot_ref, duals, tiles), refs = refs[:4], refs[4:8], refs[8:]
+    rows, cols, picked, terms, small_sems, tile_sems = refs
     n_row = out_ref.shape[0]
     chunks, head_rows = rounds_of(n_row)
     most = SLOTS - head_rows
     k_tiles = tiles.shape[0]
-    n_groups = k_tiles // GROUP
-    groups = [pl.ds(g * GROUP, GROUP) for g in range(n_groups)]
+    groups = [pl.ds(g * CHUNK, CHUNK) for g in range(k_tiles // CHUNK)]
     small = started([cols_hbm, rows_hbm, duals_hbm], [cols, rows, duals], small_sems)
     large = started([tiles_hbm.at[g] for g in groups], [tiles.at[g] for g in groups], tile_sems)
-    later = started(others_hbm, others, other_sems)
 
     small[0].wait()
     square = (k_tiles, k_tiles)
@@ -118,20 +116,23 @@
         copy.wait()
     for k in range(k_tiles):
         picked[pl.ds(k, 1), :] = duals[pl.ds(rows[k], 1), :]
-    for group, copy in zip(groups, large):
-        block = picked[group, :].astype(bf16).astype(f32)
-        left = jnp.concatenate([one_row_of(block, m) for m in range(GROUP)], axis=1)
+    for g, copy in enumerate(large):
         copy.wait()
-        terms = jnp.dot(left, tiles[group].reshape(GROUP * TILE, TILE), preferred_element_type=f32)
-        whole, exponents[group, :] = coded(terms)
-        parts[group, :] = two_parts(whole)
-
-    scaled = [to_lanes, to_lanes * jnp.concatenate([exponents[...]] * chunks, axis=1)]
+        for first in range(g * CHUNK, (g + 1) * CHUNK, GROUP):
+            group = pl.ds(first, GROUP)
+            block = picked[group, :].astype(bf16).astype(f32)
+            left = jnp.concatenate([one_row_of(block, m) for m in range(GROUP)], axis=1)
+            terms[group, :] = jnp.dot(
+                left, tiles[group].reshape(GROUP * TILE, TILE), preferred_element_type=f32
+            )
+    whole, exponents = coded(terms[...])
+
+    scaled = [to_lanes, to_lanes * jnp.concatenate([exponents] * chunks, axis=1)]
     heads = jnp.dot(head_left, jnp.concatenate(scaled, axis=1).astype(bf16), preferred_element_type=f32)
     width = n_row * SLOTS
     places = heads[:n_row, :width] + heads[n_row : 2 * n_row, :width]
     scales = heads[2 * n_row :, width:]
-    both = jnp.dot(to_slots.astype(bf16), parts[...], preferred_element_type=f32)
+    both = jnp.dot(to_slots.astype(bf16), two_parts(whole), preferred_element_type=f32)
     body = both[:, :TILE] + both[:, TILE:]
     line = iota((head_rows, TILE), 0)
     for o in range(n_row):
@@ -142,13 +143,13 @@
             head = jnp.where(line == chunks + c, scales[o : o + 1, lanes], head)
         rows_of = body[o * SLOTS + head_rows : (o + 1) * SLOTS]
         out_ref[o] = jnp.concatenate([head, rows_of], axis=0).astype(i32).astype(i16)
-    for copy in later:
-        copy.wait()
 
 
 def primal_kernel(
-    payloads, primal_ref, cost_ref, lower_ref, upper_ref, kind_ref, steps_ref, next_ref, wanted, flag_ref, extrap
+    payloads, primal_ref, cost_ref, lower_ref, upper_ref, kind_ref, steps_ref, next_hbm, flag_ref, *refs
 ):
+    wanted, (next_ref, extrap, in_order, sem) = refs[:-4], refs[-4:]
+    me = lax.axis_index("row")
     n_row = payloads.shape[0]
     chunks, head_rows = rounds_of(n_row)
     blocks = primal_ref.shape[0]
@@ -171,6 +172,8 @@
     moved = jnp.where(kind % 2 == 1, jnp.maximum(moved, lower_ref[...]), moved)
     moved = jnp.where(kind >= 2, jnp.minimum(moved, upper_ref[...]), moved)
     next_ref[...] = moved
+    copy = pltpu.make_async_copy(next_ref, next_hbm, sem)
+    copy.start()
     aligned = blocks // 8 * 8
     if padded > aligned:
         extrap[pl.ds(aligned, padded - aligned), :] = jnp.zeros((padded - aligned, TILE), f32)
@@ -182,15 +185,21 @@
         jnp.dot(where_one(across == places[:, c : c + 1]).astype(bf16), right, preferred_element_type=f32)
         for c in range(chunks)
     ]
-    wanted[...] = jnp.concatenate(sent, axis=0).astype(bf16).reshape(wanted.shape)
+    in_order[...] = jnp.concatenate(sent, axis=0).astype(bf16).reshape(in_order.shape)
+    for n, target in enumerate(wanted):
+        target[...] = in_order[place_of(me, n, n_row, back=True)]
+    copy.wait()
 
 
 def product_kernel(*refs):
-    (rows_ref, slot_ref, tiles_ref, arrived, flag_ref), others_hbm, refs = refs[:5], refs[5:7], refs[7:]
-    out_ref, others, sems = refs[0], refs[1:3], refs[3]
+    (rows_ref, slot_ref, tiles_ref, flag_ref), others_hbm, refs = refs[:4], refs[4:6], refs[6:]
+    arrived, (out_ref, *others, in_order, sems) = refs[:-5], refs[-5:]
+    me = lax.axis_index("row")
+    for n, source in enumerate(arrived):
+        in_order[place_of(me, n, len(arrived), back=False)] = source[...]
     later = started(others_hbm, others, sems)
     k_tiles = tiles_ref.shape[0]
-    received = arrived[...].reshape(-1, TILE)
+    received = in_order[...].reshape(-1, TILE)
     across = iota((k_tiles, received.shape[0]), 1)
     slots = jnp.concatenate([slot_ref[...]] * (received.shape[0] // TILE), axis=1)
     block = jnp.dot(where_one(across == slots).astype(bf16), received, preferred_element_type=f32)
@@ -231,6 +240,12 @@
     updated = duals_ref[...] + steps_ref[1] * (right_ref[...] - row_sums)
     next_ref[...] = jnp.where(kind_ref[...] == 1, jnp.maximum(updated, 0.0), updated)
     flag_ref[0] = jnp.max(flags)
+
+
+def place_of(me, n, size, back):
+    if size & (size - 1) == 0:
+        return jnp.bitwise_xor(me, n)
+    return lax.rem(me + (size - n if back else n), size)
 
 
 def partners(axis):
@@ -307,57 +322,68 @@
     by_block = lambda array: in_hbm(array.reshape(-1, TILE))
     shape_of = lambda array: jax.ShapeDtypeStruct(array.shape, array.dtype)
     params = pltpu.CompilerParams(vmem_limit_bytes=32 * 1024 * 1024)
-    primal_side = [by_block(a) for a in (primal, cost_vec, lower_bound, upper_bound, bound_kind)]
+    primal_side = [a.reshape(-1, TILE) for a in (primal, cost_vec, lower_bound, upper_bound, bound_kind)]
     dual_side = [by_block(a) for a in (right_side, row_kind)]
     own = [by_block(duals), in_hbm(tiles)]
 
-    col_terms, slots, duals_kept, tiles_kept, *primal_kept = pl.pallas_call(
+    col_terms, slots, duals_kept, tiles_kept = pl.pallas_call(
         functools.partial(transpose_product_kernel, col_blocks),
         out_shape=(
             jax.ShapeDtypeStruct((n_row, SLOTS, TILE), i16),
             jax.ShapeDtypeStruct((k_tiles, TILE), i32),
-            *[shape_of(a) for a in own + primal_side],
+            *[shape_of(a) for a in own],
         ),
-        in_specs=[HBM] * 9,
-        out_specs=(VMEM,) * 9,
+        in_specs=[HBM] * 4,
+        out_specs=(VMEM,) * 4,
         scratch_shapes=[
             pltpu.SMEM((k_tiles,), i32),
             pltpu.VMEM((1, k_tiles), i32),
             pltpu.VMEM((k_tiles, TILE), f32),
             pltpu.VMEM((k_tiles, TILE), f32),
-            pltpu.VMEM((k_tiles, 2 * TILE), bf16),
             pltpu.SemaphoreType.DMA((3,)),
-            pltpu.SemaphoreType.DMA((k_tiles // GROUP,)),
-            pltpu.SemaphoreType.DMA((5,)),
+            pltpu.SemaphoreType.DMA((k_tiles // CHUNK,)),
         ],
         compiler_params=params,
         name="transpose_product",
-    )(in_hbm(rows), in_hbm(cols.reshape(1, k_tiles)), *own, *primal_side)
-    primal_next, wanted, flag = pl.pallas_call(
+    )(in_hbm(rows), in_hbm(cols.reshape(1, k_tiles)), *own)
+    primal_next, flag, *wanted = pl.pallas_call(
         primal_kernel,
         out_shape=(
             jax.ShapeDtypeStruct((col_blocks, TILE), f32),
-            jax.ShapeDtypeStruct((n_row, SLOTS, TILE), bf16),
             jax.ShapeDtypeStruct((8, TILE), f32),
+            *[jax.ShapeDtypeStruct((SLOTS, TILE), bf16)] * n_row,
         ),
         in_specs=[VMEM] * 6 + [SMEM],
-        out_specs=(VMEM,) * 3,
-        scratch_shapes=[pltpu.VMEM((padded, TILE), f32)],
+        out_specs=(HBM, *[VMEM] * (n_row + 1)),
+        scratch_shapes=[
+            pltpu.VMEM((col_blocks, TILE), f32),
+            pltpu.VMEM((padded, TILE), f32),
+            pltpu.VMEM((n_row, SLOTS, TILE), bf16),
+            pltpu.SemaphoreType.DMA,
+        ],
         compiler_params=params,
         name="primal_step",
-    )(lax.all_to_all(col_terms, "row", 0, 0), *primal_kept, step_sizes)
+    )(lax.all_to_all(col_terms, "row", 0, 0), *primal_side, step_sizes)
     row_terms, *dual_kept = pl.pallas_call(
         product_kernel,
         out_shape=(
             jax.ShapeDtypeStruct((k_tiles + HEAD, TILE), i16),
             *[shape_of(a) for a in dual_side],
         ),
-        in_specs=[VMEM] * 5 + [HBM] * 2,
+        in_specs=[VMEM] * 4 + [HBM] * 2 + [VMEM] * n_row,
         out_specs=(VMEM,) * 3,
-        scratch_shapes=[pltpu.SemaphoreType.DMA((2,))],
+        scratch_shapes=[pltpu.VMEM((n_row, SLOTS, TILE), bf16), pltpu.SemaphoreType.DMA((2,))],
         compiler_params=params,
         name="product",
-    )(rows.reshape(1, k_tiles), slots, tiles_kept, lax.all_to_all(wanted, "row", 0, 0), flag, *dual_side)
+    )(
+        rows.reshape(1, k_tiles),
+        slots,
+        tiles_kept,
+        flag,
+        *dual_side,
+        wanted[0],
+        *[lax.ppermute(w, "row", back) for w, (_, back) in zip(wanted[1:], partners("row"))],
+    )
     dual_next, too_many = pl.pallas_call(
         functools.partial(dual_kernel, n_col),
         out_shape=(jax.ShapeDtypeStruct((row_blocks, TILE), f32), jax.ShapeDtypeStruct((1,), i32)),

time: 40 us -> 42.6 us (1.065)
  starting transfers between devices: 1.92 us -> 13.1 us
  blocking collectives: 23.8 us -> 14.3 us
  waiting for transfers between devices: 2.31 us -> 4.94 us
  Pallas kernels: 10.2 us -> 8.54 us
    ppermute x0 -> x7, starting transfers between devices: none -> 11.2 us  [local(): lax.ppermute(w, 'row', back)]
    all_to_all x1 -> x0, blocking collectives: 9.5 us -> none  [local(): lax.all_to_all(wanted, 'row', 0, 0)]
    ppermute x0 -> x7, waiting for transfers between devices: none -> 2.63 us  [local(): lax.ppermute(w, 'row', back)]
    pallas_call x1, Pallas kernels: 5.17 us -> 3.47 us  [local(): pl.pallas_call(functools.partial(transpose_product_kernel, col_blocks), o...]
  transfers between devices with their start and end apart: 3 -> 10, of which waited for: 2 -> 4; matrix products, arithmetic and copies ran while one was open for 0% -> 0% of each run, Pallas kernels for 0% -> 0%
where the time goes in v6:
time: 42.6 us; the launch traced here: 42.4 us
  blocking collectives  14.3 us (34%)
  starting transfers between devices  13.1 us (31%)
  Pallas kernels  8.54 us (20%)
  waiting for transfers between devices  4.94 us (12%)
  between operations  1.45 us (3%)
    all_to_all x1, blocking collectives, local(): lax.all_to_all(col_terms, 'row', 0, 0)  14.3 us
    ppermute x7, starting transfers between devices, local(): lax.ppermute(w, 'row', back)  11.2 us
    pallas_call x1, Pallas kernels, local(): pl.pallas_call(functools.partial(transpose_product_kernel, col_blocks), o...  3.47 us
    ppermute x7, waiting for transfers between devices, local(): lax.ppermute(w, 'row', back)  2.63 us
    ppermute x3, waiting for transfers between devices, gathered_along(): lax.ppermute(array, axis, there)  2.31 us
    ppermute x3, starting transfers between devices, gathered_along(): lax.ppermute(array, axis, there)  1.92 us
    pallas_call x1, Pallas kernels, local(): pl.pallas_call(primal_kernel, out_shape=(jax.ShapeDtypeStruct((col_blocks...  1.74 us
    pallas_call x1, Pallas kernels, local(): pl.pallas_call(product_kernel, out_shape=(jax.ShapeDtypeStruct((k_tiles +...  1.73 us
  transfers between devices with their start and end apart: 10, of which 4 were waited for; matrix products, arithmetic and copies ran while one was open for 0% of the time, Pallas kernels for 0%

profile of v6, /device:TPU:0, one launch (start us, length us, event | category | flops | bytes accessed | tf_op | source)
XLA Modules:
  0.0 42.4 jit_solution(10361584691689190565)
XLA Ops:
  0.6 0.0 copy-start.10
  0.6 0.0 copy-start.9
  0.7 0.0 copy-start.3
  0.7 0.0 copy-start.4
  0.7 0.0 copy-start.5
  0.7 0.0 copy-start.6
  0.7 0.0 copy-start.7
  0.7 3.5 %transpose_product.1 = (s16[8,48,128]{2,1,0:T(8,128)(2,1)S(1)}, s32[128,128]{1,0:T(8,128)S(1)}, f32[496,128]{1,0:T(8,128)S(1)}, bf16[128,128,128]{2,1,0:T(8,128)(2,1)S(1)}) custom-call(s32[128]{0:T(128)} %bitcast.90, s32[1,128]{1,0:T(1,128)} %bitcast.93, f32[496,128]{1,0:T(8,128)} %bitcast.67, bf16[128,128,128]{2,1,0:T(8,128)(2,1)} %bitcast.65), custom_call_target="tpu_custom_call" | custom-call | tf_op jit(solution)/shard_map/transpose_product/pallas_call | solution.py:329
  4.2 0.0 copy-start
  4.2 0.0 copy-start.1
  4.2 0.0 copy-start.2
  4.2 0.0 copy-start.11
  4.2 14.3 %all_to_all.5.payloads = s16[8,48,128]{2,1,0:T(8,128)(2,1)S(1)} all-to-all(s16[8,48,128]{2,1,0:T(8,128)(2,1)S(1)} %get-tuple-element.70), channel_id=1, replica_groups=mesh['row'=8,'col'=4] {'row'}, dimensions={0} | all-to-all | bytes 196608 | tf_op jit(solution)/shard_map/all_to_all | solution.py:366
  18.6 0.0 copy-done.9
  18.6 0.0 copy-done.3
  18.6 0.0 copy-done.4
  18.6 0.0 copy-done.5
  18.6 0.0 copy-done.6
  18.6 0.0 copy-done.7
  18.6 1.7 %primal_step.1 = (f32[488,128]{1,0:T(8,128)}, f32[8,128]{1,0:T(8,128)S(1)}, bf16[48,128]{1,0:T(8,128)(2,1)S(1)}, bf16[48,128]{1,0:T(8,128)(2,1)S(1)}, bf16[48,12...) custom-call(s16[8,48,128]{2,1,0:T(8,128)(2,1)S(1)} %all_to_all.5.pay, ...), custom_call_target="tpu_custom_call" | custom-call | tf_op jit(solution)/shard_map/primal_step/pallas_call | solution.py:349
  20.3 0.4 collective-permute-start.27
  20.7 1.0 %collective-permute-start.28 = (bf16[48,128]{1,0:T(8,128)(2,1)S(1)}, bf16[48,128]{1,0:T(8,128)(2,1)S(1)}, u32[]{:S(2)}, u32[]{:S(2)}) collective-permute-start(bf16[48,128]{1,0:T(8,128)(2,1)S(1)} %get-tuple-element.74), channel_id=1, source_target_pairs={{8,0},{12,4},{0,8},{4,12},{24,16},{28,20},{16,24},{20,28},{9,1},{1... | collective-permute-start | bytes 36872 | tf_op jit(solution)/shard_map/ppermute | solution.py:385
  21.7 2.2 %collective-permute-start.29 = (bf16[48,128]{1,0:T(8,128)(2,1)S(1)}, bf16[48,128]{1,0:T(8,128)(2,1)S(1)}, u32[]{:S(2)}, u32[]{:S(2)}) collective-permute-start(bf16[48,128]{1,0:T(8,128)(2,1)S(1)} %get-tuple-element.75), channel_id=1, source_target_pairs={{12,0},{8,4},{4,8},{0,12},{28,16},{24,20},{20,24},{16,28},{13,1},{... | collective-permute-start | bytes 36872 | tf_op jit(solution)/shard_map/ppermute | solution.py:385
  23.9 0.4 %collective-permute-start.30 = (bf16[48,128]{1,0:T(8,128)(2,1)S(1)}, bf16[48,128]{1,0:T(8,128)(2,1)S(1)}, u32[]{:S(2)}, u32[]{:S(2)}) collective-permute-start(bf16[48,128]{1,0:T(8,128)(2,1)S(1)} %get-tuple-element.76), channel_id=1, source_target_pairs={{16,0},{20,4},{24,8},{28,12},{0,16},{4,20},{8,24},{12,28},{17,1},{... | collective-permute-start | bytes 36872 | tf_op jit(solution)/shard_map/ppermute | solution.py:385
  24.3 2.2 %collective-permute-start.31 = (bf16[48,128]{1,0:T(8,128)(2,1)S(1)}, bf16[48,128]{1,0:T(8,128)(2,1)S(1)}, u32[]{:S(2)}, u32[]{:S(2)}) collective-permute-start(bf16[48,128]{1,0:T(8,128)(2,1)S(1)} %get-tuple-element.77), channel_id=1, source_target_pairs={{20,0},{16,4},{28,8},{24,12},{4,16},{0,20},{12,24},{8,28},{21,1},{... | collective-permute-start | bytes 36872 | tf_op jit(solution)/shard_map/ppermute | solution.py:385
  26.6 0.0 collective-permute-done.27.refs_7_
  26.6 1.2 %collective-permute-start.32 = (bf16[48,128]{1,0:T(8,128)(2,1)S(1)}, bf16[48,128]{1,0:T(8,128)(2,1)S(1)}, u32[]{:S(2)}, u32[]{:S(2)}) collective-permute-start(bf16[48,128]{1,0:T(8,128)(2,1)S(1)} %get-tuple-element.78), channel_id=1, source_target_pairs={{24,0},{28,4},{16,8},{20,12},{8,16},{12,20},{0,24},{4,28},{25,1},{... | collective-permute-start | bytes 36872 | tf_op jit(solution)/shard_map/ppermute | solution.py:385
  27.8 0.0 collective-permute-done.28.refs_8_
  27.8 3.8 %collective-permute-start.33 = (bf16[48,128]{1,0:T(8,128)(2,1)S(1)}, bf16[48,128]{1,0:T(8,128)(2,1)S(1)}, u32[]{:S(2)}, u32[]{:S(2)}) collective-permute-start(bf16[48,128]{1,0:T(8,128)(2,1)S(1)} %get-tuple-element.79), channel_id=1, source_target_pairs={{28,0},{24,4},{20,8},{16,12},{12,16},{8,20},{4,24},{0,28},{29,1},{... | collective-permute-start | bytes 36872 | tf_op jit(solution)/shard_map/ppermute | solution.py:385
  31.6 0.0 collective-permute-done.29.refs_9_
  31.6 0.0 collective-permute-done.30.refs_10_
  31.6 0.0 collective-permute-done.31.refs_11_
  31.6 0.5 %collective-permute-done.32.refs_12_ = bf16[48,128]{1,0:T(8,128)(2,1)S(1)} collective-permute-done((bf16[48,128]{1,0:T(8,128)(2,1)S(1)}, bf16[48,128]{1,0:T(8,128)(2,1)S(1)}, u32[]{:S(2)}, u32[]{:S(2)}) %collective-permute-start.32) | collective-permute-done | bytes 12320 | tf_op jit(solution)/shard_map/ppermute | solution.py:385
  32.1 2.1 %collective-permute-done.33.refs_13_ = bf16[48,128]{1,0:T(8,128)(2,1)S(1)} collective-permute-done((bf16[48,128]{1,0:T(8,128)(2,1)S(1)}, bf16[48,128]{1,0:T(8,128)(2,1)S(1)}, u32[]{:S(2)}, u32[]{:S(2)}) %collective-permute-start.33) | collective-permute-done | bytes 12320 | tf_op jit(solution)/shard_map/ppermute | solution.py:385
  34.2 0.0 copy-done.10
  34.2 1.7 %product.1 = (s16[144,128]{1,0:T(8,128)(2,1)S(1)}, f32[496,128]{1,0:T(8,128)S(1)}, s32[496,128]{1,0:T(8,128)S(1)}) custom-call(s32[1,128]{1,0:T(1,128)S(1)} %bitcast.91, s32[128,128]{1,0:T(8,128)S(1)} %get-tuple-element.68.refs_1_, bf16[128,128,128]{2,1,0:T(8,128)(2,1)S(1)} %get-tuple-element.69.refs_2_, f32[8,128]{1,0:T(8,128)S(1)} %get-tuple-element.71.refs_3_, ...), custom_call_target="tpu_custom_call" | custom-call | tf_op jit(solution)/shard_map/product/pallas_call | solution.py:367
  35.9 0.1 collective-permute-start.36
  36.0 1.6 %collective-permute-start.35 = (s16[144,128]{1,0:T(8,128)(2,1)S(1)}, s16[144,128]{1,0:T(8,128)(2,1)S(1)}, u32[]{:S(2)}, u32[]{:S(2)}) collective-permute-start(s16[144,128]{1,0:T(8,128)(2,1)S(1)} %get-tuple-element.80.refs_0_), channel_id=1, source_target_pairs={{0,2},{1,3},{2,0},{3,1},{4,6},{5,7},{6,4},{7,5},{8,10},{9,11},{10,... | collective-permute-start | bytes 110600 | tf_op jit(solution)/shard_map/ppermute | solution.py:261
  37.6 0.3 collective-permute-start.34
  37.9 1.9 %collective-permute-done.36.refs_3_ = s16[144,128]{1,0:T(8,128)(2,1)S(1)} collective-permute-done((s16[144,128]{1,0:T(8,128)(2,1)S(1)}, s16[144,128]{1,0:T(8,128)(2,1)S(1)}, u32[]{:S(2)}, u32[]{:S(2)}) %collective-permute-start.36) | collective-permute-done | bytes 36896 | tf_op jit(solution)/shard_map/ppermute | solution.py:261
  39.7 0.4 %collective-permute-done.35.refs_2_ = s16[144,128]{1,0:T(8,128)(2,1)S(1)} collective-permute-done((s16[144,128]{1,0:T(8,128)(2,1)S(1)}, s16[144,128]{1,0:T(8,128)(2,1)S(1)}, u32[]{:S(2)}, u32[]{:S(2)}) %collective-permute-start.35) | collective-permute-done | bytes 36896 | tf_op jit(solution)/shard_map/ppermute | solution.py:261
  40.2 0.0 collective-permute-done.34.refs_1_
  40.2 1.6 %dual_step.1 = (f32[496,128]{1,0:T(8,128)}, s32[1]{0:T(128)}) custom-call(s16[144,128]{1,0:T(8,128)(2,1)S(1)} %get-tuple-element.80.refs_0_, s16[144,128]{1,0:T(8,128)(2,1)S(1)} %collective-permute-done.34.refs_1_, s16[144,128]{1,0:T(8,128)(2,1)S(1)} %collective-permute-done.35.refs_2_, s16[144,128]{1,0:T(8,128)(2,1)S(1)} %collective-permute-done.36.refs_3_, ...), custom_call_target="tpu_custom_call" | custom-call | tf_op jit(solution)/shard_map/dual_step/pallas_call | solution.py:387
  42.4 0.0 copy-done
  42.4 0.0 copy-done.1
  42.4 0.0 copy-done.2
  42.4 0.0 copy-done.11
  (1 shorter events, 0.0 us)
Async XLA Ops:
  0.6 33.6 %copy-start.10 = (s32[1,1,128]{2,1,0:T(1,128)S(1)}, s32[1,1,128]{2,1,0:T(1,128)}, u32[]{:S(2)}) copy-start(s32[1,1,128]{2,1,0:T(1,128)} %param.15) | copy-start | bytes 1540
  0.6 17.9 %copy-start.9 = (f32[2]{0:T(128)S(1)}, f32[2]{0:T(128)}, u32[]{:S(2)}) copy-start(f32[2]{0:T(128)} %refs_7_.1) | copy-start | bytes 28
  0.7 17.9 %copy-start.3 = (f32[62464]{0:T(1024)S(1)}, f32[62464]{0:T(1024)}, u32[]{:S(2)}) copy-start(f32[62464]{0:T(1024)} %param.17) | copy-start | bytes 749572
  0.7 17.9 %copy-start.4 = (f32[62464]{0:T(1024)S(1)}, f32[62464]{0:T(1024)}, u32[]{:S(2)}) copy-start(f32[62464]{0:T(1024)} %param.19) | copy-start | bytes 749572
  0.7 17.9 %copy-start.5 = (f32[62464]{0:T(1024)S(1)}, f32[62464]{0:T(1024)}, u32[]{:S(2)}) copy-start(f32[62464]{0:T(1024)} %param.20) | copy-start | bytes 749572
  0.7 17.9 %copy-start.6 = (f32[62464]{0:T(1024)S(1)}, f32[62464]{0:T(1024)}, u32[]{:S(2)}) copy-start(f32[62464]{0:T(1024)} %param.21) | copy-start | bytes 749572
  0.7 17.9 %copy-start.7 = (s32[62464]{0:T(1024)S(1)}, s32[62464]{0:T(1024)}, u32[]{:S(2)}) copy-start(s32[62464]{0:T(1024)} %param.22) | copy-start | bytes 749572
  4.2 38.2 %copy-start = (f32[63488]{0:T(1024)S(1)}, f32[63488]{0:T(1024)}, u32[]{:S(2)}) copy-start(f32[63488]{0:T(1024)} %param.18) | copy-start | bytes 761860
  4.2 38.2 %copy-start.1 = (f32[63488]{0:T(1024)S(1)}, f32[63488]{0:T(1024)}, u32[]{:S(2)}) copy-start(f32[63488]{0:T(1024)} %param.23) | copy-start | bytes 761860
  4.2 38.2 %copy-start.2 = (s32[63488]{0:T(1024)S(1)}, s32[63488]{0:T(1024)}, u32[]{:S(2)}) copy-start(s32[63488]{0:T(1024)} %param.24) | copy-start | bytes 761860
  4.2 38.2 %copy-start.11 = (s32[1,1,128]{2,1,0:T(1,128)S(1)}, s32[1,1,128]{2,1,0:T(1,128)}, u32[]{:S(2)}) copy-start(s32[1,1,128]{2,1,0:T(1,128)} %param.16) | copy-start | bytes 1540
  20.3 6.2 %collective-permute-start.27 = (bf16[48,128]{1,0:T(8,128)(2,1)S(1)}, bf16[48,128]{1,0:T(8,128)(2,1)S(1)}, u32[]{:S(2)}, u32[]{:S(2)}) collective-permute-start(bf16[48,128]{1,0:T(8,128)(2,1)S(1)} %get-tuple-element.73), channel_id=1, source_target_pairs={{4,0},{0,4},{12,8},{8,12},{20,16},{16,20},{28,24},{24,28},{5,1},{1... | collective-permute-start | bytes 36872 | tf_op jit(solution)/shard_map/ppermute | solution.py:385
  20.7 7.1 %collective-permute-start.28 = (bf16[48,128]{1,0:T(8,128)(2,1)S(1)}, bf16[48,128]{1,0:T(8,128)(2,1)S(1)}, u32[]{:S(2)}, u32[]{:S(2)}) collective-permute-start(bf16[48,128]{1,0:T(8,128)(2,1)S(1)} %get-tuple-element.74), channel_id=1, source_target_pairs={{8,0},{12,4},{0,8},{4,12},{24,16},{28,20},{16,24},{20,28},{9,1},{1... | collective-permute-start | bytes 36872 | tf_op jit(solution)/shard_map/ppermute | solution.py:385
  21.7 9.9 %collective-permute-start.29 = (bf16[48,128]{1,0:T(8,128)(2,1)S(1)}, bf16[48,128]{1,0:T(8,128)(2,1)S(1)}, u32[]{:S(2)}, u32[]{:S(2)}) collective-permute-start(bf16[48,128]{1,0:T(8,128)(2,1)S(1)} %get-tuple-element.75), channel_id=1, source_target_pairs={{12,0},{8,4},{4,8},{0,12},{28,16},{24,20},{20,24},{16,28},{13,1},{... | collective-permute-start | bytes 36872 | tf_op jit(solution)/shard_map/ppermute | solution.py:385
  23.9 7.7 %collective-permute-start.30 = (bf16[48,128]{1,0:T(8,128)(2,1)S(1)}, bf16[48,128]{1,0:T(8,128)(2,1)S(1)}, u32[]{:S(2)}, u32[]{:S(2)}) collective-permute-start(bf16[48,128]{1,0:T(8,128)(2,1)S(1)} %get-tuple-element.76), channel_id=1, source_target_pairs={{16,0},{20,4},{24,8},{28,12},{0,16},{4,20},{8,24},{12,28},{17,1},{... | collective-permute-start | bytes 36872 | tf_op jit(solution)/shard_map/ppermute | solution.py:385
  24.3 7.2 %collective-permute-start.31 = (bf16[48,128]{1,0:T(8,128)(2,1)S(1)}, bf16[48,128]{1,0:T(8,128)(2,1)S(1)}, u32[]{:S(2)}, u32[]{:S(2)}) collective-permute-start(bf16[48,128]{1,0:T(8,128)(2,1)S(1)} %get-tuple-element.77), channel_id=1, source_target_pairs={{20,0},{16,4},{28,8},{24,12},{4,16},{0,20},{12,24},{8,28},{21,1},{... | collective-permute-start | bytes 36872 | tf_op jit(solution)/shard_map/ppermute | solution.py:385
  26.6 5.5 %collective-permute-start.32 = (bf16[48,128]{1,0:T(8,128)(2,1)S(1)}, bf16[48,128]{1,0:T(8,128)(2,1)S(1)}, u32[]{:S(2)}, u32[]{:S(2)}) collective-permute-start(bf16[48,128]{1,0:T(8,128)(2,1)S(1)} %get-tuple-element.78), channel_id=1, source_target_pairs={{24,0},{28,4},{16,8},{20,12},{8,16},{12,20},{0,24},{4,28},{25,1},{... | collective-permute-start | bytes 36872 | tf_op jit(solution)/shard_map/ppermute | solution.py:385
  27.8 6.4 %collective-permute-start.33 = (bf16[48,128]{1,0:T(8,128)(2,1)S(1)}, bf16[48,128]{1,0:T(8,128)(2,1)S(1)}, u32[]{:S(2)}, u32[]{:S(2)}) collective-permute-start(bf16[48,128]{1,0:T(8,128)(2,1)S(1)} %get-tuple-element.79), channel_id=1, source_target_pairs={{28,0},{24,4},{20,8},{16,12},{12,16},{8,20},{4,24},{0,28},{29,1},{... | collective-permute-start | bytes 36872 | tf_op jit(solution)/shard_map/ppermute | solution.py:385
  35.9 3.8 %collective-permute-start.36 = (s16[144,128]{1,0:T(8,128)(2,1)S(1)}, s16[144,128]{1,0:T(8,128)(2,1)S(1)}, u32[]{:S(2)}, u32[]{:S(2)}) collective-permute-start(s16[144,128]{1,0:T(8,128)(2,1)S(1)} %get-tuple-element.80.refs_0_), channel_id=1, source_target_pairs={{0,3},{1,2},{2,1},{3,0},{4,7},{5,6},{6,5},{7,4},{8,11},{9,10},{10,... | collective-permute-start | bytes 110600 | tf_op jit(solution)/shard_map/ppermute | solution.py:261
  36.0 4.2 %collective-permute-start.35 = (s16[144,128]{1,0:T(8,128)(2,1)S(1)}, s16[144,128]{1,0:T(8,128)(2,1)S(1)}, u32[]{:S(2)}, u32[]{:S(2)}) collective-permute-start(s16[144,128]{1,0:T(8,128)(2,1)S(1)} %get-tuple-element.80.refs_0_), channel_id=1, source_target_pairs={{0,2},{1,3},{2,0},{3,1},{4,6},{5,7},{6,4},{7,5},{8,10},{9,11},{10,... | collective-permute-start | bytes 110600 | tf_op jit(solution)/shard_map/ppermute | solution.py:261
  37.6 2.6 %collective-permute-start.34 = (s16[144,128]{1,0:T(8,128)(2,1)S(1)}, s16[144,128]{1,0:T(8,128)(2,1)S(1)}, u32[]{:S(2)}, u32[]{:S(2)}) collective-permute-start(s16[144,128]{1,0:T(8,128)(2,1)S(1)} %get-tuple-element.80.refs_0_), channel_id=1, source_target_pairs={{0,1},{1,0},{2,3},{3,2},{4,5},{5,4},{6,7},{7,6},{8,9},{9,8},{10,11... | collective-permute-start | bytes 110600 | tf_op jit(solution)/shard_map/ppermute | solution.py:261

commit v7 on v6

--- a/solution.py
+++ b/solution.py
@@ -87,7 +87,23 @@
     small = started([cols_hbm, rows_hbm, duals_hbm], [cols, rows, duals], small_sems)
     large = started([tiles_hbm.at[g] for g in groups], [tiles.at[g] for g in groups], tile_sems)
 
-    small[0].wait()
+    for copy in small:
+        copy.wait()
+    for k in range(k_tiles):
+        picked[pl.ds(k, 1), :] = duals[pl.ds(rows[k], 1), :]
+
+    def products_of(chunk):
+        large[chunk].wait()
+        for first in range(chunk * CHUNK, (chunk + 1) * CHUNK, GROUP):
+            group = pl.ds(first, GROUP)
+            block = picked[group, :].astype(bf16).astype(f32)
+            left = jnp.concatenate([one_row_of(block, m) for m in range(GROUP)], axis=1)
+            terms[group, :] = jnp.dot(
+                left, tiles[group].reshape(GROUP * TILE, TILE), preferred_element_type=f32
+            )
+
+    products_of(0)
+
     square = (k_tiles, k_tiles)
     col_across = cols[...]
     col_down = jnp.transpose(jnp.broadcast_to(col_across.astype(f32), square)).astype(i32)
@@ -112,19 +128,8 @@
         [of_owner * (place - place_low).astype(f32), of_owner * place_low.astype(f32), of_owner], axis=0
     ).astype(bf16)
 
-    for copy in small[1:]:
-        copy.wait()
-    for k in range(k_tiles):
-        picked[pl.ds(k, 1), :] = duals[pl.ds(rows[k], 1), :]
-    for g, copy in enumerate(large):
-        copy.wait()
-        for first in range(g * CHUNK, (g + 1) * CHUNK, GROUP):
-            group = pl.ds(first, GROUP)
-            block = picked[group, :].astype(bf16).astype(f32)
-            left = jnp.concatenate([one_row_of(block, m) for m in range(GROUP)], axis=1)
-            terms[group, :] = jnp.dot(
-                left, tiles[group].reshape(GROUP * TILE, TILE), preferred_element_type=f32
-            )
+    for chunk in range(1, len(large)):
+        products_of(chunk)
     whole, exponents = coded(terms[...])
 
     scaled = [to_lanes, to_lanes * jnp.concatenate([exponents] * chunks, axis=1)]
@@ -148,8 +153,7 @@
 def primal_kernel(
     payloads, primal_ref, cost_ref, lower_ref, upper_ref, kind_ref, steps_ref, next_hbm, flag_ref, *refs
 ):
-    wanted, (next_ref, extrap, in_order, sem) = refs[:-4], refs[-4:]
-    me = lax.axis_index("row")
+    wanted, next_ref, extrap, sem = refs
     n_row = payloads.shape[0]
     chunks, head_rows = rounds_of(n_row)
     blocks = primal_ref.shape[0]
@@ -185,21 +189,16 @@
         jnp.dot(where_one(across == places[:, c : c + 1]).astype(bf16), right, preferred_element_type=f32)
         for c in range(chunks)
     ]
-    in_order[...] = jnp.concatenate(sent, axis=0).astype(bf16).reshape(in_order.shape)
-    for n, target in enumerate(wanted):
-        target[...] = in_order[place_of(me, n, n_row, back=True)]
+    wanted[...] = jnp.concatenate(sent, axis=0).astype(bf16).reshape(wanted.shape)
     copy.wait()
 
 
 def product_kernel(*refs):
-    (rows_ref, slot_ref, tiles_ref, flag_ref), others_hbm, refs = refs[:4], refs[4:6], refs[6:]
-    arrived, (out_ref, *others, in_order, sems) = refs[:-5], refs[-5:]
-    me = lax.axis_index("row")
-    for n, source in enumerate(arrived):
-        in_order[place_of(me, n, len(arrived), back=False)] = source[...]
+    (rows_ref, slot_ref, tiles_ref, arrived, flag_ref), others_hbm, refs = refs[:5], refs[5:7], refs[7:]
+    out_ref, others, sems = refs[0], refs[1:3], refs[3]
     later = started(others_hbm, others, sems)
     k_tiles = tiles_ref.shape[0]
-    received = in_order[...].reshape(-1, TILE)
+    received = arrived[...].reshape(-1, TILE)
     across = iota((k_tiles, received.shape[0]), 1)
     slots = jnp.concatenate([slot_ref[...]] * (received.shape[0] // TILE), axis=1)
     block = jnp.dot(where_one(across == slots).astype(bf16), received, preferred_element_type=f32)
@@ -240,12 +239,6 @@
     updated = duals_ref[...] + steps_ref[1] * (right_ref[...] - row_sums)
     next_ref[...] = jnp.where(kind_ref[...] == 1, jnp.maximum(updated, 0.0), updated)
     flag_ref[0] = jnp.max(flags)
-
-
-def place_of(me, n, size, back):
-    if size & (size - 1) == 0:
-        return jnp.bitwise_xor(me, n)
-    return lax.rem(me + (size - n if back else n), size)
 
 
 def partners(axis):
@@ -346,19 +339,18 @@
         compiler_params=params,
         name="transpose_product",
     )(in_hbm(rows), in_hbm(cols.reshape(1, k_tiles)), *own)
-    primal_next, flag, *wanted = pl.pallas_call(
+    primal_next, flag, wanted = pl.pallas_call(
         primal_kernel,
         out_shape=(
             jax.ShapeDtypeStruct((col_blocks, TILE), f32),
             jax.ShapeDtypeStruct((8, TILE), f32),
-            *[jax.ShapeDtypeStruct((SLOTS, TILE), bf16)] * n_row,
+            jax.ShapeDtypeStruct((n_row, SLOTS, TILE), bf16),
         ),
         in_specs=[VMEM] * 6 + [SMEM],
-        out_specs=(HBM, *[VMEM] * (n_row + 1)),
+        out_specs=(HBM, VMEM, VMEM),
         scratch_shapes=[
             pltpu.VMEM((col_blocks, TILE), f32),
             pltpu.VMEM((padded, TILE), f32),
-            pltpu.VMEM((n_row, SLOTS, TILE), bf16),
             pltpu.SemaphoreType.DMA,
         ],
         compiler_params=params,
@@ -370,20 +362,12 @@
             jax.ShapeDtypeStruct((k_tiles + HEAD, TILE), i16),
             *[shape_of(a) for a in dual_side],
         ),
-        in_specs=[VMEM] * 4 + [HBM] * 2 + [VMEM] * n_row,
+        in_specs=[VMEM] * 5 + [HBM] * 2,
         out_specs=(VMEM,) * 3,
-        scratch_shapes=[pltpu.VMEM((n_row, SLOTS, TILE), bf16), pltpu.SemaphoreType.DMA((2,))],
+        scratch_shapes=[pltpu.SemaphoreType.DMA((2,))],
         compiler_params=params,
         name="product",
-    )(
-        rows.reshape(1, k_tiles),
-        slots,
-        tiles_kept,
-        flag,
-        *dual_side,
-        wanted[0],
-        *[lax.ppermute(w, "row", back) for w, (_, back) in zip(wanted[1:], partners("row"))],
-    )
+    )(rows.reshape(1, k_tiles), slots, tiles_kept, lax.all_to_all(wanted, "row", 0, 0), flag, *dual_side)
     dual_next, too_many = pl.pallas_call(
         functools.partial(dual_kernel, n_col),
         out_shape=(jax.ShapeDtypeStruct((row_blocks, TILE), f32), jax.ShapeDtypeStruct((1,), i32)),

time: 42.6 us -> 38.3 us (0.90)
  starting transfers between devices: 13.1 us -> 1.92 us
  blocking collectives: 14.3 us -> 23.8 us
  waiting for transfers between devices: 4.94 us -> 2.31 us
    ppermute x7 -> x0, starting transfers between devices: 11.2 us -> none  [local(): lax.ppermute(w, 'row', back)]
    all_to_all x0 -> x1, blocking collectives: none -> 9.51 us  [local(): lax.all_to_all(wanted, 'row', 0, 0)]
    ppermute x7 -> x0, waiting for transfers between devices: 2.63 us -> none  [local(): lax.ppermute(w, 'row', back)]
  transfers between devices with their start and end apart: 10 -> 3, of which waited for: 4 -> 2; matrix products, arithmetic and copies ran while one was open for 0% -> 0% of each run, Pallas kernels for 0% -> 0%
where the time goes in v7:
time: 38.3 us; the launch traced here: 38.1 us
  blocking collectives  23.8 us (62%)
  Pallas kernels  8.54 us (22%)
  waiting for transfers between devices  2.31 us (6%)
  starting transfers between devices  1.92 us (5%)
  between operations  1.46 us (4%)
    all_to_all x1, blocking collectives, local(): lax.all_to_all(col_terms, 'row', 0, 0)  14.3 us
    all_to_all x1, blocking collectives, local(): lax.all_to_all(wanted, 'row', 0, 0)  9.51 us
    pallas_call x1, Pallas kernels, local(): pl.pallas_call(functools.partial(transpose_product_kernel, col_blocks), o...  3.52 us
    ppermute x3, waiting for transfers between devices, gathered_along(): lax.ppermute(array, axis, there)  2.31 us
    ppermute x3, starting transfers between devices, gathered_along(): lax.ppermute(array, axis, there)  1.92 us
    pallas_call x1, Pallas kernels, local(): pl.pallas_call(primal_kernel, out_shape=(jax.ShapeDtypeStruct((col_blocks...  1.74 us
    pallas_call x1, Pallas kernels, local(): pl.pallas_call(product_kernel, out_shape=(jax.ShapeDtypeStruct((k_tiles +...  1.71 us
    pallas_call x1, Pallas kernels, local(): pl.pallas_call(functools.partial(dual_kernel, n_col), out_shape=(jax.Shap...  1.57 us
  transfers between devices with their start and end apart: 3, of which 2 were waited for; matrix products, arithmetic and copies ran while one was open for 0% of the time, Pallas kernels for 0%

profile of v7, /device:TPU:0, one launch (start us, length us, event | category | flops | bytes accessed | tf_op | source)
XLA Modules:
  0.0 38.1 jit_solution(12806283563435700730)
XLA Ops:
  0.6 0.0 copy-start.10
  0.6 0.0 copy-start.9
  0.7 0.0 copy-start.3
  0.7 0.0 copy-start.4
  0.7 0.0 copy-start.5
  0.7 0.0 copy-start.6
  0.7 0.0 copy-start.7
  0.7 3.5 %transpose_product.1 = (s16[8,48,128]{2,1,0:T(8,128)(2,1)S(1)}, s32[128,128]{1,0:T(8,128)S(1)}, f32[496,128]{1,0:T(8,128)S(1)}, bf16[128,128,128]{2,1,0:T(8,128)(2,1)S(1)}) custom-call(s32[128]{0:T(128)} %bitcast.90, s32[1,128]{1,0:T(1,128)} %bitcast.93, f32[496,128]{1,0:T(8,128)} %bitcast.67, bf16[128,128,128]{2,1,0:T(8,128)(2,1)} %bitcast.65), custom_call_target="tpu_custom_call" | custom-call | tf_op jit(solution)/shard_map/transpose_product/pallas_call | solution.py:322
  4.2 0.0 copy-start
  4.2 0.0 copy-start.1
  4.3 0.0 copy-start.2
  4.3 0.0 copy-start.11
  4.3 14.3 %all_to_all.10.payloads = s16[8,48,128]{2,1,0:T(8,128)(2,1)S(1)} all-to-all(s16[8,48,128]{2,1,0:T(8,128)(2,1)S(1)} %get-tuple-element.63), channel_id=1, replica_groups=mesh['row'=8,'col'=4] {'row'}, dimensions={0} | all-to-all | bytes 196608 | tf_op jit(solution)/shard_map/all_to_all | solution.py:358
  18.6 0.0 copy-done.9
  18.6 0.0 copy-done.3
  18.6 0.0 copy-done.4
  18.6 0.0 copy-done.5
  18.6 0.0 copy-done.6
  18.6 0.0 copy-done.7
  18.7 1.7 %primal_step.1 = (f32[488,128]{1,0:T(8,128)}, f32[8,128]{1,0:T(8,128)S(1)}, bf16[8,48,128]{2,1,0:T(8,128)(2,1)S(1)}) custom-call(s16[8,48,128]{2,1,0:T(8,128)(2,1)S(1)} %all_to_all.10.payloads, f32[488,128]{1,0:T(8,128)S(1)} %bitcast.70, f32[488,128]{1,0:T(8,128)S(1)} %bitcast.85, f32[488,128]{1,0:T(8,128)S(1)} %bitcast.86, f32[488,128]{1,0:T(8,128)S(1)} %bitcast.87, ...), custom_call_target="tpu_custom_call" | custom-call | tf_op jit(solution)/shard_map/primal_step/pallas_call | solution.py:342
  20.4 9.5 %all_to_all.11.refs_3_ = bf16[8,48,128]{2,1,0:T(8,128)(2,1)S(1)} all-to-all(bf16[8,48,128]{2,1,0:T(8,128)(2,1)S(1)} %get-tuple-element.64), channel_id=1, replica_groups=mesh['row'=8,'col'=4] {'row'}, dimensions={0} | all-to-all | bytes 196608 | tf_op jit(solution)/shard_map/all_to_all | solution.py:370
  29.9 0.0 copy-done.10
  29.9 1.7 %product.1 = (s16[144,128]{1,0:T(8,128)(2,1)S(1)}, f32[496,128]{1,0:T(8,128)S(1)}, s32[496,128]{1,0:T(8,128)S(1)}) custom-call(s32[1,128]{1,0:T(1,128)S(1)} %bitcast.91, s32[128,128]{1,0:T(8,128)S(1)} %get-tuple-element.61.refs_1_, bf16[128,128,128]{2,1,0:T(8,128)(2,1)S(1)} %get-tuple-element.62.refs_2_, bf16[8,48,128]{2,1,0:T(8,128)(2,1)S(1)} %all_to_all.11.refs_3_, ...), custom_call_target="tpu_custom_call" | custom-call | tf_op jit(solution)/shard_map/product/pallas_call | solution.py:359
  31.6 0.1 collective-permute-start.29
  31.7 1.6 %collective-permute-start.28 = (s16[144,128]{1,0:T(8,128)(2,1)S(1)}, s16[144,128]{1,0:T(8,128)(2,1)S(1)}, u32[]{:S(2)}, u32[]{:S(2)}) collective-permute-start(s16[144,128]{1,0:T(8,128)(2,1)S(1)} %get-tuple-element.66.refs_0_), channel_id=1, source_target_pairs={{0,2},{1,3},{2,0},{3,1},{4,6},{5,7},{6,4},{7,5},{8,10},{9,11},{10,... | collective-permute-start | bytes 110600 | tf_op jit(solution)/shard_map/ppermute | solution.py:254
  33.3 0.3 collective-permute-start.27
  33.6 1.9 %collective-permute-done.29.refs_3_ = s16[144,128]{1,0:T(8,128)(2,1)S(1)} collective-permute-done((s16[144,128]{1,0:T(8,128)(2,1)S(1)}, s16[144,128]{1,0:T(8,128)(2,1)S(1)}, u32[]{:S(2)}, u32[]{:S(2)}) %collective-permute-start.29) | collective-permute-done | bytes 36896 | tf_op jit(solution)/shard_map/ppermute | solution.py:254
  35.4 0.4 %collective-permute-done.28.refs_2_ = s16[144,128]{1,0:T(8,128)(2,1)S(1)} collective-permute-done((s16[144,128]{1,0:T(8,128)(2,1)S(1)}, s16[144,128]{1,0:T(8,128)(2,1)S(1)}, u32[]{:S(2)}, u32[]{:S(2)}) %collective-permute-start.28) | collective-permute-done | bytes 36896 | tf_op jit(solution)/shard_map/ppermute | solution.py:254
  35.9 0.0 collective-permute-done.27.refs_1_
  35.9 1.6 %dual_step.1 = (f32[496,128]{1,0:T(8,128)}, s32[1]{0:T(128)}) custom-call(s16[144,128]{1,0:T(8,128)(2,1)S(1)} %get-tuple-element.66.refs_0_, s16[144,128]{1,0:T(8,128)(2,1)S(1)} %collective-permute-done.27.refs_1_, s16[144,128]{1,0:T(8,128)(2,1)S(1)} %collective-permute-done.28.refs_2_, s16[144,128]{1,0:T(8,128)(2,1)S(1)} %collective-permute-done.29.refs_3_, ...), custom_call_target="tpu_custom_call" | custom-call | tf_op jit(solution)/shard_map/dual_step/pallas_call | solution.py:371
  38.1 0.0 copy-done
  38.1 0.0 copy-done.1
  38.1 0.0 copy-done.2
  38.1 0.0 copy-done.11
  (1 shorter events, 0.0 us)
Async XLA Ops:
  0.6 29.3 %copy-start.10 = (s32[1,1,128]{2,1,0:T(1,128)S(1)}, s32[1,1,128]{2,1,0:T(1,128)}, u32[]{:S(2)}) copy-start(s32[1,1,128]{2,1,0:T(1,128)} %param.15) | copy-start | bytes 1540
  0.6 18.0 %copy-start.9 = (f32[2]{0:T(128)S(1)}, f32[2]{0:T(128)}, u32[]{:S(2)}) copy-start(f32[2]{0:T(128)} %refs_7_.1) | copy-start | bytes 28
  0.7 18.0 %copy-start.3 = (f32[62464]{0:T(1024)S(1)}, f32[62464]{0:T(1024)}, u32[]{:S(2)}) copy-start(f32[62464]{0:T(1024)} %param.17) | copy-start | bytes 749572
  0.7 18.0 %copy-start.4 = (f32[62464]{0:T(1024)S(1)}, f32[62464]{0:T(1024)}, u32[]{:S(2)}) copy-start(f32[62464]{0:T(1024)} %param.19) | copy-start | bytes 749572
  0.7 18.0 %copy-start.5 = (f32[62464]{0:T(1024)S(1)}, f32[62464]{0:T(1024)}, u32[]{:S(2)}) copy-start(f32[62464]{0:T(1024)} %param.20) | copy-start | bytes 749572
  0.7 18.0 %copy-start.6 = (f32[62464]{0:T(1024)S(1)}, f32[62464]{0:T(1024)}, u32[]{:S(2)}) copy-start(f32[62464]{0:T(1024)} %param.21) | copy-start | bytes 749572
  0.7 18.0 %copy-start.7 = (s32[62464]{0:T(1024)S(1)}, s32[62464]{0:T(1024)}, u32[]{:S(2)}) copy-start(s32[62464]{0:T(1024)} %param.22) | copy-start | bytes 749572
  4.2 33.9 %copy-start = (f32[63488]{0:T(1024)S(1)}, f32[63488]{0:T(1024)}, u32[]{:S(2)}) copy-start(f32[63488]{0:T(1024)} %param.18) | copy-start | bytes 761860
  4.2 33.9 %copy-start.1 = (f32[63488]{0:T(1024)S(1)}, f32[63488]{0:T(1024)}, u32[]{:S(2)}) copy-start(f32[63488]{0:T(1024)} %param.23) | copy-start | bytes 761860
  4.3 33.9 %copy-start.2 = (s32[63488]{0:T(1024)S(1)}, s32[63488]{0:T(1024)}, u32[]{:S(2)}) copy-start(s32[63488]{0:T(1024)} %param.24) | copy-start | bytes 761860
  4.3 33.9 %copy-start.11 = (s32[1,1,128]{2,1,0:T(1,128)S(1)}, s32[1,1,128]{2,1,0:T(1,128)}, u32[]{:S(2)}) copy-start(s32[1,1,128]{2,1,0:T(1,128)} %param.16) | copy-start | bytes 1540
  31.6 3.8 %collective-permute-start.29 = (s16[144,128]{1,0:T(8,128)(2,1)S(1)}, s16[144,128]{1,0:T(8,128)(2,1)S(1)}, u32[]{:S(2)}, u32[]{:S(2)}) collective-permute-start(s16[144,128]{1,0:T(8,128)(2,1)S(1)} %get-tuple-element.66.refs_0_), channel_id=1, source_target_pairs={{0,3},{1,2},{2,1},{3,0},{4,7},{5,6},{6,5},{7,4},{8,11},{9,10},{10,... | collective-permute-start | bytes 110600 | tf_op jit(solution)/shard_map/ppermute | solution.py:254
  31.7 4.2 %collective-permute-start.28 = (s16[144,128]{1,0:T(8,128)(2,1)S(1)}, s16[144,128]{1,0:T(8,128)(2,1)S(1)}, u32[]{:S(2)}, u32[]{:S(2)}) collective-permute-start(s16[144,128]{1,0:T(8,128)(2,1)S(1)} %get-tuple-element.66.refs_0_), channel_id=1, source_target_pairs={{0,2},{1,3},{2,0},{3,1},{4,6},{5,7},{6,4},{7,5},{8,10},{9,11},{10,... | collective-permute-start | bytes 110600 | tf_op jit(solution)/shard_map/ppermute | solution.py:254
  33.3 2.6 %collective-permute-start.27 = (s16[144,128]{1,0:T(8,128)(2,1)S(1)}, s16[144,128]{1,0:T(8,128)(2,1)S(1)}, u32[]{:S(2)}, u32[]{:S(2)}) collective-permute-start(s16[144,128]{1,0:T(8,128)(2,1)S(1)} %get-tuple-element.66.refs_0_), channel_id=1, source_target_pairs={{0,1},{1,0},{2,3},{3,2},{4,5},{5,4},{6,7},{7,6},{8,9},{9,8},{10,11... | collective-permute-start | bytes 110600 | tf_op jit(solution)/shard_map/ppermute | solution.py:254

commit v8 on v7

--- a/solution.py
+++ b/solution.py
@@ -8,10 +8,11 @@
 
 TILE = 128
 GROUP = 16
-CHUNK = 32
-SLOTS = 48
+CHUNK = 16
+SLOTS = 40
 HEAD = 16
 BITS = 14
+LEAST = -60
 
 f32 = jnp.float32
 bf16 = jnp.bfloat16
@@ -35,13 +36,13 @@
 
 
 def rounds_of(n_row):
-    chunks = n_row * SLOTS // TILE
-    return chunks, -(-(2 * chunks + 1) // 8) * 8
+    chunks = -(-n_row * SLOTS // TILE)
+    return chunks, chunks + 1
 
 
 def coded(values):
     largest = jnp.maximum(jnp.max(jnp.abs(values), axis=1, keepdims=True), 1e-30)
-    exponent = jnp.ceil(jnp.log2(largest))
+    exponent = jnp.maximum(jnp.ceil(jnp.log2(largest)), LEAST)
     whole = jnp.floor(values * jnp.exp2(BITS - exponent) + 0.5).astype(i32)
     return whole, jnp.broadcast_to(exponent, values.shape)
 
@@ -64,6 +65,11 @@
 
 def scaled_mask(down, places, exponents):
     return jnp.where(down == places, jnp.exp2(exponents.astype(f32) - BITS), 0.0)
+
+
+def padded_rows(blocks, rows):
+    missing = rows - sum(b.shape[0] for b in blocks)
+    return jnp.concatenate(blocks + [jnp.zeros((missing, TILE), blocks[0].dtype)] * (missing > 0), axis=0)
 
 
 def started(sources, targets, sems):
@@ -120,7 +126,8 @@
     too_many = where_one(jnp.max(rank_across, axis=1, keepdims=True) >= most)
     to_slots = where_one(iota((n_row * SLOTS, k_tiles), 0) == slot_across)
     here = jnp.where(rank_down < most, lax.axis_index("row") * SLOTS + head_rows + rank_down, -1)
-    to_lanes = where_one(iota((k_tiles, n_row * SLOTS), 1) == here)
+    width = chunks * TILE
+    to_lanes = where_one(iota((k_tiles, width), 1) == here)
     of_owner = where_one(iota((n_row, k_tiles), 0) == owner_across)
     place = col_across - owner_across * owned + 1
     place_low = jnp.bitwise_and(place, 255)
@@ -134,20 +141,22 @@
 
     scaled = [to_lanes, to_lanes * jnp.concatenate([exponents] * chunks, axis=1)]
     heads = jnp.dot(head_left, jnp.concatenate(scaled, axis=1).astype(bf16), preferred_element_type=f32)
-    width = n_row * SLOTS
     places = heads[:n_row, :width] + heads[n_row : 2 * n_row, :width]
-    scales = heads[2 * n_row :, width:]
+    packed = heads[2 * n_row :, width:] * place_range(owned) + places
     both = jnp.dot(to_slots.astype(bf16), two_parts(whole), preferred_element_type=f32)
     body = both[:, :TILE] + both[:, TILE:]
-    line = iota((head_rows, TILE), 0)
+    top = -(-head_rows // 8) * 8
+    line = iota((top, TILE), 0)
     for o in range(n_row):
-        head = jnp.where(line == 2 * chunks, too_many, 0.0)
+        head = jnp.where(line == chunks, too_many, body[o * SLOTS : o * SLOTS + top])
         for c in range(chunks):
-            lanes = slice(c * TILE, (c + 1) * TILE)
-            head = jnp.where(line == c, places[o : o + 1, lanes], head)
-            head = jnp.where(line == chunks + c, scales[o : o + 1, lanes], head)
-        rows_of = body[o * SLOTS + head_rows : (o + 1) * SLOTS]
+            head = jnp.where(line == c, packed[o : o + 1, c * TILE : (c + 1) * TILE], head)
+        rows_of = body[o * SLOTS + top : (o + 1) * SLOTS]
         out_ref[o] = jnp.concatenate([head, rows_of], axis=0).astype(i32).astype(i16)
+
+
+def place_range(owned):
+    return 1 << owned.bit_length()
 
 
 def primal_kernel(
@@ -158,16 +167,17 @@
     chunks, head_rows = rounds_of(n_row)
     blocks = primal_ref.shape[0]
     padded = extrap.shape[0]
-    head = jnp.zeros((head_rows, TILE), f32)
-    for s in range(n_row):
-        head += payloads[s].astype(i32)[:head_rows].astype(f32)
-    flag_ref[...] = jnp.broadcast_to(head[2 * chunks : 2 * chunks + 1], flag_ref.shape)
-    whole = payloads[...].reshape(n_row * SLOTS, TILE).astype(i32)
+    wholes = [payloads[s].astype(i32) for s in range(n_row)]
+    top = -(-head_rows // 8) * 8
+    head = sum(w[:top] for w in wholes)
+    flag_ref[...] = jnp.broadcast_to(head[chunks:head_rows], flag_ref.shape)
+    whole = padded_rows(wholes, chunks * TILE)
     down = iota((blocks, TILE), 0) + 1
-    head_whole = head.astype(i32)
+    places = jnp.bitwise_and(head, place_range(blocks) - 1)
+    scales = lax.shift_right_arithmetic(head, blocks.bit_length())
     masks, wholes = [], []
     for c in range(chunks):
-        masks.append(scaled_mask(down, head_whole[c : c + 1], head_whole[chunks + c : chunks + c + 1]))
+        masks.append(scaled_mask(down, places[c : c + 1], scales[c : c + 1]))
         wholes.append(whole[c * TILE : (c + 1) * TILE])
     col_sums = picked_sums(masks, wholes)
     primal = primal_ref[...]
@@ -184,12 +194,14 @@
     extrap[pl.ds(0, blocks), :] = 2.0 * moved - primal
     right = extrap[...].astype(bf16)
     across = iota((TILE, padded), 1) + 1
-    places = jnp.transpose(head).astype(i32)
+    places = jnp.transpose(places.astype(f32)).astype(i32)
     sent = [
         jnp.dot(where_one(across == places[:, c : c + 1]).astype(bf16), right, preferred_element_type=f32)
         for c in range(chunks)
     ]
-    wanted[...] = jnp.concatenate(sent, axis=0).astype(bf16).reshape(wanted.shape)
+    sent = jnp.concatenate(sent, axis=0)
+    for s in range(n_row):
+        wanted[s] = sent[s * SLOTS : (s + 1) * SLOTS].astype(bf16)
     copy.wait()
 
 
@@ -198,7 +210,9 @@
     out_ref, others, sems = refs[0], refs[1:3], refs[3]
     later = started(others_hbm, others, sems)
     k_tiles = tiles_ref.shape[0]
-    received = arrived[...].reshape(-1, TILE)
+    chunks, _ = rounds_of(arrived.shape[0])
+    blocks = [arrived[s].astype(f32) for s in range(arrived.shape[0])]
+    received = padded_rows(blocks, chunks * TILE).astype(bf16)
     across = iota((k_tiles, received.shape[0]), 1)
     slots = jnp.concatenate([slot_ref[...]] * (received.shape[0] // TILE), axis=1)
     block = jnp.dot(where_one(across == slots).astype(bf16), received, preferred_element_type=f32)
@@ -218,7 +232,7 @@
     out_ref[pl.ds(0, k_tiles), :] = whole.astype(i16)
     line = iota((HEAD, TILE), 0)
     head = jnp.where(line == 0, rows_ref[...], jnp.transpose(exponents)[0:HEAD, :].astype(i32))
-    head = jnp.where(line == 2, flag_ref[0:1, :].astype(i32), head)
+    head = jnp.where(line == 2, flag_ref[0:1, :], head)
     out_ref[pl.ds(k_tiles, HEAD), :] = head.astype(i16)
     for copy in later:
         copy.wait()
@@ -343,7 +357,7 @@
         primal_kernel,
         out_shape=(
             jax.ShapeDtypeStruct((col_blocks, TILE), f32),
-            jax.ShapeDtypeStruct((8, TILE), f32),
+            jax.ShapeDtypeStruct((8, TILE), i32),
             jax.ShapeDtypeStruct((n_row, SLOTS, TILE), bf16),
         ),
         in_specs=[VMEM] * 6 + [SMEM],

time: 38.3 us -> 38.8 us (1.013)
  Pallas kernels: 8.54 us -> 9.2 us
    pallas_call x1, Pallas kernels: 3.52 us -> 4.23 us  [local(): pl.pallas_call(functools.partial(transpose_product_kernel, col_blocks), o...]
where the time goes in v8:
time: 38.8 us; the launch traced here: 38.6 us
  blocking collectives  23.6 us (61%)
  Pallas kernels  9.2 us (24%)
  waiting for transfers between devices  2.31 us (6%)
  starting transfers between devices  1.92 us (5%)
  between operations  1.46 us (4%)
    all_to_all x1, blocking collectives, local(): lax.all_to_all(col_terms, 'row', 0, 0)  14.2 us
    all_to_all x1, blocking collectives, local(): lax.all_to_all(wanted, 'row', 0, 0)  9.4 us
    pallas_call x1, Pallas kernels, local(): pl.pallas_call(functools.partial(transpose_product_kernel, col_blocks), o...  4.23 us
    ppermute x3, waiting for transfers between devices, gathered_along(): lax.ppermute(array, axis, there)  2.31 us
    ppermute x3, starting transfers between devices, gathered_along(): lax.ppermute(array, axis, there)  1.92 us
    pallas_call x1, Pallas kernels, local(): pl.pallas_call(product_kernel, out_shape=(jax.ShapeDtypeStruct((k_tiles +...  1.71 us
    pallas_call x1, Pallas kernels, local(): pl.pallas_call(primal_kernel, out_shape=(jax.ShapeDtypeStruct((col_blocks...  1.69 us
    pallas_call x1, Pallas kernels, local(): pl.pallas_call(functools.partial(dual_kernel, n_col), out_shape=(jax.Shap...  1.57 us
  transfers between devices with their start and end apart: 3, of which 2 were waited for; matrix products, arithmetic and copies ran while one was open for 0% of the time, Pallas kernels for 0%

profile of v8, /device:TPU:0, one launch (start us, length us, event | category | flops | bytes accessed | tf_op | source)
XLA Modules:
  0.0 38.6 jit_solution(2180619409680084492)
XLA Ops:
  0.6 0.0 copy-start.10
  0.6 0.0 copy-start.9
  0.7 0.0 copy-start.3
  0.7 0.0 copy-start.4
  0.7 0.0 copy-start.5
  0.7 0.0 copy-start.6
  0.7 0.0 copy-start.7
  0.7 4.2 %transpose_product.1 = (s16[8,40,128]{2,1,0:T(8,128)(2,1)S(1)}, s32[128,128]{1,0:T(8,128)S(1)}, f32[496,128]{1,0:T(8,128)S(1)}, bf16[128,128,128]{2,1,0:T(8,128)(2,1)S(1)}) custom-call(s32[128]{0:T(128)} %bitcast.90, s32[1,128]{1,0:T(1,128)} %bitcast.93, f32[496,128]{1,0:T(8,128)} %bitcast.67, bf16[128,128,128]{2,1,0:T(8,128)(2,1)} %bitcast.65), custom_call_target="tpu_custom_call" | custom-call | tf_op jit(solution)/shard_map/transpose_product/pallas_call | solution.py:336
  4.9 0.0 copy-start
  4.9 0.0 copy-start.1
  5.0 0.0 copy-start.2
  5.0 0.0 copy-start.11
  5.0 14.2 %all_to_all.10.payloads = s16[8,40,128]{2,1,0:T(8,128)(2,1)S(1)} all-to-all(s16[8,40,128]{2,1,0:T(8,128)(2,1)S(1)} %get-tuple-element.63), channel_id=1, replica_groups=mesh['row'=8,'col'=4] {'row'}, dimensions={0} | all-to-all | bytes 163840 | tf_op jit(solution)/shard_map/all_to_all | solution.py:372
  19.2 0.0 copy-done.9
  19.2 0.0 copy-done.3
  19.2 0.0 copy-done.4
  19.2 0.0 copy-done.5
  19.2 0.0 copy-done.6
  19.2 0.0 copy-done.7
  19.3 1.7 %primal_step.1 = (f32[488,128]{1,0:T(8,128)}, s32[8,128]{1,0:T(8,128)S(1)}, bf16[8,40,128]{2,1,0:T(8,128)(2,1)S(1)}) custom-call(s16[8,40,128]{2,1,0:T(8,128)(2,1)S(1)} %all_to_all.10.payloads, f32[488,128]{1,0:T(8,128)S(1)} %bitcast.70, f32[488,128]{1,0:T(8,128)S(1)} %bitcast.85, f32[488,128]{1,0:T(8,128)S(1)} %bitcast.86, f32[488,128]{1,0:T(8,128)S(1)} %bitcast.87, ...), custom_call_target="tpu_custom_call" | custom-call | tf_op jit(solution)/shard_map/primal_step/pallas_call | solution.py:356
  20.9 9.4 %all_to_all.11.refs_3_ = bf16[8,40,128]{2,1,0:T(8,128)(2,1)S(1)} all-to-all(bf16[8,40,128]{2,1,0:T(8,128)(2,1)S(1)} %get-tuple-element.64), channel_id=1, replica_groups=mesh['row'=8,'col'=4] {'row'}, dimensions={0} | all-to-all | bytes 163840 | tf_op jit(solution)/shard_map/all_to_all | solution.py:384
  30.3 0.0 copy-done.10
  30.4 1.7 %product.1 = (s16[144,128]{1,0:T(8,128)(2,1)S(1)}, f32[496,128]{1,0:T(8,128)S(1)}, s32[496,128]{1,0:T(8,128)S(1)}) custom-call(s32[1,128]{1,0:T(1,128)S(1)} %bitcast.91, s32[128,128]{1,0:T(8,128)S(1)} %get-tuple-element.61.refs_1_, bf16[128,128,128]{2,1,0:T(8,128)(2,1)S(1)} %get-tuple-element.62.refs_2_, bf16[8,40,128]{2,1,0:T(8,128)(2,1)S(1)} %all_to_all.11.refs_3_, ...), custom_call_target="tpu_custom_call" | custom-call | tf_op jit(solution)/shard_map/product/pallas_call | solution.py:373
  32.1 0.1 collective-permute-start.29
  32.1 1.6 %collective-permute-start.28 = (s16[144,128]{1,0:T(8,128)(2,1)S(1)}, s16[144,128]{1,0:T(8,128)(2,1)S(1)}, u32[]{:S(2)}, u32[]{:S(2)}) collective-permute-start(s16[144,128]{1,0:T(8,128)(2,1)S(1)} %get-tuple-element.66.refs_0_), channel_id=1, source_target_pairs={{0,2},{1,3},{2,0},{3,1},{4,6},{5,7},{6,4},{7,5},{8,10},{9,11},{10,... | collective-permute-start | bytes 110600 | tf_op jit(solution)/shard_map/ppermute | solution.py:268
  33.7 0.3 collective-permute-start.27
  34.0 1.9 %collective-permute-done.29.refs_3_ = s16[144,128]{1,0:T(8,128)(2,1)S(1)} collective-permute-done((s16[144,128]{1,0:T(8,128)(2,1)S(1)}, s16[144,128]{1,0:T(8,128)(2,1)S(1)}, u32[]{:S(2)}, u32[]{:S(2)}) %collective-permute-start.29) | collective-permute-done | bytes 36896 | tf_op jit(solution)/shard_map/ppermute | solution.py:268
  35.9 0.4 %collective-permute-done.28.refs_2_ = s16[144,128]{1,0:T(8,128)(2,1)S(1)} collective-permute-done((s16[144,128]{1,0:T(8,128)(2,1)S(1)}, s16[144,128]{1,0:T(8,128)(2,1)S(1)}, u32[]{:S(2)}, u32[]{:S(2)}) %collective-permute-start.28) | collective-permute-done | bytes 36896 | tf_op jit(solution)/shard_map/ppermute | solution.py:268
  36.3 0.0 collective-permute-done.27.refs_1_
  36.3 1.6 %dual_step.1 = (f32[496,128]{1,0:T(8,128)}, s32[1]{0:T(128)}) custom-call(s16[144,128]{1,0:T(8,128)(2,1)S(1)} %get-tuple-element.66.refs_0_, s16[144,128]{1,0:T(8,128)(2,1)S(1)} %collective-permute-done.27.refs_1_, s16[144,128]{1,0:T(8,128)(2,1)S(1)} %collective-permute-done.28.refs_2_, s16[144,128]{1,0:T(8,128)(2,1)S(1)} %collective-permute-done.29.refs_3_, ...), custom_call_target="tpu_custom_call" | custom-call | tf_op jit(solution)/shard_map/dual_step/pallas_call | solution.py:385
  38.5 0.0 copy-done
  38.5 0.0 copy-done.1
  38.5 0.0 copy-done.2
  38.6 0.0 copy-done.11
  (1 shorter events, 0.0 us)
Async XLA Ops:
  0.6 29.7 %copy-start.10 = (s32[1,1,128]{2,1,0:T(1,128)S(1)}, s32[1,1,128]{2,1,0:T(1,128)}, u32[]{:S(2)}) copy-start(s32[1,1,128]{2,1,0:T(1,128)} %param.15) | copy-start | bytes 1540
  0.6 18.6 %copy-start.9 = (f32[2]{0:T(128)S(1)}, f32[2]{0:T(128)}, u32[]{:S(2)}) copy-start(f32[2]{0:T(128)} %refs_7_.1) | copy-start | bytes 28
  0.7 18.6 %copy-start.3 = (f32[62464]{0:T(1024)S(1)}, f32[62464]{0:T(1024)}, u32[]{:S(2)}) copy-start(f32[62464]{0:T(1024)} %param.17) | copy-start | bytes 749572
  0.7 18.6 %copy-start.4 = (f32[62464]{0:T(1024)S(1)}, f32[62464]{0:T(1024)}, u32[]{:S(2)}) copy-start(f32[62464]{0:T(1024)} %param.19) | copy-start | bytes 749572
  0.7 18.6 %copy-start.5 = (f32[62464]{0:T(1024)S(1)}, f32[62464]{0:T(1024)}, u32[]{:S(2)}) copy-start(f32[62464]{0:T(1024)} %param.20) | copy-start | bytes 749572
  0.7 18.6 %copy-start.6 = (f32[62464]{0:T(1024)S(1)}, f32[62464]{0:T(1024)}, u32[]{:S(2)}) copy-start(f32[62464]{0:T(1024)} %param.21) | copy-start | bytes 749572
  0.7 18.6 %copy-start.7 = (s32[62464]{0:T(1024)S(1)}, s32[62464]{0:T(1024)}, u32[]{:S(2)}) copy-start(s32[62464]{0:T(1024)} %param.22) | copy-start | bytes 749572
  4.9 33.6 %copy-start = (f32[63488]{0:T(1024)S(1)}, f32[63488]{0:T(1024)}, u32[]{:S(2)}) copy-start(f32[63488]{0:T(1024)} %param.18) | copy-start | bytes 761860
  4.9 33.6 %copy-start.1 = (f32[63488]{0:T(1024)S(1)}, f32[63488]{0:T(1024)}, u32[]{:S(2)}) copy-start(f32[63488]{0:T(1024)} %param.23) | copy-start | bytes 761860
  5.0 33.6 %copy-start.2 = (s32[63488]{0:T(1024)S(1)}, s32[63488]{0:T(1024)}, u32[]{:S(2)}) copy-start(s32[63488]{0:T(1024)} %param.24) | copy-start | bytes 761860
  5.0 33.6 %copy-start.11 = (s32[1,1,128]{2,1,0:T(1,128)S(1)}, s32[1,1,128]{2,1,0:T(1,128)}, u32[]{:S(2)}) copy-start(s32[1,1,128]{2,1,0:T(1,128)} %param.16) | copy-start | bytes 1540
  32.1 3.8 %collective-permute-start.29 = (s16[144,128]{1,0:T(8,128)(2,1)S(1)}, s16[144,128]{1,0:T(8,128)(2,1)S(1)}, u32[]{:S(2)}, u32[]{:S(2)}) collective-permute-start(s16[144,128]{1,0:T(8,128)(2,1)S(1)} %get-tuple-element.66.refs_0_), channel_id=1, source_target_pairs={{0,3},{1,2},{2,1},{3,0},{4,7},{5,6},{6,5},{7,4},{8,11},{9,10},{10,... | collective-permute-start | bytes 110600 | tf_op jit(solution)/shard_map/ppermute | solution.py:268
  32.1 4.2 %collective-permute-start.28 = (s16[144,128]{1,0:T(8,128)(2,1)S(1)}, s16[144,128]{1,0:T(8,128)(2,1)S(1)}, u32[]{:S(2)}, u32[]{:S(2)}) collective-permute-start(s16[144,128]{1,0:T(8,128)(2,1)S(1)} %get-tuple-element.66.refs_0_), channel_id=1, source_target_pairs={{0,2},{1,3},{2,0},{3,1},{4,6},{5,7},{6,4},{7,5},{8,10},{9,11},{10,... | collective-permute-start | bytes 110600 | tf_op jit(solution)/shard_map/ppermute | solution.py:268
  33.7 2.6 %collective-permute-start.27 = (s16[144,128]{1,0:T(8,128)(2,1)S(1)}, s16[144,128]{1,0:T(8,128)(2,1)S(1)}, u32[]{:S(2)}, u32[]{:S(2)}) collective-permute-start(s16[144,128]{1,0:T(8,128)(2,1)S(1)} %get-tuple-element.66.refs_0_), channel_id=1, source_target_pairs={{0,1},{1,0},{2,3},{3,2},{4,5},{5,4},{6,7},{7,6},{8,9},{9,8},{10,11... | collective-permute-start | bytes 110600 | tf_op jit(solution)/shard_map/ppermute | solution.py:268

commit v9 on v8

--- a/solution.py
+++ b/solution.py
@@ -8,7 +8,7 @@
 
 TILE = 128
 GROUP = 16
-CHUNK = 16
+CHUNK = 32
 SLOTS = 40
 HEAD = 16
 BITS = 14
@@ -84,7 +84,7 @@
 
 def transpose_product_kernel(owned, *refs):
     (rows_hbm, cols_hbm, duals_hbm, tiles_hbm), (out_ref, slot_ref, duals, tiles), refs = refs[:4], refs[4:8], refs[8:]
-    rows, cols, picked, terms, small_sems, tile_sems = refs
+    rows, cols, picked, small_sems, tile_sems = refs
     n_row = out_ref.shape[0]
     chunks, head_rows = rounds_of(n_row)
     most = SLOTS - head_rows
@@ -98,14 +98,16 @@
     for k in range(k_tiles):
         picked[pl.ds(k, 1), :] = duals[pl.ds(rows[k], 1), :]
 
+    terms = []
+
     def products_of(chunk):
         large[chunk].wait()
         for first in range(chunk * CHUNK, (chunk + 1) * CHUNK, GROUP):
             group = pl.ds(first, GROUP)
             block = picked[group, :].astype(bf16).astype(f32)
             left = jnp.concatenate([one_row_of(block, m) for m in range(GROUP)], axis=1)
-            terms[group, :] = jnp.dot(
-                left, tiles[group].reshape(GROUP * TILE, TILE), preferred_element_type=f32
+            terms.append(
+                jnp.dot(left, tiles[group].reshape(GROUP * TILE, TILE), preferred_element_type=f32)
             )
 
     products_of(0)
@@ -137,7 +139,7 @@
 
     for chunk in range(1, len(large)):
         products_of(chunk)
-    whole, exponents = coded(terms[...])
+    whole, exponents = coded(jnp.concatenate(terms, axis=0))
 
     scaled = [to_lanes, to_lanes * jnp.concatenate([exponents] * chunks, axis=1)]
     heads = jnp.dot(head_left, jnp.concatenate(scaled, axis=1).astype(bf16), preferred_element_type=f32)
@@ -238,10 +240,9 @@
         copy.wait()
 
 
-def dual_kernel(n_col, *refs):
-    payloads, (duals_ref, right_ref, kind_ref, steps_ref, next_ref, flag_ref) = refs[:n_col], refs[n_col:]
+def row_sums_of(payloads, blocks):
     k_tiles = payloads[0].shape[0] - HEAD
-    down = iota((duals_ref.shape[0], k_tiles), 0)
+    down = iota((blocks, k_tiles), 0)
     masks, wholes = [], []
     flags = jnp.zeros((1, TILE), i32)
     for payload in payloads:
@@ -249,8 +250,18 @@
         masks.append(scaled_mask(down, head[0:1], head[1:2]))
         wholes.append(payload[pl.ds(0, k_tiles), :].astype(i32))
         flags += head[2:3]
-    row_sums = picked_sums(masks, wholes)
-    updated = duals_ref[...] + steps_ref[1] * (right_ref[...] - row_sums)
+    return picked_sums(masks, wholes), flags
+
+
+def own_dual_kernel(payload, duals_ref, right_ref, steps_ref, part_ref):
+    row_sums, _ = row_sums_of([payload], duals_ref.shape[0])
+    part_ref[...] = duals_ref[...] + steps_ref[1] * (right_ref[...] - row_sums)
+
+
+def dual_kernel(*refs):
+    payloads, (part_ref, kind_ref, steps_ref, next_ref, flag_ref) = refs[:-5], refs[-5:]
+    row_sums, flags = row_sums_of(payloads, part_ref.shape[0])
+    updated = part_ref[...] - steps_ref[1] * row_sums
     next_ref[...] = jnp.where(kind_ref[...] == 1, jnp.maximum(updated, 0.0), updated)
     flag_ref[0] = jnp.max(flags)
 
@@ -345,7 +356,6 @@
         scratch_shapes=[
             pltpu.SMEM((k_tiles,), i32),
             pltpu.VMEM((1, k_tiles), i32),
-            pltpu.VMEM((k_tiles, TILE), f32),
             pltpu.VMEM((k_tiles, TILE), f32),
             pltpu.SemaphoreType.DMA((3,)),
             pltpu.SemaphoreType.DMA((k_tiles // CHUNK,)),
@@ -382,14 +392,24 @@
         compiler_params=params,
         name="product",
     )(rows.reshape(1, k_tiles), slots, tiles_kept, lax.all_to_all(wanted, "row", 0, 0), flag, *dual_side)
+    _, *others = gathered_along(row_terms, "col")
+    part = pl.pallas_call(
+        own_dual_kernel,
+        out_shape=jax.ShapeDtypeStruct((row_blocks, TILE), f32),
+        in_specs=[VMEM] * 3 + [SMEM],
+        out_specs=VMEM,
+        compiler_params=params,
+        cost_estimate=pl.CostEstimate(flops=4 * row_blocks * k_tiles * TILE, bytes_accessed=2**20, transcendentals=0),
+        name="own_dual_step",
+    )(row_terms, duals_kept, dual_kept[0], step_sizes)
     dual_next, too_many = pl.pallas_call(
-        functools.partial(dual_kernel, n_col),
+        dual_kernel,
         out_shape=(jax.ShapeDtypeStruct((row_blocks, TILE), f32), jax.ShapeDtypeStruct((1,), i32)),
-        in_specs=[VMEM] * (n_col + 3) + [SMEM],
+        in_specs=[VMEM] * (n_col + 1) + [SMEM],
         out_specs=(VMEM, SMEM),
         compiler_params=params,
         name="dual_step",
-    )(*gathered_along(row_terms, "col"), duals_kept, *dual_kept, step_sizes)
+    )(*others, part, dual_kept[1], step_sizes)
     vectors = (primal, duals, cost_vec, lower_bound, upper_bound, bound_kind, right_side, row_kind, step_sizes)
     return lax.cond(
         too_many[0] > 0,

time: 38.8 us -> 38.1 us (0.982)
  waiting for transfers between devices: 2.31 us -> 1.55 us
    ppermute x3, waiting for transfers between devices: 2.31 us -> 1.55 us  [gathered_along(): lax.ppermute(array, axis, there)]
    pallas_call x1 -> x2, Pallas kernels: 1.57 us -> 2.32 us  [the longest x1 1.56 us: local(): pl.pallas_call(dual_kernel, out_shape=(jax.ShapeDtypeStruct((row_blocks,...]
    pallas_call x1, Pallas kernels: 4.23 us -> 3.52 us  [local(): pl.pallas_call(functools.partial(transpose_product_kernel, col_blocks), o...]
  transfers between devices with their start and end apart: 3 -> 3, of which waited for: 2 -> 2; matrix products, arithmetic and copies ran while one was open for 0% -> 0% of each run, Pallas kernels for 0% -> 2%
where the time goes in v9:
time: 38.1 us; the launch traced here: 37.9 us
  blocking collectives  23.6 us (62%)
  Pallas kernels  9.24 us (24%)
  starting transfers between devices  1.92 us (5%)
  waiting for transfers between devices  1.55 us (4%)
  between operations  1.46 us (4%)
    all_to_all x1, blocking collectives, local(): lax.all_to_all(col_terms, 'row', 0, 0)  14.2 us
    all_to_all x1, blocking collectives, local(): lax.all_to_all(wanted, 'row', 0, 0)  9.4 us
    pallas_call x1, Pallas kernels, local(): pl.pallas_call(functools.partial(transpose_product_kernel, col_blocks), o...  3.52 us
    ppermute x3, starting transfers between devices, gathered_along(): lax.ppermute(array, axis, there)  1.92 us
    pallas_call x1, Pallas kernels, local(): pl.pallas_call(product_kernel, out_shape=(jax.ShapeDtypeStruct((k_tiles +...  1.71 us
    pallas_call x1, Pallas kernels, local(): pl.pallas_call(primal_kernel, out_shape=(jax.ShapeDtypeStruct((col_blocks...  1.69 us
    pallas_call x1, Pallas kernels, local(): pl.pallas_call(dual_kernel, out_shape=(jax.ShapeDtypeStruct((row_blocks,...  1.56 us
    ppermute x3, waiting for transfers between devices, gathered_along(): lax.ppermute(array, axis, there)  1.55 us
  transfers between devices with their start and end apart: 3, of which 2 were waited for; matrix products, arithmetic and copies ran while one was open for 0% of the time, Pallas kernels for 2%

profile of v9, /device:TPU:0, one launch (start us, length us, event | category | flops | bytes accessed | tf_op | source)
XLA Modules:
  0.0 37.9 jit_solution(17983817170981402321)
XLA Ops:
  0.6 0.0 copy-start.10
  0.6 0.0 copy-start.9
  0.7 0.0 copy-start.3
  0.7 0.0 copy-start.4
  0.7 0.0 copy-start.5
  0.7 0.0 copy-start.6
  0.7 0.0 copy-start.7
  0.7 3.5 %transpose_product.1 = (s16[8,40,128]{2,1,0:T(8,128)(2,1)S(1)}, s32[128,128]{1,0:T(8,128)S(1)}, f32[496,128]{1,0:T(8,128)S(1)}, bf16[128,128,128]{2,1,0:T(8,128)(2,1)S(1)}) custom-call(s32[128]{0:T(128)} %bitcast.90, s32[1,128]{1,0:T(1,128)} %bitcast.93, f32[496,128]{1,0:T(8,128)} %bitcast.67, bf16[128,128,128]{2,1,0:T(8,128)(2,1)} %bitcast.65), custom_call_target="tpu_custom_call" | custom-call | tf_op jit(solution)/shard_map/transpose_product/pallas_call | solution.py:347
  4.2 0.0 copy-start
  4.2 0.0 copy-start.1
  4.3 0.0 copy-start.2
  4.3 0.0 copy-start.11
  4.3 14.2 %all_to_all.10.payloads = s16[8,40,128]{2,1,0:T(8,128)(2,1)S(1)} all-to-all(s16[8,40,128]{2,1,0:T(8,128)(2,1)S(1)} %get-tuple-element.63), channel_id=1, replica_groups=mesh['row'=8,'col'=4] {'row'}, dimensions={0} | all-to-all | bytes 163840 | tf_op jit(solution)/shard_map/all_to_all | solution.py:382
  18.5 0.0 copy-done.9
  18.5 0.0 copy-done.3
  18.5 0.0 copy-done.4
  18.5 0.0 copy-done.5
  18.5 0.0 copy-done.6
  18.5 0.0 copy-done.7
  18.5 1.7 %primal_step.1 = (f32[488,128]{1,0:T(8,128)}, s32[8,128]{1,0:T(8,128)S(1)}, bf16[8,40,128]{2,1,0:T(8,128)(2,1)S(1)}) custom-call(s16[8,40,128]{2,1,0:T(8,128)(2,1)S(1)} %all_to_all.10.payloads, f32[488,128]{1,0:T(8,128)S(1)} %bitcast.70, f32[488,128]{1,0:T(8,128)S(1)} %bitcast.85, f32[488,128]{1,0:T(8,128)S(1)} %bitcast.86, f32[488,128]{1,0:T(8,128)S(1)} %bitcast.87, ...), custom_call_target="tpu_custom_call" | custom-call | tf_op jit(solution)/shard_map/primal_step/pallas_call | solution.py:366
  20.2 9.4 %all_to_all.11.refs_3_ = bf16[8,40,128]{2,1,0:T(8,128)(2,1)S(1)} all-to-all(bf16[8,40,128]{2,1,0:T(8,128)(2,1)S(1)} %get-tuple-element.64), channel_id=1, replica_groups=mesh['row'=8,'col'=4] {'row'}, dimensions={0} | all-to-all | bytes 163840 | tf_op jit(solution)/shard_map/all_to_all | solution.py:394
  29.6 0.0 copy-done.10
  29.6 1.7 %product.1 = (s16[144,128]{1,0:T(8,128)(2,1)S(1)}, f32[496,128]{1,0:T(8,128)S(1)}, s32[496,128]{1,0:T(8,128)S(1)}) custom-call(s32[1,128]{1,0:T(1,128)S(1)} %bitcast.91, s32[128,128]{1,0:T(8,128)S(1)} %get-tuple-element.61.refs_1_, bf16[128,128,128]{2,1,0:T(8,128)(2,1)S(1)} %get-tuple-element.62.refs_2_, bf16[8,40,128]{2,1,0:T(8,128)(2,1)S(1)} %all_to_all.11.refs_3_, ...), custom_call_target="tpu_custom_call" | custom-call | tf_op jit(solution)/shard_map/product/pallas_call | solution.py:383
  31.4 0.1 collective-permute-start.29
  31.4 1.6 %collective-permute-start.28 = (s16[144,128]{1,0:T(8,128)(2,1)S(1)}, s16[144,128]{1,0:T(8,128)(2,1)S(1)}, u32[]{:S(2)}, u32[]{:S(2)}) collective-permute-start(s16[144,128]{1,0:T(8,128)(2,1)S(1)} %get-tuple-element.66.payload), channel_id=1, source_target_pairs={{0,2},{1,3},{2,0},{3,1},{4,6},{5,7},{6,4},{7,5},{8,10},{9,11},{10,... | collective-permute-start | bytes 110600 | tf_op jit(solution)/shard_map/ppermute | solution.py:279
  33.0 0.3 collective-permute-start.27
  33.3 0.8 %own_dual_step.1.refs_3_ = f32[496,128]{1,0:T(8,128)S(1)} custom-call(s16[144,128]{1,0:T(8,128)(2,1)S(1)} %get-tuple-element.66.payload, f32[496,128]{1,0:T(8,128)S(1)} %get-tuple-element.67.duals_ref, f32[496,128]{1,0:T(8,128)S(1)} %get-tuple-element.68.right_ref, f32[2]{0:T(128)S(1)} %copy-done.9), custom_call_target="tpu_custom_call" | custom-call | flops 32505856 | bytes 1048576 | tf_op jit(solution)/shard_map/own_dual_step/pallas_call | solution.py:396
  34.1 1.1 %collective-permute-done.29.refs_2_ = s16[144,128]{1,0:T(8,128)(2,1)S(1)} collective-permute-done((s16[144,128]{1,0:T(8,128)(2,1)S(1)}, s16[144,128]{1,0:T(8,128)(2,1)S(1)}, u32[]{:S(2)}, u32[]{:S(2)}) %collective-permute-start.29) | collective-permute-done | bytes 36896 | tf_op jit(solution)/shard_map/ppermute | solution.py:279
  35.2 0.4 %collective-permute-done.28.refs_1_ = s16[144,128]{1,0:T(8,128)(2,1)S(1)} collective-permute-done((s16[144,128]{1,0:T(8,128)(2,1)S(1)}, s16[144,128]{1,0:T(8,128)(2,1)S(1)}, u32[]{:S(2)}, u32[]{:S(2)}) %collective-permute-start.28) | collective-permute-done | bytes 36896 | tf_op jit(solution)/shard_map/ppermute | solution.py:279
  35.6 0.0 collective-permute-done.27.refs_0_
  35.6 1.6 %dual_step.1 = (f32[496,128]{1,0:T(8,128)}, s32[1]{0:T(128)}) custom-call(s16[144,128]{1,0:T(8,128)(2,1)S(1)} %collective-permute-done.27.refs_0_, s16[144,128]{1,0:T(8,128)(2,1)S(1)} %collective-permute-done.28.refs_1_, s16[144,128]{1,0:T(8,128)(2,1)S(1)} %collective-permute-done.29.refs_2_, f32[496,128]{1,0:T(8,128)S(1)} %own_dual_step.1.refs_3_, ...), custom_call_target="tpu_custom_call" | custom-call | tf_op jit(solution)/shard_map/dual_step/pallas_call | solution.py:405
  37.8 0.0 copy-done
  37.8 0.0 copy-done.1
  37.8 0.0 copy-done.2
  37.8 0.0 copy-done.11
  (1 shorter events, 0.0 us)
Async XLA Ops:
  0.6 29.0 %copy-start.10 = (s32[1,1,128]{2,1,0:T(1,128)S(1)}, s32[1,1,128]{2,1,0:T(1,128)}, u32[]{:S(2)}) copy-start(s32[1,1,128]{2,1,0:T(1,128)} %param.15) | copy-start | bytes 1540
  0.6 17.9 %copy-start.9 = (f32[2]{0:T(128)S(1)}, f32[2]{0:T(128)}, u32[]{:S(2)}) copy-start(f32[2]{0:T(128)} %refs_5_.1) | copy-start | bytes 28
  0.7 17.9 %copy-start.3 = (f32[62464]{0:T(1024)S(1)}, f32[62464]{0:T(1024)}, u32[]{:S(2)}) copy-start(f32[62464]{0:T(1024)} %param.17) | copy-start | bytes 749572
  0.7 17.8 %copy-start.4 = (f32[62464]{0:T(1024)S(1)}, f32[62464]{0:T(1024)}, u32[]{:S(2)}) copy-start(f32[62464]{0:T(1024)} %param.19) | copy-start | bytes 749572
  0.7 17.8 %copy-start.5 = (f32[62464]{0:T(1024)S(1)}, f32[62464]{0:T(1024)}, u32[]{:S(2)}) copy-start(f32[62464]{0:T(1024)} %param.20) | copy-start | bytes 749572
  0.7 17.8 %copy-start.6 = (f32[62464]{0:T(1024)S(1)}, f32[62464]{0:T(1024)}, u32[]{:S(2)}) copy-start(f32[62464]{0:T(1024)} %param.21) | copy-start | bytes 749572
  0.7 17.8 %copy-start.7 = (s32[62464]{0:T(1024)S(1)}, s32[62464]{0:T(1024)}, u32[]{:S(2)}) copy-start(s32[62464]{0:T(1024)} %param.22) | copy-start | bytes 749572
  4.2 33.6 %copy-start = (f32[63488]{0:T(1024)S(1)}, f32[63488]{0:T(1024)}, u32[]{:S(2)}) copy-start(f32[63488]{0:T(1024)} %param.18) | copy-start | bytes 761860
  4.2 33.6 %copy-start.1 = (f32[63488]{0:T(1024)S(1)}, f32[63488]{0:T(1024)}, u32[]{:S(2)}) copy-start(f32[63488]{0:T(1024)} %param.23) | copy-start | bytes 761860
  4.3 33.6 %copy-start.2 = (s32[63488]{0:T(1024)S(1)}, s32[63488]{0:T(1024)}, u32[]{:S(2)}) copy-start(s32[63488]{0:T(1024)} %param.24) | copy-start | bytes 761860
  4.3 33.6 %copy-start.11 = (s32[1,1,128]{2,1,0:T(1,128)S(1)}, s32[1,1,128]{2,1,0:T(1,128)}, u32[]{:S(2)}) copy-start(s32[1,1,128]{2,1,0:T(1,128)} %param.16) | copy-start | bytes 1540
  31.4 3.8 %collective-permute-start.29 = (s16[144,128]{1,0:T(8,128)(2,1)S(1)}, s16[144,128]{1,0:T(8,128)(2,1)S(1)}, u32[]{:S(2)}, u32[]{:S(2)}) collective-permute-start(s16[144,128]{1,0:T(8,128)(2,1)S(1)} %get-tuple-element.66.payload), channel_id=1, source_target_pairs={{0,3},{1,2},{2,1},{3,0},{4,7},{5,6},{6,5},{7,4},{8,11},{9,10},{10,... | collective-permute-start | bytes 110600 | tf_op jit(solution)/shard_map/ppermute | solution.py:279
  31.4 4.2 %collective-permute-start.28 = (s16[144,128]{1,0:T(8,128)(2,1)S(1)}, s16[144,128]{1,0:T(8,128)(2,1)S(1)}, u32[]{:S(2)}, u32[]{:S(2)}) collective-permute-start(s16[144,128]{1,0:T(8,128)(2,1)S(1)} %get-tuple-element.66.payload), channel_id=1, source_target_pairs={{0,2},{1,3},{2,0},{3,1},{4,6},{5,7},{6,4},{7,5},{8,10},{9,11},{10,... | collective-permute-start | bytes 110600 | tf_op jit(solution)/shard_map/ppermute | solution.py:279
  33.0 2.6 %collective-permute-start.27 = (s16[144,128]{1,0:T(8,128)(2,1)S(1)}, s16[144,128]{1,0:T(8,128)(2,1)S(1)}, u32[]{:S(2)}, u32[]{:S(2)}) collective-permute-start(s16[144,128]{1,0:T(8,128)(2,1)S(1)} %get-tuple-element.66.payload), channel_id=1, source_target_pairs={{0,1},{1,0},{2,3},{3,2},{4,5},{5,4},{6,7},{7,6},{8,9},{9,8},{10,11... | collective-permute-start | bytes 110600 | tf_op jit(solution)/shard_map/ppermute | solution.py:279

commit v10 on v9

--- a/solution.py
+++ b/solution.py
@@ -83,8 +83,9 @@
 
 
 def transpose_product_kernel(owned, *refs):
-    (rows_hbm, cols_hbm, duals_hbm, tiles_hbm), (out_ref, slot_ref, duals, tiles), refs = refs[:4], refs[4:8], refs[8:]
-    rows, cols, picked, small_sems, tile_sems = refs
+    (rows_hbm, cols_hbm, duals_hbm, tiles_hbm), others_hbm, refs = refs[:4], refs[4:9], refs[9:]
+    (out_ref, slot_ref, duals, tiles), others, refs = refs[:4], refs[4:9], refs[9:]
+    rows, cols, picked, small_sems, tile_sems, other_sems = refs
     n_row = out_ref.shape[0]
     chunks, head_rows = rounds_of(n_row)
     most = SLOTS - head_rows
@@ -137,8 +138,10 @@
         [of_owner * (place - place_low).astype(f32), of_owner * place_low.astype(f32), of_owner], axis=0
     ).astype(bf16)
 
-    for chunk in range(1, len(large)):
+    for chunk in range(1, len(large) - 1):
         products_of(chunk)
+    later = started(others_hbm, others, other_sems)
+    products_of(len(large) - 1)
     whole, exponents = coded(jnp.concatenate(terms, axis=0))
 
     scaled = [to_lanes, to_lanes * jnp.concatenate([exponents] * chunks, axis=1)]
@@ -155,6 +158,8 @@
             head = jnp.where(line == c, packed[o : o + 1, c * TILE : (c + 1) * TILE], head)
         rows_of = body[o * SLOTS + top : (o + 1) * SLOTS]
         out_ref[o] = jnp.concatenate([head, rows_of], axis=0).astype(i32).astype(i16)
+    for copy in later:
+        copy.wait()
 
 
 def place_range(owned):
@@ -240,30 +245,40 @@
         copy.wait()
 
 
-def row_sums_of(payloads, blocks):
+def coded_rows(payloads):
     k_tiles = payloads[0].shape[0] - HEAD
-    down = iota((blocks, k_tiles), 0)
-    masks, wholes = [], []
-    flags = jnp.zeros((1, TILE), i32)
-    for payload in payloads:
-        head = payload[pl.ds(k_tiles, HEAD), :].astype(i32)
-        masks.append(scaled_mask(down, head[0:1], head[1:2]))
-        wholes.append(payload[pl.ds(0, k_tiles), :].astype(i32))
-        flags += head[2:3]
-    return picked_sums(masks, wholes), flags
+    heads = [payload[pl.ds(k_tiles, HEAD), :].astype(i32) for payload in payloads]
+    rows = [two_parts(payload[pl.ds(0, k_tiles), :].astype(i32)) for payload in payloads]
+    return heads, jnp.concatenate(rows, axis=0)
+
+
+def row_sums_of(heads, rows, first, blocks):
+    down = iota((blocks, TILE), 0) + first
+    masks = [scaled_mask(down, head[0:1], head[1:2]) for head in heads]
+    both = jnp.dot(jnp.concatenate(masks, axis=1).astype(bf16), rows, preferred_element_type=f32)
+    return both[:, :TILE] + both[:, TILE:]
 
 
 def own_dual_kernel(payload, duals_ref, right_ref, steps_ref, part_ref):
-    row_sums, _ = row_sums_of([payload], duals_ref.shape[0])
+    row_sums = row_sums_of(*coded_rows([payload]), 0, duals_ref.shape[0])
     part_ref[...] = duals_ref[...] + steps_ref[1] * (right_ref[...] - row_sums)
 
 
 def dual_kernel(*refs):
-    payloads, (part_ref, kind_ref, steps_ref, next_ref, flag_ref) = refs[:-5], refs[-5:]
-    row_sums, flags = row_sums_of(payloads, part_ref.shape[0])
-    updated = part_ref[...] - steps_ref[1] * row_sums
-    next_ref[...] = jnp.where(kind_ref[...] == 1, jnp.maximum(updated, 0.0), updated)
-    flag_ref[0] = jnp.max(flags)
+    payloads, (part_ref, kind_ref, steps_ref, next_hbm, flag_ref, next_ref, sems) = refs[:-7], refs[-7:]
+    heads, rows = coded_rows(payloads)
+    flag_ref[0] = jnp.max(sum(head[2:3] for head in heads))
+    blocks = part_ref.shape[0]
+    half = blocks // 16 * 8
+    copies = []
+    for n, (first, count) in enumerate([(0, half), (half, blocks - half)]):
+        here = pl.ds(first, count)
+        updated = part_ref[here, :] - steps_ref[1] * row_sums_of(heads, rows, first, count)
+        next_ref[here, :] = jnp.where(kind_ref[here, :] == 1, jnp.maximum(updated, 0.0), updated)
+        copies.append(pltpu.make_async_copy(next_ref.at[here], next_hbm.at[here], sems.at[n]))
+        copies[-1].start()
+    for copy in copies:
+        copy.wait()
 
 
 def partners(axis):
@@ -340,29 +355,30 @@
     by_block = lambda array: in_hbm(array.reshape(-1, TILE))
     shape_of = lambda array: jax.ShapeDtypeStruct(array.shape, array.dtype)
     params = pltpu.CompilerParams(vmem_limit_bytes=32 * 1024 * 1024)
-    primal_side = [a.reshape(-1, TILE) for a in (primal, cost_vec, lower_bound, upper_bound, bound_kind)]
+    primal_side = [by_block(a) for a in (primal, cost_vec, lower_bound, upper_bound, bound_kind)]
     dual_side = [by_block(a) for a in (right_side, row_kind)]
     own = [by_block(duals), in_hbm(tiles)]
 
-    col_terms, slots, duals_kept, tiles_kept = pl.pallas_call(
+    col_terms, slots, duals_kept, tiles_kept, *primal_kept = pl.pallas_call(
         functools.partial(transpose_product_kernel, col_blocks),
         out_shape=(
             jax.ShapeDtypeStruct((n_row, SLOTS, TILE), i16),
             jax.ShapeDtypeStruct((k_tiles, TILE), i32),
-            *[shape_of(a) for a in own],
+            *[shape_of(a) for a in own + primal_side],
         ),
-        in_specs=[HBM] * 4,
-        out_specs=(VMEM,) * 4,
+        in_specs=[HBM] * 9,
+        out_specs=(VMEM,) * 9,
         scratch_shapes=[
             pltpu.SMEM((k_tiles,), i32),
             pltpu.VMEM((1, k_tiles), i32),
             pltpu.VMEM((k_tiles, TILE), f32),
             pltpu.SemaphoreType.DMA((3,)),
             pltpu.SemaphoreType.DMA((k_tiles // CHUNK,)),
+            pltpu.SemaphoreType.DMA((5,)),
         ],
         compiler_params=params,
         name="transpose_product",
-    )(in_hbm(rows), in_hbm(cols.reshape(1, k_tiles)), *own)
+    )(in_hbm(rows), in_hbm(cols.reshape(1, k_tiles)), *own, *primal_side)
     primal_next, flag, wanted = pl.pallas_call(
         primal_kernel,
         out_shape=(
@@ -379,7 +395,7 @@
         ],
         compiler_params=params,
         name="primal_step",
-    )(lax.all_to_all(col_terms, "row", 0, 0), *primal_side, step_sizes)
+    )(lax.all_to_all(col_terms, "row", 0, 0), *primal_kept, step_sizes)
     row_terms, *dual_kept = pl.pallas_call(
         product_kernel,
         out_shape=(
@@ -406,7 +422,8 @@
         dual_kernel,
         out_shape=(jax.ShapeDtypeStruct((row_blocks, TILE), f32), jax.ShapeDtypeStruct((1,), i32)),
         in_specs=[VMEM] * (n_col + 1) + [SMEM],
-        out_specs=(VMEM, SMEM),
+        out_specs=(HBM, SMEM),
+        scratch_shapes=[pltpu.VMEM((row_blocks, TILE), f32), pltpu.SemaphoreType.DMA((2,))],
         compiler_params=params,
         name="dual_step",
     )(*others, part, dual_kept[1], step_sizes)

time: 38.1 us -> 39.2 us (1.029)
  Pallas kernels: 9.24 us -> 10.3 us
    pallas_call x1, Pallas kernels: 3.52 us -> 4.06 us  [local(): pl.pallas_call(functools.partial(transpose_product_kernel, col_blocks), o...]
    pallas_call x1, Pallas kernels: 1.56 us -> 2.08 us  [local(): pl.pallas_call(dual_kernel, out_shape=(jax.ShapeDtypeStruct((row_blocks,...]
where the time goes in v10:
time: 39.2 us; the launch traced here: 38.9 us
  blocking collectives  23.6 us (60%)
  Pallas kernels  10.3 us (26%)
  starting transfers between devices  1.92 us (5%)
  waiting for transfers between devices  1.55 us (4%)
  between operations  1.47 us (4%)
    all_to_all x1, blocking collectives, local(): lax.all_to_all(col_terms, 'row', 0, 0)  14.2 us
    all_to_all x1, blocking collectives, local(): lax.all_to_all(wanted, 'row', 0, 0)  9.4 us
    pallas_call x1, Pallas kernels, local(): pl.pallas_call(functools.partial(transpose_product_kernel, col_blocks), o...  4.06 us
    pallas_call x1, Pallas kernels, local(): pl.pallas_call(dual_kernel, out_shape=(jax.ShapeDtypeStruct((row_blocks,...  2.08 us
    ppermute x3, starting transfers between devices, gathered_along(): lax.ppermute(array, axis, there)  1.92 us
    pallas_call x1, Pallas kernels, local(): pl.pallas_call(product_kernel, out_shape=(jax.ShapeDtypeStruct((k_tiles +...  1.71 us
    pallas_call x1, Pallas kernels, local(): pl.pallas_call(primal_kernel, out_shape=(jax.ShapeDtypeStruct((col_blocks...  1.69 us
    ppermute x3, waiting for transfers between devices, gathered_along(): lax.ppermute(array, axis, there)  1.55 us
  transfers between devices with their start and end apart: 3, of which 2 were waited for; matrix products, arithmetic and copies ran while one was open for 0% of the time, Pallas kernels for 2%

profile of v10, /device:TPU:0, one launch (start us, length us, event | category | flops | bytes accessed | tf_op | source)
XLA Modules:
  0.0 38.9 jit_solution(503093068640502114)
XLA Ops:
  0.6 0.0 copy-start.10
  0.6 0.0 copy-start.9
  0.6 4.1 %transpose_product.1 = (s16[8,40,128]{2,1,0:T(8,128)(2,1)S(1)}, s32[128,128]{1,0:T(8,128)S(1)}, f32[496,128]{1,0:T(8,128)S(1)}, bf16[128,128,128]{2,1,0:T(8,128)...) custom-call(s32[128]{0:T(128)} %bitcast.90, ...), custom_call_target="tpu_custom_call" | custom-call | tf_op jit(solution)/shard_map/transpose_product/pallas_call | solution.py:362
  4.7 0.0 copy-start
  4.7 0.0 copy-start.1
  4.7 0.0 copy-start.2
  4.8 0.0 copy-start.3
  4.8 0.0 copy-start.4
  4.8 0.0 copy-start.5
  4.8 0.0 copy-start.6
  4.8 0.0 copy-start.7
  4.8 0.0 copy-start.11
  4.8 14.2 %all_to_all.10.payloads = s16[8,40,128]{2,1,0:T(8,128)(2,1)S(1)} all-to-all(s16[8,40,128]{2,1,0:T(8,128)(2,1)S(1)} %get-tuple-element.68), channel_id=1, replica_groups=mesh['row'=8,'col'=4] {'row'}, dimensions={0} | all-to-all | bytes 163840 | tf_op jit(solution)/shard_map/all_to_all | solution.py:398
  19.1 0.0 copy-done.9
  19.1 1.7 %primal_step.1 = (f32[488,128]{1,0:T(8,128)}, s32[8,128]{1,0:T(8,128)S(1)}, bf16[8,40,128]{2,1,0:T(8,128)(2,1)S(1)}) custom-call(s16[8,40,128]{2,1,0:T(8,128)(2,1)S(1)} %all_to_all.10.payloads, f32[488,128]{1,0:T(8,128)S(1)} %get-tuple-element.69.primal_ref, f32[488,128]{1,0:T(8,128)S(1)} %get-tuple-element.70.cost_ref, ...), custom_call_target="tpu_custom_call" | custom-call | tf_op jit(solution)/shard_map/primal_step/pallas_call | solution.py:382
  20.8 9.4 %all_to_all.11.refs_3_ = bf16[8,40,128]{2,1,0:T(8,128)(2,1)S(1)} all-to-all(bf16[8,40,128]{2,1,0:T(8,128)(2,1)S(1)} %get-tuple-element.74), channel_id=1, replica_groups=mesh['row'=8,'col'=4] {'row'}, dimensions={0} | all-to-all | bytes 163840 | tf_op jit(solution)/shard_map/all_to_all | solution.py:410
  30.2 0.0 copy-done.10
  30.2 1.7 %product.1 = (s16[144,128]{1,0:T(8,128)(2,1)S(1)}, f32[496,128]{1,0:T(8,128)S(1)}, s32[496,128]{1,0:T(8,128)S(1)}) custom-call(s32[1,128]{1,0:T(1,128)S(1)} %bitcast.91, s32[128,128]{1,0:T(8,128)S(1)} %get-tuple-element.66.refs_1_, bf16[128,128,128]{2,1,0:T(8,128)(2,1)S(1)} %get-tuple-element.67.refs_2_, bf16[8,40,128]{2,1,0:T(8,128)(2,1)S(1)} %all_to_all.11.refs_3_, ...), custom_call_target="tpu_custom_call" | custom-call | tf_op jit(solution)/shard_map/product/pallas_call | solution.py:399
  31.9 0.1 collective-permute-start.29
  32.0 1.6 %collective-permute-start.28 = (s16[144,128]{1,0:T(8,128)(2,1)S(1)}, s16[144,128]{1,0:T(8,128)(2,1)S(1)}, u32[]{:S(2)}, u32[]{:S(2)}) collective-permute-start(s16[144,128]{1,0:T(8,128)(2,1)S(1)} %get-tuple-element.76.payload), channel_id=1, source_target_pairs={{0,2},{1,3},{2,0},{3,1},{4,6},{5,7},{6,4},{7,5},{8,10},{9,11},{10,... | collective-permute-start | bytes 110600 | tf_op jit(solution)/shard_map/ppermute | solution.py:294
  33.5 0.3 collective-permute-start.27
  33.8 0.8 %own_dual_step.1.refs_3_ = f32[496,128]{1,0:T(8,128)S(1)} custom-call(s16[144,128]{1,0:T(8,128)(2,1)S(1)} %get-tuple-element.76.payload, f32[496,128]{1,0:T(8,128)S(1)} %get-tuple-element.77.duals_ref, f32[496,128]{1,0:T(8,128)S(1)} %get-tuple-element.78.right_ref, f32[2]{0:T(128)S(1)} %copy-done.9), custom_call_target="tpu_custom_call" | custom-call | flops 32505856 | bytes 1048576 | tf_op jit(solution)/shard_map/own_dual_step/pallas_call | solution.py:412
  34.6 1.1 %collective-permute-done.29.refs_2_ = s16[144,128]{1,0:T(8,128)(2,1)S(1)} collective-permute-done((s16[144,128]{1,0:T(8,128)(2,1)S(1)}, s16[144,128]{1,0:T(8,128)(2,1)S(1)}, u32[]{:S(2)}, u32[]{:S(2)}) %collective-permute-start.29) | collective-permute-done | bytes 36896 | tf_op jit(solution)/shard_map/ppermute | solution.py:294
  35.7 0.4 %collective-permute-done.28.refs_1_ = s16[144,128]{1,0:T(8,128)(2,1)S(1)} collective-permute-done((s16[144,128]{1,0:T(8,128)(2,1)S(1)}, s16[144,128]{1,0:T(8,128)(2,1)S(1)}, u32[]{:S(2)}, u32[]{:S(2)}) %collective-permute-start.28) | collective-permute-done | bytes 36896 | tf_op jit(solution)/shard_map/ppermute | solution.py:294
  36.1 0.0 collective-permute-done.27.refs_0_
  36.1 2.1 %dual_step.1 = (f32[496,128]{1,0:T(8,128)}, s32[1]{0:T(128)}) custom-call(s16[144,128]{1,0:T(8,128)(2,1)S(1)} %collective-permute-done.27.refs_0_, s16[144,128]{1,0:T(8,128)(2,1)S(1)} %collective-permute-done.28.refs_1_, s16[144,128]{1,0:T(8,128)(2,1)S(1)} %collective-permute-done.29.refs_2_, f32[496,128]{1,0:T(8,128)S(1)} %own_dual_step.1.refs_3_, ...), custom_call_target="tpu_custom_call" | custom-call | tf_op jit(solution)/shard_map/dual_step/pallas_call | solution.py:421
  38.8 0.0 copy-done
  38.9 0.0 copy-done.1
  38.9 0.0 copy-done.2
  38.9 0.0 copy-done.3
  38.9 0.0 copy-done.4
  38.9 0.0 copy-done.5
  38.9 0.0 copy-done.6
  38.9 0.0 copy-done.7
  38.9 0.0 copy-done.11
  (1 shorter events, 0.0 us)
Async XLA Ops:
  0.6 29.5 %copy-start.10 = (s32[1,1,128]{2,1,0:T(1,128)S(1)}, s32[1,1,128]{2,1,0:T(1,128)}, u32[]{:S(2)}) copy-start(s32[1,1,128]{2,1,0:T(1,128)} %param.15) | copy-start | bytes 1540
  0.6 18.4 %copy-start.9 = (f32[2]{0:T(128)S(1)}, f32[2]{0:T(128)}, u32[]{:S(2)}) copy-start(f32[2]{0:T(128)} %refs_5_.1) | copy-start | bytes 28
  4.7 34.1 %copy-start = (f32[63488]{0:T(1024)S(1)}, f32[63488]{0:T(1024)}, u32[]{:S(2)}) copy-start(f32[63488]{0:T(1024)} %param.18) | copy-start | bytes 761860
  4.7 34.1 %copy-start.1 = (f32[63488]{0:T(1024)S(1)}, f32[63488]{0:T(1024)}, u32[]{:S(2)}) copy-start(f32[63488]{0:T(1024)} %param.23) | copy-start | bytes 761860
  4.7 34.1 %copy-start.2 = (s32[63488]{0:T(1024)S(1)}, s32[63488]{0:T(1024)}, u32[]{:S(2)}) copy-start(s32[63488]{0:T(1024)} %param.24) | copy-start | bytes 761860
  4.8 34.1 %copy-start.3 = (f32[62464]{0:T(1024)S(1)}, f32[62464]{0:T(1024)}, u32[]{:S(2)}) copy-start(f32[62464]{0:T(1024)} %param.17) | copy-start | bytes 749572
  4.8 34.1 %copy-start.4 = (f32[62464]{0:T(1024)S(1)}, f32[62464]{0:T(1024)}, u32[]{:S(2)}) copy-start(f32[62464]{0:T(1024)} %param.19) | copy-start | bytes 749572
  4.8 34.1 %copy-start.5 = (f32[62464]{0:T(1024)S(1)}, f32[62464]{0:T(1024)}, u32[]{:S(2)}) copy-start(f32[62464]{0:T(1024)} %param.20) | copy-start | bytes 749572
  4.8 34.1 %copy-start.6 = (f32[62464]{0:T(1024)S(1)}, f32[62464]{0:T(1024)}, u32[]{:S(2)}) copy-start(f32[62464]{0:T(1024)} %param.21) | copy-start | bytes 749572
  4.8 34.1 %copy-start.7 = (s32[62464]{0:T(1024)S(1)}, s32[62464]{0:T(1024)}, u32[]{:S(2)}) copy-start(s32[62464]{0:T(1024)} %param.22) | copy-start | bytes 749572
  4.8 34.1 %copy-start.11 = (s32[1,1,128]{2,1,0:T(1,128)S(1)}, s32[1,1,128]{2,1,0:T(1,128)}, u32[]{:S(2)}) copy-start(s32[1,1,128]{2,1,0:T(1,128)} %param.16) | copy-start | bytes 1540
  31.9 3.8 %collective-permute-start.29 = (s16[144,128]{1,0:T(8,128)(2,1)S(1)}, s16[144,128]{1,0:T(8,128)(2,1)S(1)}, u32[]{:S(2)}, u32[]{:S(2)}) collective-permute-start(s16[144,128]{1,0:T(8,128)(2,1)S(1)} %get-tuple-element.76.payload), channel_id=1, source_target_pairs={{0,3},{1,2},{2,1},{3,0},{4,7},{5,6},{6,5},{7,4},{8,11},{9,10},{10,... | collective-permute-start | bytes 110600 | tf_op jit(solution)/shard_map/ppermute | solution.py:294
  32.0 4.2 %collective-permute-start.28 = (s16[144,128]{1,0:T(8,128)(2,1)S(1)}, s16[144,128]{1,0:T(8,128)(2,1)S(1)}, u32[]{:S(2)}, u32[]{:S(2)}) collective-permute-start(s16[144,128]{1,0:T(8,128)(2,1)S(1)} %get-tuple-element.76.payload), channel_id=1, source_target_pairs={{0,2},{1,3},{2,0},{3,1},{4,6},{5,7},{6,4},{7,5},{8,10},{9,11},{10,... | collective-permute-start | bytes 110600 | tf_op jit(solution)/shard_map/ppermute | solution.py:294
  33.5 2.6 %collective-permute-start.27 = (s16[144,128]{1,0:T(8,128)(2,1)S(1)}, s16[144,128]{1,0:T(8,128)(2,1)S(1)}, u32[]{:S(2)}, u32[]{:S(2)}) collective-permute-start(s16[144,128]{1,0:T(8,128)(2,1)S(1)} %get-tuple-element.76.payload), channel_id=1, source_target_pairs={{0,1},{1,0},{2,3},{3,2},{4,5},{5,4},{6,7},{7,6},{8,9},{9,8},{10,11... | collective-permute-start | bytes 110600 | tf_op jit(solution)/shard_map/ppermute | solution.py:294

commit v11 on v9

--- a/solution.py
+++ b/solution.py
@@ -8,7 +8,7 @@
 
 TILE = 128
 GROUP = 16
-CHUNK = 32
+CHUNK = 64
 SLOTS = 40
 HEAD = 16
 BITS = 14

time: 38.1 us -> 37.7 us (0.990)
  no operation moved by 1% of the time
where the time goes in v11:
time: 37.7 us; the launch traced here: 37.5 us
  blocking collectives  23.6 us (63%)
  Pallas kernels  8.87 us (24%)
  starting transfers between devices  1.92 us (5%)
  waiting for transfers between devices  1.55 us (4%)
  between operations  1.46 us (4%)
    all_to_all x1, blocking collectives, local(): lax.all_to_all(col_terms, 'row', 0, 0)  14.2 us
    all_to_all x1, blocking collectives, local(): lax.all_to_all(wanted, 'row', 0, 0)  9.4 us
    pallas_call x1, Pallas kernels, local(): pl.pallas_call(functools.partial(transpose_product_kernel, col_blocks), o...  3.14 us
    ppermute x3, starting transfers between devices, gathered_along(): lax.ppermute(array, axis, there)  1.92 us
    pallas_call x1, Pallas kernels, local(): pl.pallas_call(product_kernel, out_shape=(jax.ShapeDtypeStruct((k_tiles +...  1.71 us
    pallas_call x1, Pallas kernels, local(): pl.pallas_call(primal_kernel, out_shape=(jax.ShapeDtypeStruct((col_blocks...  1.69 us
    pallas_call x1, Pallas kernels, local(): pl.pallas_call(dual_kernel, out_shape=(jax.ShapeDtypeStruct((row_blocks,...  1.56 us
    ppermute x3, waiting for transfers between devices, gathered_along(): lax.ppermute(array, axis, there)  1.55 us
  transfers between devices with their start and end apart: 3, of which 2 were waited for; matrix products, arithmetic and copies ran while one was open for 0% of the time, Pallas kernels for 2%

profile of v11, /device:TPU:0, one launch (start us, length us, event | category | flops | bytes accessed | tf_op | source)
XLA Modules:
  0.0 37.5 jit_solution(9955787127281012585)
XLA Ops:
  0.6 0.0 copy-start.10
  0.6 0.0 copy-start.9
  0.7 0.0 copy-start.3
  0.7 0.0 copy-start.4
  0.7 0.0 copy-start.5
  0.7 0.0 copy-start.6
  0.7 0.0 copy-start.7
  0.7 3.1 %transpose_product.1 = (s16[8,40,128]{2,1,0:T(8,128)(2,1)S(1)}, s32[128,128]{1,0:T(8,128)S(1)}, f32[496,128]{1,0:T(8,128)S(1)}, bf16[128,128,128]{2,1,0:T(8,128)(2,1)S(1)}) custom-call(s32[128]{0:T(128)} %bitcast.90, s32[1,128]{1,0:T(1,128)} %bitcast.93, f32[496,128]{1,0:T(8,128)} %bitcast.67, bf16[128,128,128]{2,1,0:T(8,128)(2,1)} %bitcast.65), custom_call_target="tpu_custom_call" | custom-call | tf_op jit(solution)/shard_map/transpose_product/pallas_call | solution.py:347
  3.9 0.0 copy-start
  3.9 0.0 copy-start.1
  3.9 0.0 copy-start.2
  3.9 0.0 copy-start.11
  3.9 14.2 %all_to_all.10.payloads = s16[8,40,128]{2,1,0:T(8,128)(2,1)S(1)} all-to-all(s16[8,40,128]{2,1,0:T(8,128)(2,1)S(1)} %get-tuple-element.63), channel_id=1, replica_groups=mesh['row'=8,'col'=4] {'row'}, dimensions={0} | all-to-all | bytes 163840 | tf_op jit(solution)/shard_map/all_to_all | solution.py:382
  18.1 0.0 copy-done.9
  18.1 0.0 copy-done.3
  18.1 0.0 copy-done.4
  18.1 0.0 copy-done.5
  18.1 0.0 copy-done.6
  18.2 0.0 copy-done.7
  18.2 1.7 %primal_step.1 = (f32[488,128]{1,0:T(8,128)}, s32[8,128]{1,0:T(8,128)S(1)}, bf16[8,40,128]{2,1,0:T(8,128)(2,1)S(1)}) custom-call(s16[8,40,128]{2,1,0:T(8,128)(2,1)S(1)} %all_to_all.10.payloads, f32[488,128]{1,0:T(8,128)S(1)} %bitcast.70, f32[488,128]{1,0:T(8,128)S(1)} %bitcast.85, f32[488,128]{1,0:T(8,128)S(1)} %bitcast.86, f32[488,128]{1,0:T(8,128)S(1)} %bitcast.87, ...), custom_call_target="tpu_custom_call" | custom-call | tf_op jit(solution)/shard_map/primal_step/pallas_call | solution.py:366
  19.9 9.4 %all_to_all.11.refs_3_ = bf16[8,40,128]{2,1,0:T(8,128)(2,1)S(1)} all-to-all(bf16[8,40,128]{2,1,0:T(8,128)(2,1)S(1)} %get-tuple-element.64), channel_id=1, replica_groups=mesh['row'=8,'col'=4] {'row'}, dimensions={0} | all-to-all | bytes 163840 | tf_op jit(solution)/shard_map/all_to_all | solution.py:394
  29.3 0.0 copy-done.10
  29.3 1.7 %product.1 = (s16[144,128]{1,0:T(8,128)(2,1)S(1)}, f32[496,128]{1,0:T(8,128)S(1)}, s32[496,128]{1,0:T(8,128)S(1)}) custom-call(s32[1,128]{1,0:T(1,128)S(1)} %bitcast.91, s32[128,128]{1,0:T(8,128)S(1)} %get-tuple-element.61.refs_1_, bf16[128,128,128]{2,1,0:T(8,128)(2,1)S(1)} %get-tuple-element.62.refs_2_, bf16[8,40,128]{2,1,0:T(8,128)(2,1)S(1)} %all_to_all.11.refs_3_, ...), custom_call_target="tpu_custom_call" | custom-call | tf_op jit(solution)/shard_map/product/pallas_call | solution.py:383
  31.0 0.1 collective-permute-start.29
  31.1 1.6 %collective-permute-start.28 = (s16[144,128]{1,0:T(8,128)(2,1)S(1)}, s16[144,128]{1,0:T(8,128)(2,1)S(1)}, u32[]{:S(2)}, u32[]{:S(2)}) collective-permute-start(s16[144,128]{1,0:T(8,128)(2,1)S(1)} %get-tuple-element.66.payload), channel_id=1, source_target_pairs={{0,2},{1,3},{2,0},{3,1},{4,6},{5,7},{6,4},{7,5},{8,10},{9,11},{10,... | collective-permute-start | bytes 110600 | tf_op jit(solution)/shard_map/ppermute | solution.py:279
  32.6 0.3 collective-permute-start.27
  32.9 0.8 %own_dual_step.1.refs_3_ = f32[496,128]{1,0:T(8,128)S(1)} custom-call(s16[144,128]{1,0:T(8,128)(2,1)S(1)} %get-tuple-element.66.payload, f32[496,128]{1,0:T(8,128)S(1)} %get-tuple-element.67.duals_ref, f32[496,128]{1,0:T(8,128)S(1)} %get-tuple-element.68.right_ref, f32[2]{0:T(128)S(1)} %copy-done.9), custom_call_target="tpu_custom_call" | custom-call | flops 32505856 | bytes 1048576 | tf_op jit(solution)/shard_map/own_dual_step/pallas_call | solution.py:396
  33.7 1.1 %collective-permute-done.29.refs_2_ = s16[144,128]{1,0:T(8,128)(2,1)S(1)} collective-permute-done((s16[144,128]{1,0:T(8,128)(2,1)S(1)}, s16[144,128]{1,0:T(8,128)(2,1)S(1)}, u32[]{:S(2)}, u32[]{:S(2)}) %collective-permute-start.29) | collective-permute-done | bytes 36896 | tf_op jit(solution)/shard_map/ppermute | solution.py:279
  34.8 0.4 %collective-permute-done.28.refs_1_ = s16[144,128]{1,0:T(8,128)(2,1)S(1)} collective-permute-done((s16[144,128]{1,0:T(8,128)(2,1)S(1)}, s16[144,128]{1,0:T(8,128)(2,1)S(1)}, u32[]{:S(2)}, u32[]{:S(2)}) %collective-permute-start.28) | collective-permute-done | bytes 36896 | tf_op jit(solution)/shard_map/ppermute | solution.py:279
  35.2 0.0 collective-permute-done.27.refs_0_
  35.2 1.6 %dual_step.1 = (f32[496,128]{1,0:T(8,128)}, s32[1]{0:T(128)}) custom-call(s16[144,128]{1,0:T(8,128)(2,1)S(1)} %collective-permute-done.27.refs_0_, s16[144,128]{1,0:T(8,128)(2,1)S(1)} %collective-permute-done.28.refs_1_, s16[144,128]{1,0:T(8,128)(2,1)S(1)} %collective-permute-done.29.refs_2_, f32[496,128]{1,0:T(8,128)S(1)} %own_dual_step.1.refs_3_, ...), custom_call_target="tpu_custom_call" | custom-call | tf_op jit(solution)/shard_map/dual_step/pallas_call | solution.py:405
  37.4 0.0 copy-done
  37.4 0.0 copy-done.1
  37.5 0.0 copy-done.2
  37.5 0.0 copy-done.11
  (1 shorter events, 0.0 us)
Async XLA Ops:
  0.6 28.6 %copy-start.10 = (s32[1,1,128]{2,1,0:T(1,128)S(1)}, s32[1,1,128]{2,1,0:T(1,128)}, u32[]{:S(2)}) copy-start(s32[1,1,128]{2,1,0:T(1,128)} %param.15) | copy-start | bytes 1540
  0.6 17.5 %copy-start.9 = (f32[2]{0:T(128)S(1)}, f32[2]{0:T(128)}, u32[]{:S(2)}) copy-start(f32[2]{0:T(128)} %refs_5_.1) | copy-start | bytes 28
  0.7 17.5 %copy-start.3 = (f32[62464]{0:T(1024)S(1)}, f32[62464]{0:T(1024)}, u32[]{:S(2)}) copy-start(f32[62464]{0:T(1024)} %param.17) | copy-start | bytes 749572
  0.7 17.5 %copy-start.4 = (f32[62464]{0:T(1024)S(1)}, f32[62464]{0:T(1024)}, u32[]{:S(2)}) copy-start(f32[62464]{0:T(1024)} %param.19) | copy-start | bytes 749572
  0.7 17.5 %copy-start.5 = (f32[62464]{0:T(1024)S(1)}, f32[62464]{0:T(1024)}, u32[]{:S(2)}) copy-start(f32[62464]{0:T(1024)} %param.20) | copy-start | bytes 749572
  0.7 17.5 %copy-start.6 = (f32[62464]{0:T(1024)S(1)}, f32[62464]{0:T(1024)}, u32[]{:S(2)}) copy-start(f32[62464]{0:T(1024)} %param.21) | copy-start | bytes 749572
  0.7 17.5 %copy-start.7 = (s32[62464]{0:T(1024)S(1)}, s32[62464]{0:T(1024)}, u32[]{:S(2)}) copy-start(s32[62464]{0:T(1024)} %param.22) | copy-start | bytes 749572
  3.9 33.6 %copy-start = (f32[63488]{0:T(1024)S(1)}, f32[63488]{0:T(1024)}, u32[]{:S(2)}) copy-start(f32[63488]{0:T(1024)} %param.18) | copy-start | bytes 761860
  3.9 33.6 %copy-start.1 = (f32[63488]{0:T(1024)S(1)}, f32[63488]{0:T(1024)}, u32[]{:S(2)}) copy-start(f32[63488]{0:T(1024)} %param.23) | copy-start | bytes 761860
  3.9 33.6 %copy-start.2 = (s32[63488]{0:T(1024)S(1)}, s32[63488]{0:T(1024)}, u32[]{:S(2)}) copy-start(s32[63488]{0:T(1024)} %param.24) | copy-start | bytes 761860
  3.9 33.6 %copy-start.11 = (s32[1,1,128]{2,1,0:T(1,128)S(1)}, s32[1,1,128]{2,1,0:T(1,128)}, u32[]{:S(2)}) copy-start(s32[1,1,128]{2,1,0:T(1,128)} %param.16) | copy-start | bytes 1540
  31.0 3.8 %collective-permute-start.29 = (s16[144,128]{1,0:T(8,128)(2,1)S(1)}, s16[144,128]{1,0:T(8,128)(2,1)S(1)}, u32[]{:S(2)}, u32[]{:S(2)}) collective-permute-start(s16[144,128]{1,0:T(8,128)(2,1)S(1)} %get-tuple-element.66.payload), channel_id=1, source_target_pairs={{0,3},{1,2},{2,1},{3,0},{4,7},{5,6},{6,5},{7,4},{8,11},{9,10},{10,... | collective-permute-start | bytes 110600 | tf_op jit(solution)/shard_map/ppermute | solution.py:279
  31.1 4.2 %collective-permute-start.28 = (s16[144,128]{1,0:T(8,128)(2,1)S(1)}, s16[144,128]{1,0:T(8,128)(2,1)S(1)}, u32[]{:S(2)}, u32[]{:S(2)}) collective-permute-start(s16[144,128]{1,0:T(8,128)(2,1)S(1)} %get-tuple-element.66.payload), channel_id=1, source_target_pairs={{0,2},{1,3},{2,0},{3,1},{4,6},{5,7},{6,4},{7,5},{8,10},{9,11},{10,... | collective-permute-start | bytes 110600 | tf_op jit(solution)/shard_map/ppermute | solution.py:279
  32.6 2.6 %collective-permute-start.27 = (s16[144,128]{1,0:T(8,128)(2,1)S(1)}, s16[144,128]{1,0:T(8,128)(2,1)S(1)}, u32[]{:S(2)}, u32[]{:S(2)}) collective-permute-start(s16[144,128]{1,0:T(8,128)(2,1)S(1)} %get-tuple-element.66.payload), channel_id=1, source_target_pairs={{0,1},{1,0},{2,3},{3,2},{4,5},{5,4},{6,7},{7,6},{8,9},{9,8},{10,11... | collective-permute-start | bytes 110600 | tf_op jit(solution)/shard_map/ppermute | solution.py:279

commit v12 on v11

--- a/solution.py
+++ b/solution.py
@@ -131,22 +131,13 @@
     width = chunks * TILE
     to_lanes = where_one(iota((k_tiles, width), 1) == here)
     of_owner = where_one(iota((n_row, k_tiles), 0) == owner_across)
-    place = col_across - owner_across * owned + 1
-    place_low = jnp.bitwise_and(place, 255)
-    head_left = jnp.concatenate(
-        [of_owner * (place - place_low).astype(f32), of_owner * place_low.astype(f32), of_owner], axis=0
-    ).astype(bf16)
+    place = place_coded(col_across - owner_across * owned)
+    packed = jnp.dot((of_owner * place).astype(bf16), to_lanes.astype(bf16), preferred_element_type=f32)
 
     for chunk in range(1, len(large)):
         products_of(chunk)
-    whole, exponents = coded(jnp.concatenate(terms, axis=0))
-
-    scaled = [to_lanes, to_lanes * jnp.concatenate([exponents] * chunks, axis=1)]
-    heads = jnp.dot(head_left, jnp.concatenate(scaled, axis=1).astype(bf16), preferred_element_type=f32)
-    places = heads[:n_row, :width] + heads[n_row : 2 * n_row, :width]
-    packed = heads[2 * n_row :, width:] * place_range(owned) + places
-    both = jnp.dot(to_slots.astype(bf16), two_parts(whole), preferred_element_type=f32)
-    body = both[:, :TILE] + both[:, TILE:]
+    products = jnp.concatenate(terms, axis=0).astype(bf16)
+    body = jnp.dot(to_slots.astype(bf16), products, preferred_element_type=f32)
     top = -(-head_rows // 8) * 8
     line = iota((top, TILE), 0)
     for o in range(n_row):
@@ -154,11 +145,19 @@
         for c in range(chunks):
             head = jnp.where(line == c, packed[o : o + 1, c * TILE : (c + 1) * TILE], head)
         rows_of = body[o * SLOTS + top : (o + 1) * SLOTS]
-        out_ref[o] = jnp.concatenate([head, rows_of], axis=0).astype(i32).astype(i16)
-
-
-def place_range(owned):
-    return 1 << owned.bit_length()
+        out_ref[o] = jnp.concatenate([head, rows_of], axis=0).astype(bf16)
+
+
+def place_coded(place):
+    high = lax.shift_right_logical(place, 7)
+    return jnp.exp2((8 * high).astype(f32)) * (128 + jnp.bitwise_and(place, 127)).astype(f32)
+
+
+def place_of(number, blocks):
+    place = number - 129.0 + where_one(number >= 128.0)
+    for high in range(1, -(-blocks // TILE)):
+        place = jnp.where(number >= 2.0 ** (7 + 8 * high), number * 2.0 ** (-8 * high) - 128.0 + 128.0 * high, place)
+    return place.astype(i32)
 
 
 def primal_kernel(
@@ -169,19 +168,18 @@
     chunks, head_rows = rounds_of(n_row)
     blocks = primal_ref.shape[0]
     padded = extrap.shape[0]
-    wholes = [payloads[s].astype(i32) for s in range(n_row)]
+    arrived = [payloads[s].astype(f32) for s in range(n_row)]
     top = -(-head_rows // 8) * 8
-    head = sum(w[:top] for w in wholes)
-    flag_ref[...] = jnp.broadcast_to(head[chunks:head_rows], flag_ref.shape)
-    whole = padded_rows(wholes, chunks * TILE)
-    down = iota((blocks, TILE), 0) + 1
-    places = jnp.bitwise_and(head, place_range(blocks) - 1)
-    scales = lax.shift_right_arithmetic(head, blocks.bit_length())
-    masks, wholes = [], []
-    for c in range(chunks):
-        masks.append(scaled_mask(down, places[c : c + 1], scales[c : c + 1]))
-        wholes.append(whole[c * TILE : (c + 1) * TILE])
-    col_sums = picked_sums(masks, wholes)
+    head = sum(a[:top] for a in arrived)
+    flag_ref[...] = jnp.broadcast_to(head[chunks:head_rows], flag_ref.shape).astype(i32)
+    places = place_of(head, blocks)
+    down = iota((blocks, TILE), 0)
+    masks = [where_one(down == places[c : c + 1]) for c in range(chunks)]
+    col_sums = jnp.dot(
+        jnp.concatenate(masks, axis=1).astype(bf16),
+        padded_rows(arrived, chunks * TILE).astype(bf16),
+        preferred_element_type=f32,
+    )
     primal = primal_ref[...]
     kind = kind_ref[...]
     moved = primal - steps_ref[0] * (cost_ref[...] - col_sums)
@@ -195,7 +193,7 @@
         extrap[pl.ds(aligned, padded - aligned), :] = jnp.zeros((padded - aligned, TILE), f32)
     extrap[pl.ds(0, blocks), :] = 2.0 * moved - primal
     right = extrap[...].astype(bf16)
-    across = iota((TILE, padded), 1) + 1
+    across = iota((TILE, padded), 1)
     places = jnp.transpose(places.astype(f32)).astype(i32)
     sent = [
         jnp.dot(where_one(across == places[:, c : c + 1]).astype(bf16), right, preferred_element_type=f32)
@@ -347,7 +345,7 @@
     col_terms, slots, duals_kept, tiles_kept = pl.pallas_call(
         functools.partial(transpose_product_kernel, col_blocks),
         out_shape=(
-            jax.ShapeDtypeStruct((n_row, SLOTS, TILE), i16),
+            jax.ShapeDtypeStruct((n_row, SLOTS, TILE), bf16),
             jax.ShapeDtypeStruct((k_tiles, TILE), i32),
             *[shape_of(a) for a in own],
         ),

time: 37.7 us -> 37.6 us (level)
  no operation moved by 1% of the time
where the time goes in v12:
time: 37.6 us; the launch traced here: 37.3 us
  blocking collectives  23.6 us (63%)
  Pallas kernels  8.73 us (23%)
  starting transfers between devices  1.92 us (5%)
  waiting for transfers between devices  1.55 us (4%)
  between operations  1.46 us (4%)
    all_to_all x1, blocking collectives, local(): lax.all_to_all(col_terms, 'row', 0, 0)  14.2 us
    all_to_all x1, blocking collectives, local(): lax.all_to_all(wanted, 'row', 0, 0)  9.4 us
    pallas_call x1, Pallas kernels, local(): pl.pallas_call(functools.partial(transpose_product_kernel, col_blocks), o...  3 us
    ppermute x3, starting transfers between devices, gathered_along(): lax.ppermute(array, axis, there)  1.92 us
    pallas_call x1, Pallas kernels, local(): pl.pallas_call(product_kernel, out_shape=(jax.ShapeDtypeStruct((k_tiles +...  1.71 us
    pallas_call x1, Pallas kernels, local(): pl.pallas_call(primal_kernel, out_shape=(jax.ShapeDtypeStruct((col_blocks...  1.7 us
    pallas_call x1, Pallas kernels, local(): pl.pallas_call(dual_kernel, out_shape=(jax.ShapeDtypeStruct((row_blocks,...  1.56 us
    ppermute x3, waiting for transfers between devices, gathered_along(): lax.ppermute(array, axis, there)  1.55 us
  transfers between devices with their start and end apart: 3, of which 2 were waited for; matrix products, arithmetic and copies ran while one was open for 0% of the time, Pallas kernels for 2%

profile of v12, /device:TPU:0, one launch (start us, length us, event | category | flops | bytes accessed | tf_op | source)
XLA Modules:
  0.0 37.3 jit_solution(3834896376342574910)
XLA Ops:
  0.6 0.0 copy-start.10
  0.6 0.0 copy-start.9
  0.7 0.0 copy-start.3
  0.7 0.0 copy-start.4
  0.7 0.0 copy-start.5
  0.7 0.0 copy-start.6
  0.7 0.0 copy-start.7
  0.7 3.0 %transpose_product.1 = (bf16[8,40,128]{2,1,0:T(8,128)(2,1)S(1)}, s32[128,128]{1,0:T(8,128)S(1)}, f32[496,128]{1,0:T(8,128)S(1)}, bf16[128,128,128]{2,1,0:T(8,128)(2,1)S(1)}) custom-call(s32[128]{0:T(128)} %bitcast.90, s32[1,128]{1,0:T(1,128)} %bitcast.93, f32[496,128]{1,0:T(8,128)} %bitcast.67, bf16[128,128,128]{2,1,0:T(8,128)(2,1)} %bitcast.65), custom_call_target="tpu_custom_call" | custom-call | tf_op jit(solution)/shard_map/transpose_product/pallas_call | solution.py:345
  3.7 0.0 copy-start
  3.7 0.0 copy-start.1
  3.7 0.0 copy-start.2
  3.7 0.0 copy-start.11
  3.8 14.2 %all_to_all.10.payloads = bf16[8,40,128]{2,1,0:T(8,128)(2,1)S(1)} all-to-all(bf16[8,40,128]{2,1,0:T(8,128)(2,1)S(1)} %get-tuple-element.63), channel_id=1, replica_groups=mesh['row'=8,'col'=4] {'row'}, dimensions={0} | all-to-all | bytes 163840 | tf_op jit(solution)/shard_map/all_to_all | solution.py:380
  18.0 0.0 copy-done.9
  18.0 0.0 copy-done.3
  18.0 0.0 copy-done.4
  18.0 0.0 copy-done.5
  18.0 0.0 copy-done.6
  18.0 0.0 copy-done.7
  18.0 1.7 %primal_step.1 = (f32[488,128]{1,0:T(8,128)}, s32[8,128]{1,0:T(8,128)S(1)}, bf16[8,40,128]{2,1,0:T(8,128)(2,1)S(1)}) custom-call(bf16[8,40,128]{2,1,0:T(8,128)(2,1)S(1)} %all_to_all.10.payloads, f32[488,128]{1,0:T(8,128)S(1)} %bitcast.70, f32[488,128]{1,0:T(8,128)S(1)} %bitcast.85, f32[488,128]{1,0:T(8,128)S(1)} %bitcast.86, f32[488,128]{1,0:T(8,128)S(1)} %bitcast.87, ...), custom_call_target="tpu_custom_call" | custom-call | tf_op jit(solution)/shard_map/primal_step/pallas_call | solution.py:364
  19.7 9.4 %all_to_all.11.refs_3_ = bf16[8,40,128]{2,1,0:T(8,128)(2,1)S(1)} all-to-all(bf16[8,40,128]{2,1,0:T(8,128)(2,1)S(1)} %get-tuple-element.64), channel_id=1, replica_groups=mesh['row'=8,'col'=4] {'row'}, dimensions={0} | all-to-all | bytes 163840 | tf_op jit(solution)/shard_map/all_to_all | solution.py:392
  29.1 0.0 copy-done.10
  29.1 1.7 %product.1 = (s16[144,128]{1,0:T(8,128)(2,1)S(1)}, f32[496,128]{1,0:T(8,128)S(1)}, s32[496,128]{1,0:T(8,128)S(1)}) custom-call(s32[1,128]{1,0:T(1,128)S(1)} %bitcast.91, s32[128,128]{1,0:T(8,128)S(1)} %get-tuple-element.61.refs_1_, bf16[128,128,128]{2,1,0:T(8,128)(2,1)S(1)} %get-tuple-element.62.refs_2_, bf16[8,40,128]{2,1,0:T(8,128)(2,1)S(1)} %all_to_all.11.refs_3_, ...), custom_call_target="tpu_custom_call" | custom-call | tf_op jit(solution)/shard_map/product/pallas_call | solution.py:381
  30.9 0.1 collective-permute-start.29
  30.9 1.6 %collective-permute-start.28 = (s16[144,128]{1,0:T(8,128)(2,1)S(1)}, s16[144,128]{1,0:T(8,128)(2,1)S(1)}, u32[]{:S(2)}, u32[]{:S(2)}) collective-permute-start(s16[144,128]{1,0:T(8,128)(2,1)S(1)} %get-tuple-element.66.payload), channel_id=1, source_target_pairs={{0,2},{1,3},{2,0},{3,1},{4,6},{5,7},{6,4},{7,5},{8,10},{9,11},{10,... | collective-permute-start | bytes 110600 | tf_op jit(solution)/shard_map/ppermute | solution.py:277
  32.5 0.3 collective-permute-start.27
  32.8 0.8 %own_dual_step.1.refs_3_ = f32[496,128]{1,0:T(8,128)S(1)} custom-call(s16[144,128]{1,0:T(8,128)(2,1)S(1)} %get-tuple-element.66.payload, f32[496,128]{1,0:T(8,128)S(1)} %get-tuple-element.67.duals_ref, f32[496,128]{1,0:T(8,128)S(1)} %get-tuple-element.68.right_ref, f32[2]{0:T(128)S(1)} %copy-done.9), custom_call_target="tpu_custom_call" | custom-call | flops 32505856 | bytes 1048576 | tf_op jit(solution)/shard_map/own_dual_step/pallas_call | solution.py:394
  33.5 1.1 %collective-permute-done.29.refs_2_ = s16[144,128]{1,0:T(8,128)(2,1)S(1)} collective-permute-done((s16[144,128]{1,0:T(8,128)(2,1)S(1)}, s16[144,128]{1,0:T(8,128)(2,1)S(1)}, u32[]{:S(2)}, u32[]{:S(2)}) %collective-permute-start.29) | collective-permute-done | bytes 36896 | tf_op jit(solution)/shard_map/ppermute | solution.py:277
  34.6 0.4 %collective-permute-done.28.refs_1_ = s16[144,128]{1,0:T(8,128)(2,1)S(1)} collective-permute-done((s16[144,128]{1,0:T(8,128)(2,1)S(1)}, s16[144,128]{1,0:T(8,128)(2,1)S(1)}, u32[]{:S(2)}, u32[]{:S(2)}) %collective-permute-start.28) | collective-permute-done | bytes 36896 | tf_op jit(solution)/shard_map/ppermute | solution.py:277
  35.1 0.0 collective-permute-done.27.refs_0_
  35.1 1.6 %dual_step.1 = (f32[496,128]{1,0:T(8,128)}, s32[1]{0:T(128)}) custom-call(s16[144,128]{1,0:T(8,128)(2,1)S(1)} %collective-permute-done.27.refs_0_, s16[144,128]{1,0:T(8,128)(2,1)S(1)} %collective-permute-done.28.refs_1_, s16[144,128]{1,0:T(8,128)(2,1)S(1)} %collective-permute-done.29.refs_2_, f32[496,128]{1,0:T(8,128)S(1)} %own_dual_step.1.refs_3_, ...), custom_call_target="tpu_custom_call" | custom-call | tf_op jit(solution)/shard_map/dual_step/pallas_call | solution.py:403
  37.3 0.0 copy-done
  37.3 0.0 copy-done.1
  37.3 0.0 copy-done.2
  37.3 0.0 copy-done.11
  (1 shorter events, 0.0 us)
Async XLA Ops:
  0.6 28.5 %copy-start.10 = (s32[1,1,128]{2,1,0:T(1,128)S(1)}, s32[1,1,128]{2,1,0:T(1,128)}, u32[]{:S(2)}) copy-start(s32[1,1,128]{2,1,0:T(1,128)} %param.15) | copy-start | bytes 1540
  0.6 17.3 %copy-start.9 = (f32[2]{0:T(128)S(1)}, f32[2]{0:T(128)}, u32[]{:S(2)}) copy-start(f32[2]{0:T(128)} %refs_5_.1) | copy-start | bytes 28
  0.7 17.3 %copy-start.3 = (f32[62464]{0:T(1024)S(1)}, f32[62464]{0:T(1024)}, u32[]{:S(2)}) copy-start(f32[62464]{0:T(1024)} %param.17) | copy-start | bytes 749572
  0.7 17.3 %copy-start.4 = (f32[62464]{0:T(1024)S(1)}, f32[62464]{0:T(1024)}, u32[]{:S(2)}) copy-start(f32[62464]{0:T(1024)} %param.19) | copy-start | bytes 749572
  0.7 17.3 %copy-start.5 = (f32[62464]{0:T(1024)S(1)}, f32[62464]{0:T(1024)}, u32[]{:S(2)}) copy-start(f32[62464]{0:T(1024)} %param.20) | copy-start | bytes 749572
  0.7 17.3 %copy-start.6 = (f32[62464]{0:T(1024)S(1)}, f32[62464]{0:T(1024)}, u32[]{:S(2)}) copy-start(f32[62464]{0:T(1024)} %param.21) | copy-start | bytes 749572
  0.7 17.3 %copy-start.7 = (s32[62464]{0:T(1024)S(1)}, s32[62464]{0:T(1024)}, u32[]{:S(2)}) copy-start(s32[62464]{0:T(1024)} %param.22) | copy-start | bytes 749572
  3.7 33.6 %copy-start = (f32[63488]{0:T(1024)S(1)}, f32[63488]{0:T(1024)}, u32[]{:S(2)}) copy-start(f32[63488]{0:T(1024)} %param.18) | copy-start | bytes 761860
  3.7 33.6 %copy-start.1 = (f32[63488]{0:T(1024)S(1)}, f32[63488]{0:T(1024)}, u32[]{:S(2)}) copy-start(f32[63488]{0:T(1024)} %param.23) | copy-start | bytes 761860
  3.7 33.6 %copy-start.2 = (s32[63488]{0:T(1024)S(1)}, s32[63488]{0:T(1024)}, u32[]{:S(2)}) copy-start(s32[63488]{0:T(1024)} %param.24) | copy-start | bytes 761860
  3.7 33.6 %copy-start.11 = (s32[1,1,128]{2,1,0:T(1,128)S(1)}, s32[1,1,128]{2,1,0:T(1,128)}, u32[]{:S(2)}) copy-start(s32[1,1,128]{2,1,0:T(1,128)} %param.16) | copy-start | bytes 1540
  30.9 3.8 %collective-permute-start.29 = (s16[144,128]{1,0:T(8,128)(2,1)S(1)}, s16[144,128]{1,0:T(8,128)(2,1)S(1)}, u32[]{:S(2)}, u32[]{:S(2)}) collective-permute-start(s16[144,128]{1,0:T(8,128)(2,1)S(1)} %get-tuple-element.66.payload), channel_id=1, source_target_pairs={{0,3},{1,2},{2,1},{3,0},{4,7},{5,6},{6,5},{7,4},{8,11},{9,10},{10,... | collective-permute-start | bytes 110600 | tf_op jit(solution)/shard_map/ppermute | solution.py:277
  30.9 4.2 %collective-permute-start.28 = (s16[144,128]{1,0:T(8,128)(2,1)S(1)}, s16[144,128]{1,0:T(8,128)(2,1)S(1)}, u32[]{:S(2)}, u32[]{:S(2)}) collective-permute-start(s16[144,128]{1,0:T(8,128)(2,1)S(1)} %get-tuple-element.66.payload), channel_id=1, source_target_pairs={{0,2},{1,3},{2,0},{3,1},{4,6},{5,7},{6,4},{7,5},{8,10},{9,11},{10,... | collective-permute-start | bytes 110600 | tf_op jit(solution)/shard_map/ppermute | solution.py:277
  32.5 2.6 %collective-permute-start.27 = (s16[144,128]{1,0:T(8,128)(2,1)S(1)}, s16[144,128]{1,0:T(8,128)(2,1)S(1)}, u32[]{:S(2)}, u32[]{:S(2)}) collective-permute-start(s16[144,128]{1,0:T(8,128)(2,1)S(1)} %get-tuple-element.66.payload), channel_id=1, source_target_pairs={{0,1},{1,0},{2,3},{3,2},{4,5},{5,4},{6,7},{7,6},{8,9},{9,8},{10,11... | collective-permute-start | bytes 110600 | tf_op jit(solution)/shard_map/ppermute | solution.py:277

commit v13 on v11

--- a/solution.py
+++ b/solution.py
@@ -8,7 +8,7 @@
 
 TILE = 128
 GROUP = 16
-CHUNK = 64
+CHUNK = 128
 SLOTS = 40
 HEAD = 16
 BITS = 14

time: 37.7 us -> 38 us (level)
  no operation moved by 1% of the time
where the time goes in v13:
time: 38 us; the launch traced here: 37.8 us
  blocking collectives  23.6 us (62%)
  Pallas kernels  9.15 us (24%)
  starting transfers between devices  1.92 us (5%)
  waiting for transfers between devices  1.55 us (4%)
  between operations  1.46 us (4%)
    all_to_all x1, blocking collectives, local(): lax.all_to_all(col_terms, 'row', 0, 0)  14.2 us
    all_to_all x1, blocking collectives, local(): lax.all_to_all(wanted, 'row', 0, 0)  9.4 us
    pallas_call x1, Pallas kernels, local(): pl.pallas_call(functools.partial(transpose_product_kernel, col_blocks), o...  3.43 us
    ppermute x3, starting transfers between devices, gathered_along(): lax.ppermute(array, axis, there)  1.92 us
    pallas_call x1, Pallas kernels, local(): pl.pallas_call(product_kernel, out_shape=(jax.ShapeDtypeStruct((k_tiles +...  1.71 us
    pallas_call x1, Pallas kernels, local(): pl.pallas_call(primal_kernel, out_shape=(jax.ShapeDtypeStruct((col_blocks...  1.69 us
    pallas_call x1, Pallas kernels, local(): pl.pallas_call(dual_kernel, out_shape=(jax.ShapeDtypeStruct((row_blocks,...  1.56 us
    ppermute x3, waiting for transfers between devices, gathered_along(): lax.ppermute(array, axis, there)  1.55 us
  transfers between devices with their start and end apart: 3, of which 2 were waited for; matrix products, arithmetic and copies ran while one was open for 0% of the time, Pallas kernels for 2%

profile of v13, /device:TPU:0, one launch (start us, length us, event | category | flops | bytes accessed | tf_op | source)
XLA Modules:
  0.0 37.8 jit_solution(16595466659749263283)
XLA Ops:
  0.6 0.0 copy-start.10
  0.6 0.0 copy-start.9
  0.7 0.0 copy-start.3
  0.7 0.0 copy-start.4
  0.7 0.0 copy-start.5
  0.7 0.0 copy-start.6
  0.7 0.0 copy-start.7
  0.7 3.4 %transpose_product.1 = (s16[8,40,128]{2,1,0:T(8,128)(2,1)S(1)}, s32[128,128]{1,0:T(8,128)S(1)}, f32[496,128]{1,0:T(8,128)S(1)}, bf16[128,128,128]{2,1,0:T(8,128)(2,1)S(1)}) custom-call(s32[128]{0:T(128)} %bitcast.90, s32[1,128]{1,0:T(1,128)} %bitcast.93, f32[496,128]{1,0:T(8,128)} %bitcast.67, bf16[128,128,128]{2,1,0:T(8,128)(2,1)} %bitcast.65), custom_call_target="tpu_custom_call" | custom-call | tf_op jit(solution)/shard_map/transpose_product/pallas_call | solution.py:347
  4.1 0.0 copy-start
  4.2 0.0 copy-start.1
  4.2 0.0 copy-start.2
  4.2 0.0 copy-start.11
  4.2 14.2 %all_to_all.10.payloads = s16[8,40,128]{2,1,0:T(8,128)(2,1)S(1)} all-to-all(s16[8,40,128]{2,1,0:T(8,128)(2,1)S(1)} %get-tuple-element.63), channel_id=1, replica_groups=mesh['row'=8,'col'=4] {'row'}, dimensions={0} | all-to-all | bytes 163840 | tf_op jit(solution)/shard_map/all_to_all | solution.py:382
  18.4 0.0 copy-done.9
  18.4 0.0 copy-done.3
  18.4 0.0 copy-done.4
  18.4 0.0 copy-done.5
  18.4 0.0 copy-done.6
  18.4 0.0 copy-done.7
  18.5 1.7 %primal_step.1 = (f32[488,128]{1,0:T(8,128)}, s32[8,128]{1,0:T(8,128)S(1)}, bf16[8,40,128]{2,1,0:T(8,128)(2,1)S(1)}) custom-call(s16[8,40,128]{2,1,0:T(8,128)(2,1)S(1)} %all_to_all.10.payloads, f32[488,128]{1,0:T(8,128)S(1)} %bitcast.70, f32[488,128]{1,0:T(8,128)S(1)} %bitcast.85, f32[488,128]{1,0:T(8,128)S(1)} %bitcast.86, f32[488,128]{1,0:T(8,128)S(1)} %bitcast.87, ...), custom_call_target="tpu_custom_call" | custom-call | tf_op jit(solution)/shard_map/primal_step/pallas_call | solution.py:366
  20.2 9.4 %all_to_all.11.refs_3_ = bf16[8,40,128]{2,1,0:T(8,128)(2,1)S(1)} all-to-all(bf16[8,40,128]{2,1,0:T(8,128)(2,1)S(1)} %get-tuple-element.64), channel_id=1, replica_groups=mesh['row'=8,'col'=4] {'row'}, dimensions={0} | all-to-all | bytes 163840 | tf_op jit(solution)/shard_map/all_to_all | solution.py:394
  29.6 0.0 copy-done.10
  29.6 1.7 %product.1 = (s16[144,128]{1,0:T(8,128)(2,1)S(1)}, f32[496,128]{1,0:T(8,128)S(1)}, s32[496,128]{1,0:T(8,128)S(1)}) custom-call(s32[1,128]{1,0:T(1,128)S(1)} %bitcast.91, s32[128,128]{1,0:T(8,128)S(1)} %get-tuple-element.61.refs_1_, bf16[128,128,128]{2,1,0:T(8,128)(2,1)S(1)} %get-tuple-element.62.refs_2_, bf16[8,40,128]{2,1,0:T(8,128)(2,1)S(1)} %all_to_all.11.refs_3_, ...), custom_call_target="tpu_custom_call" | custom-call | tf_op jit(solution)/shard_map/product/pallas_call | solution.py:383
  31.3 0.1 collective-permute-start.29
  31.4 1.6 %collective-permute-start.28 = (s16[144,128]{1,0:T(8,128)(2,1)S(1)}, s16[144,128]{1,0:T(8,128)(2,1)S(1)}, u32[]{:S(2)}, u32[]{:S(2)}) collective-permute-start(s16[144,128]{1,0:T(8,128)(2,1)S(1)} %get-tuple-element.66.payload), channel_id=1, source_target_pairs={{0,2},{1,3},{2,0},{3,1},{4,6},{5,7},{6,4},{7,5},{8,10},{9,11},{10,... | collective-permute-start | bytes 110600 | tf_op jit(solution)/shard_map/ppermute | solution.py:279
  32.9 0.3 collective-permute-start.27
  33.2 0.8 %own_dual_step.1.refs_3_ = f32[496,128]{1,0:T(8,128)S(1)} custom-call(s16[144,128]{1,0:T(8,128)(2,1)S(1)} %get-tuple-element.66.payload, f32[496,128]{1,0:T(8,128)S(1)} %get-tuple-element.67.duals_ref, f32[496,128]{1,0:T(8,128)S(1)} %get-tuple-element.68.right_ref, f32[2]{0:T(128)S(1)} %copy-done.9), custom_call_target="tpu_custom_call" | custom-call | flops 32505856 | bytes 1048576 | tf_op jit(solution)/shard_map/own_dual_step/pallas_call | solution.py:396
  34.0 1.1 %collective-permute-done.29.refs_2_ = s16[144,128]{1,0:T(8,128)(2,1)S(1)} collective-permute-done((s16[144,128]{1,0:T(8,128)(2,1)S(1)}, s16[144,128]{1,0:T(8,128)(2,1)S(1)}, u32[]{:S(2)}, u32[]{:S(2)}) %collective-permute-start.29) | collective-permute-done | bytes 36896 | tf_op jit(solution)/shard_map/ppermute | solution.py:279
  35.1 0.4 %collective-permute-done.28.refs_1_ = s16[144,128]{1,0:T(8,128)(2,1)S(1)} collective-permute-done((s16[144,128]{1,0:T(8,128)(2,1)S(1)}, s16[144,128]{1,0:T(8,128)(2,1)S(1)}, u32[]{:S(2)}, u32[]{:S(2)}) %collective-permute-start.28) | collective-permute-done | bytes 36896 | tf_op jit(solution)/shard_map/ppermute | solution.py:279
  35.5 0.0 collective-permute-done.27.refs_0_
  35.5 1.6 %dual_step.1 = (f32[496,128]{1,0:T(8,128)}, s32[1]{0:T(128)}) custom-call(s16[144,128]{1,0:T(8,128)(2,1)S(1)} %collective-permute-done.27.refs_0_, s16[144,128]{1,0:T(8,128)(2,1)S(1)} %collective-permute-done.28.refs_1_, s16[144,128]{1,0:T(8,128)(2,1)S(1)} %collective-permute-done.29.refs_2_, f32[496,128]{1,0:T(8,128)S(1)} %own_dual_step.1.refs_3_, ...), custom_call_target="tpu_custom_call" | custom-call | tf_op jit(solution)/shard_map/dual_step/pallas_call | solution.py:405
  37.7 0.0 copy-done
  37.7 0.0 copy-done.1
  37.7 0.0 copy-done.2
  37.8 0.0 copy-done.11
  (1 shorter events, 0.0 us)
Async XLA Ops:
  0.6 28.9 %copy-start.10 = (s32[1,1,128]{2,1,0:T(1,128)S(1)}, s32[1,1,128]{2,1,0:T(1,128)}, u32[]{:S(2)}) copy-start(s32[1,1,128]{2,1,0:T(1,128)} %param.15) | copy-start | bytes 1540
  0.6 17.8 %copy-start.9 = (f32[2]{0:T(128)S(1)}, f32[2]{0:T(128)}, u32[]{:S(2)}) copy-start(f32[2]{0:T(128)} %refs_5_.1) | copy-start | bytes 28
  0.7 17.8 %copy-start.3 = (f32[62464]{0:T(1024)S(1)}, f32[62464]{0:T(1024)}, u32[]{:S(2)}) copy-start(f32[62464]{0:T(1024)} %param.17) | copy-start | bytes 749572
  0.7 17.8 %copy-start.4 = (f32[62464]{0:T(1024)S(1)}, f32[62464]{0:T(1024)}, u32[]{:S(2)}) copy-start(f32[62464]{0:T(1024)} %param.19) | copy-start | bytes 749572
  0.7 17.8 %copy-start.5 = (f32[62464]{0:T(1024)S(1)}, f32[62464]{0:T(1024)}, u32[]{:S(2)}) copy-start(f32[62464]{0:T(1024)} %param.20) | copy-start | bytes 749572
  0.7 17.8 %copy-start.6 = (f32[62464]{0:T(1024)S(1)}, f32[62464]{0:T(1024)}, u32[]{:S(2)}) copy-start(f32[62464]{0:T(1024)} %param.21) | copy-start | bytes 749572
  0.7 17.8 %copy-start.7 = (s32[62464]{0:T(1024)S(1)}, s32[62464]{0:T(1024)}, u32[]{:S(2)}) copy-start(s32[62464]{0:T(1024)} %param.22) | copy-start | bytes 749572
  4.1 33.6 %copy-start = (f32[63488]{0:T(1024)S(1)}, f32[63488]{0:T(1024)}, u32[]{:S(2)}) copy-start(f32[63488]{0:T(1024)} %param.18) | copy-start | bytes 761860
  4.2 33.6 %copy-start.1 = (f32[63488]{0:T(1024)S(1)}, f32[63488]{0:T(1024)}, u32[]{:S(2)}) copy-start(f32[63488]{0:T(1024)} %param.23) | copy-start | bytes 761860
  4.2 33.6 %copy-start.2 = (s32[63488]{0:T(1024)S(1)}, s32[63488]{0:T(1024)}, u32[]{:S(2)}) copy-start(s32[63488]{0:T(1024)} %param.24) | copy-start | bytes 761860
  4.2 33.6 %copy-start.11 = (s32[1,1,128]{2,1,0:T(1,128)S(1)}, s32[1,1,128]{2,1,0:T(1,128)}, u32[]{:S(2)}) copy-start(s32[1,1,128]{2,1,0:T(1,128)} %param.16) | copy-start | bytes 1540
  31.3 3.8 %collective-permute-start.29 = (s16[144,128]{1,0:T(8,128)(2,1)S(1)}, s16[144,128]{1,0:T(8,128)(2,1)S(1)}, u32[]{:S(2)}, u32[]{:S(2)}) collective-permute-start(s16[144,128]{1,0:T(8,128)(2,1)S(1)} %get-tuple-element.66.payload), channel_id=1, source_target_pairs={{0,3},{1,2},{2,1},{3,0},{4,7},{5,6},{6,5},{7,4},{8,11},{9,10},{10,... | collective-permute-start | bytes 110600 | tf_op jit(solution)/shard_map/ppermute | solution.py:279
  31.4 4.2 %collective-permute-start.28 = (s16[144,128]{1,0:T(8,128)(2,1)S(1)}, s16[144,128]{1,0:T(8,128)(2,1)S(1)}, u32[]{:S(2)}, u32[]{:S(2)}) collective-permute-start(s16[144,128]{1,0:T(8,128)(2,1)S(1)} %get-tuple-element.66.payload), channel_id=1, source_target_pairs={{0,2},{1,3},{2,0},{3,1},{4,6},{5,7},{6,4},{7,5},{8,10},{9,11},{10,... | collective-permute-start | bytes 110600 | tf_op jit(solution)/shard_map/ppermute | solution.py:279
  32.9 2.6 %collective-permute-start.27 = (s16[144,128]{1,0:T(8,128)(2,1)S(1)}, s16[144,128]{1,0:T(8,128)(2,1)S(1)}, u32[]{:S(2)}, u32[]{:S(2)}) collective-permute-start(s16[144,128]{1,0:T(8,128)(2,1)S(1)} %get-tuple-element.66.payload), channel_id=1, source_target_pairs={{0,1},{1,0},{2,3},{3,2},{4,5},{5,4},{6,7},{7,6},{8,9},{9,8},{10,11... | collective-permute-start | bytes 110600 | tf_op jit(solution)/shard_map/ppermute | solution.py:279

commit v14 on v11

--- a/solution.py
+++ b/solution.py
@@ -259,11 +259,11 @@
 
 
 def dual_kernel(*refs):
-    payloads, (part_ref, kind_ref, steps_ref, next_ref, flag_ref) = refs[:-5], refs[-5:]
+    payloads, (part_ref, kind_ref, own_flag_ref, steps_ref, next_ref, flag_ref) = refs[:-6], refs[-6:]
     row_sums, flags = row_sums_of(payloads, part_ref.shape[0])
     updated = part_ref[...] - steps_ref[1] * row_sums
     next_ref[...] = jnp.where(kind_ref[...] == 1, jnp.maximum(updated, 0.0), updated)
-    flag_ref[0] = jnp.max(flags)
+    flag_ref[0] = jnp.max(flags + own_flag_ref[0:1, :])
 
 
 def partners(axis):
@@ -405,11 +405,11 @@
     dual_next, too_many = pl.pallas_call(
         dual_kernel,
         out_shape=(jax.ShapeDtypeStruct((row_blocks, TILE), f32), jax.ShapeDtypeStruct((1,), i32)),
-        in_specs=[VMEM] * (n_col + 1) + [SMEM],
+        in_specs=[VMEM] * (n_col + 2) + [SMEM],
         out_specs=(VMEM, SMEM),
         compiler_params=params,
         name="dual_step",
-    )(*others, part, dual_kept[1], step_sizes)
+    )(*others, part, dual_kept[1], flag, step_sizes)
     vectors = (primal, duals, cost_vec, lower_bound, upper_bound, bound_kind, right_side, row_kind, step_sizes)
     return lax.cond(
         too_many[0] > 0,

time: 37.7 us -> 37.7 us (level)
  no operation moved by 1% of the time
where the time goes in v14:
time: 37.7 us; the launch traced here: 37.5 us
  blocking collectives  23.6 us (63%)
  Pallas kernels  8.86 us (24%)
  starting transfers between devices  1.92 us (5%)
  waiting for transfers between devices  1.55 us (4%)
  between operations  1.46 us (4%)
    all_to_all x1, blocking collectives, local(): lax.all_to_all(col_terms, 'row', 0, 0)  14.2 us
    all_to_all x1, blocking collectives, local(): lax.all_to_all(wanted, 'row', 0, 0)  9.4 us
    pallas_call x1, Pallas kernels, local(): pl.pallas_call(functools.partial(transpose_product_kernel, col_blocks), o...  3.14 us
    ppermute x3, starting transfers between devices, gathered_along(): lax.ppermute(array, axis, there)  1.92 us
    pallas_call x1, Pallas kernels, local(): pl.pallas_call(product_kernel, out_shape=(jax.ShapeDtypeStruct((k_tiles +...  1.71 us
    pallas_call x1, Pallas kernels, local(): pl.pallas_call(primal_kernel, out_shape=(jax.ShapeDtypeStruct((col_blocks...  1.69 us
    pallas_call x1, Pallas kernels, local(): pl.pallas_call(dual_kernel, out_shape=(jax.ShapeDtypeStruct((row_blocks,...  1.56 us
    ppermute x3, waiting for transfers between devices, gathered_along(): lax.ppermute(array, axis, there)  1.55 us
  transfers between devices with their start and end apart: 3, of which 2 were waited for; matrix products, arithmetic and copies ran while one was open for 0% of the time, Pallas kernels for 2%

profile of v14, /device:TPU:0, one launch (start us, length us, event | category | flops | bytes accessed | tf_op | source)
XLA Modules:
  0.0 37.5 jit_solution(12394433859855223872)
XLA Ops:
  0.6 0.0 copy-start.10
  0.6 0.0 copy-start.9
  0.7 0.0 copy-start.3
  0.7 0.0 copy-start.4
  0.7 0.0 copy-start.5
  0.7 0.0 copy-start.6
  0.7 0.0 copy-start.7
  0.7 3.1 %transpose_product.1 = (s16[8,40,128]{2,1,0:T(8,128)(2,1)S(1)}, s32[128,128]{1,0:T(8,128)S(1)}, f32[496,128]{1,0:T(8,128)S(1)}, bf16[128,128,128]{2,1,0:T(8,128)(2,1)S(1)}) custom-call(s32[128]{0:T(128)} %bitcast.90, s32[1,128]{1,0:T(1,128)} %bitcast.93, f32[496,128]{1,0:T(8,128)} %bitcast.67, bf16[128,128,128]{2,1,0:T(8,128)(2,1)} %bitcast.65), custom_call_target="tpu_custom_call" | custom-call | tf_op jit(solution)/shard_map/transpose_product/pallas_call | solution.py:347
  3.9 0.0 copy-start
  3.9 0.0 copy-start.1
  3.9 0.0 copy-start.2
  3.9 0.0 copy-start.11
  3.9 14.2 %all_to_all.10.payloads = s16[8,40,128]{2,1,0:T(8,128)(2,1)S(1)} all-to-all(s16[8,40,128]{2,1,0:T(8,128)(2,1)S(1)} %get-tuple-element.63), channel_id=1, replica_groups=mesh['row'=8,'col'=4] {'row'}, dimensions={0} | all-to-all | bytes 163840 | tf_op jit(solution)/shard_map/all_to_all | solution.py:382
  18.1 0.0 copy-done.9
  18.1 0.0 copy-done.3
  18.1 0.0 copy-done.4
  18.1 0.0 copy-done.5
  18.2 0.0 copy-done.6
  18.2 0.0 copy-done.7
  18.2 1.7 %primal_step.1 = (f32[488,128]{1,0:T(8,128)}, s32[8,128]{1,0:T(8,128)S(1)}, bf16[8,40,128]{2,1,0:T(8,128)(2,1)S(1)}) custom-call(s16[8,40,128]{2,1,0:T(8,128)(2,1)S(1)} %all_to_all.10.payloads, f32[488,128]{1,0:T(8,128)S(1)} %bitcast.70, f32[488,128]{1,0:T(8,128)S(1)} %bitcast.85, f32[488,128]{1,0:T(8,128)S(1)} %bitcast.86, f32[488,128]{1,0:T(8,128)S(1)} %bitcast.87, ...), custom_call_target="tpu_custom_call" | custom-call | tf_op jit(solution)/shard_map/primal_step/pallas_call | solution.py:366
  19.9 9.4 %all_to_all.11.refs_3_ = bf16[8,40,128]{2,1,0:T(8,128)(2,1)S(1)} all-to-all(bf16[8,40,128]{2,1,0:T(8,128)(2,1)S(1)} %get-tuple-element.64), channel_id=1, replica_groups=mesh['row'=8,'col'=4] {'row'}, dimensions={0} | all-to-all | bytes 163840 | tf_op jit(solution)/shard_map/all_to_all | solution.py:394
  29.3 0.0 copy-done.10
  29.3 1.7 %product.1 = (s16[144,128]{1,0:T(8,128)(2,1)S(1)}, f32[496,128]{1,0:T(8,128)S(1)}, s32[496,128]{1,0:T(8,128)S(1)}) custom-call(s32[1,128]{1,0:T(1,128)S(1)} %bitcast.91, s32[128,128]{1,0:T(8,128)S(1)} %get-tuple-element.61.refs_1_, bf16[128,128,128]{2,1,0:T(8,128)(2,1)S(1)} %get-tuple-element.62.refs_2_, bf16[8,40,128]{2,1,0:T(8,128)(2,1)S(1)} %all_to_all.11.refs_3_, ...), custom_call_target="tpu_custom_call" | custom-call | tf_op jit(solution)/shard_map/product/pallas_call | solution.py:383
  31.0 0.1 collective-permute-start.29
  31.1 1.6 %collective-permute-start.28 = (s16[144,128]{1,0:T(8,128)(2,1)S(1)}, s16[144,128]{1,0:T(8,128)(2,1)S(1)}, u32[]{:S(2)}, u32[]{:S(2)}) collective-permute-start(s16[144,128]{1,0:T(8,128)(2,1)S(1)} %get-tuple-element.66.payload), channel_id=1, source_target_pairs={{0,2},{1,3},{2,0},{3,1},{4,6},{5,7},{6,4},{7,5},{8,10},{9,11},{10,... | collective-permute-start | bytes 110600 | tf_op jit(solution)/shard_map/ppermute | solution.py:279
  32.6 0.3 collective-permute-start.27
  32.9 0.8 %own_dual_step.1.refs_3_ = f32[496,128]{1,0:T(8,128)S(1)} custom-call(s16[144,128]{1,0:T(8,128)(2,1)S(1)} %get-tuple-element.66.payload, f32[496,128]{1,0:T(8,128)S(1)} %get-tuple-element.67.duals_ref, f32[496,128]{1,0:T(8,128)S(1)} %get-tuple-element.68.right_ref, f32[2]{0:T(128)S(1)} %copy-done.9), custom_call_target="tpu_custom_call" | custom-call | flops 32505856 | bytes 1048576 | tf_op jit(solution)/shard_map/own_dual_step/pallas_call | solution.py:396
  33.7 1.1 %collective-permute-done.29.refs_2_ = s16[144,128]{1,0:T(8,128)(2,1)S(1)} collective-permute-done((s16[144,128]{1,0:T(8,128)(2,1)S(1)}, s16[144,128]{1,0:T(8,128)(2,1)S(1)}, u32[]{:S(2)}, u32[]{:S(2)}) %collective-permute-start.29) | collective-permute-done | bytes 36896 | tf_op jit(solution)/shard_map/ppermute | solution.py:279
  34.8 0.4 %collective-permute-done.28.refs_1_ = s16[144,128]{1,0:T(8,128)(2,1)S(1)} collective-permute-done((s16[144,128]{1,0:T(8,128)(2,1)S(1)}, s16[144,128]{1,0:T(8,128)(2,1)S(1)}, u32[]{:S(2)}, u32[]{:S(2)}) %collective-permute-start.28) | collective-permute-done | bytes 36896 | tf_op jit(solution)/shard_map/ppermute | solution.py:279
  35.2 0.0 collective-permute-done.27.refs_0_
  35.2 1.6 %dual_step.1 = (f32[496,128]{1,0:T(8,128)}, s32[1]{0:T(128)}) custom-call(s16[144,128]{1,0:T(8,128)(2,1)S(1)} %collective-permute-done.27.refs_0_, s16[144,128]{1,0:T(8,128)(2,1)S(1)} %collective-permute-done.28.refs_1_, s16[144,128]{1,0:T(8,128)(2,1)S(1)} %collective-permute-done.29.refs_2_, f32[496,128]{1,0:T(8,128)S(1)} %own_dual_step.1.refs_3_, ...), custom_call_target="tpu_custom_call" | custom-call | tf_op jit(solution)/shard_map/dual_step/pallas_call | solution.py:405
  37.4 0.0 copy-done
  37.4 0.0 copy-done.1
  37.5 0.0 copy-done.2
  37.5 0.0 copy-done.11
  (1 shorter events, 0.0 us)
Async XLA Ops:
  0.6 28.6 %copy-start.10 = (s32[1,1,128]{2,1,0:T(1,128)S(1)}, s32[1,1,128]{2,1,0:T(1,128)}, u32[]{:S(2)}) copy-start(s32[1,1,128]{2,1,0:T(1,128)} %param.15) | copy-start | bytes 1540
  0.6 17.5 %copy-start.9 = (f32[2]{0:T(128)S(1)}, f32[2]{0:T(128)}, u32[]{:S(2)}) copy-start(f32[2]{0:T(128)} %refs_6_.1) | copy-start | bytes 28
  0.7 17.5 %copy-start.3 = (f32[62464]{0:T(1024)S(1)}, f32[62464]{0:T(1024)}, u32[]{:S(2)}) copy-start(f32[62464]{0:T(1024)} %param.17) | copy-start | bytes 749572
  0.7 17.5 %copy-start.4 = (f32[62464]{0:T(1024)S(1)}, f32[62464]{0:T(1024)}, u32[]{:S(2)}) copy-start(f32[62464]{0:T(1024)} %param.19) | copy-start | bytes 749572
  0.7 17.5 %copy-start.5 = (f32[62464]{0:T(1024)S(1)}, f32[62464]{0:T(1024)}, u32[]{:S(2)}) copy-start(f32[62464]{0:T(1024)} %param.20) | copy-start | bytes 749572
  0.7 17.5 %copy-start.6 = (f32[62464]{0:T(1024)S(1)}, f32[62464]{0:T(1024)}, u32[]{:S(2)}) copy-start(f32[62464]{0:T(1024)} %param.21) | copy-start | bytes 749572
  0.7 17.5 %copy-start.7 = (s32[62464]{0:T(1024)S(1)}, s32[62464]{0:T(1024)}, u32[]{:S(2)}) copy-start(s32[62464]{0:T(1024)} %param.22) | copy-start | bytes 749572
  3.9 33.6 %copy-start = (f32[63488]{0:T(1024)S(1)}, f32[63488]{0:T(1024)}, u32[]{:S(2)}) copy-start(f32[63488]{0:T(1024)} %param.18) | copy-start | bytes 761860
  3.9 33.6 %copy-start.1 = (f32[63488]{0:T(1024)S(1)}, f32[63488]{0:T(1024)}, u32[]{:S(2)}) copy-start(f32[63488]{0:T(1024)} %param.23) | copy-start | bytes 761860
  3.9 33.6 %copy-start.2 = (s32[63488]{0:T(1024)S(1)}, s32[63488]{0:T(1024)}, u32[]{:S(2)}) copy-start(s32[63488]{0:T(1024)} %param.24) | copy-start | bytes 761860
  3.9 33.6 %copy-start.11 = (s32[1,1,128]{2,1,0:T(1,128)S(1)}, s32[1,1,128]{2,1,0:T(1,128)}, u32[]{:S(2)}) copy-start(s32[1,1,128]{2,1,0:T(1,128)} %param.16) | copy-start | bytes 1540
  31.0 3.8 %collective-permute-start.29 = (s16[144,128]{1,0:T(8,128)(2,1)S(1)}, s16[144,128]{1,0:T(8,128)(2,1)S(1)}, u32[]{:S(2)}, u32[]{:S(2)}) collective-permute-start(s16[144,128]{1,0:T(8,128)(2,1)S(1)} %get-tuple-element.66.payload), channel_id=1, source_target_pairs={{0,3},{1,2},{2,1},{3,0},{4,7},{5,6},{6,5},{7,4},{8,11},{9,10},{10,... | collective-permute-start | bytes 110600 | tf_op jit(solution)/shard_map/ppermute | solution.py:279
  31.1 4.2 %collective-permute-start.28 = (s16[144,128]{1,0:T(8,128)(2,1)S(1)}, s16[144,128]{1,0:T(8,128)(2,1)S(1)}, u32[]{:S(2)}, u32[]{:S(2)}) collective-permute-start(s16[144,128]{1,0:T(8,128)(2,1)S(1)} %get-tuple-element.66.payload), channel_id=1, source_target_pairs={{0,2},{1,3},{2,0},{3,1},{4,6},{5,7},{6,4},{7,5},{8,10},{9,11},{10,... | collective-permute-start | bytes 110600 | tf_op jit(solution)/shard_map/ppermute | solution.py:279
  32.6 2.6 %collective-permute-start.27 = (s16[144,128]{1,0:T(8,128)(2,1)S(1)}, s16[144,128]{1,0:T(8,128)(2,1)S(1)}, u32[]{:S(2)}, u32[]{:S(2)}) collective-permute-start(s16[144,128]{1,0:T(8,128)(2,1)S(1)} %get-tuple-element.66.payload), channel_id=1, source_target_pairs={{0,1},{1,0},{2,3},{3,2},{4,5},{5,4},{6,7},{7,6},{8,9},{9,8},{10,11... | collective-permute-start | bytes 110600 | tf_op jit(solution)/shard_map/ppermute | solution.py:279
